TPU v7x, 512 devices: a whole 4x4x16 slice. The times are simulated.
512 devices in a mesh: gx: 16 (over y, x), gy: 32 (over z, core).
Axes of the slice: x: 4, y: 4, z: 16, core: 2. Of those that a mesh axis runs over, the one named last changes fastest.
Arguments:
- points: float32 [3, 1048576], P(None, ('gx', 'gy')), as said below
- targets: float32 [64, 1048576], P(None, ('gx', 'gy')), may hold values from -6 to 6
- basis: float32 [2048, 64, 512], P(('gx', 'gy')), may hold values from -0.25 to 0.25
- leaf_transfer: float32 [2048, 64, 64], P(('gx', 'gy')), may hold values from -0.75 to 0.75
- cell_transfer: float32 [512, 64, 64], P(('gx', 'gy')), may hold values from -0.75 to 0.75
- box_parent_transfer: float32 [16, 64, 64], replicated, may hold values from -0.75 to 0.75
- cell_coupling: float32 [512, 4, 64, 64], P(('gx', 'gy')), as said below
- box_coupling: float32 [16, 3, 64, 64], replicated, as said below
- top_coupling: float32 [8, 4, 64, 64], replicated, as said below
- neighbours: int32 [2048, 6], P(('gx', 'gy')), may hold values from 0 to 2047, as said below
- cell_lists: int32 [512, 4], P(('gx', 'gy')), may hold values from 0 to 511, as said below
Outputs:
- solution: float32 [64, 1048576], P(None, ('gx', 'gy'))
- residual: float32 [64, 1048576], P(None, ('gx', 'gy'))
Inputs may be any that keep to these rules, and one draw needn't show every extreme that they name: Leaf i's points lie in the unit cell whose corner is the grid position decoded from i's Morton code. `neighbours`: row i is i, i ^ 4, then i ^ m for 4 distinct masks m among 1, 2, 3, 5, 6, 7 (^ is bitwise exclusive or), the same masks in the same order for all leaves of a block of 8 leaves (the same i // 8); so j stands in row i exactly when i stands in row j, and their cells touch. `cell_lists`: the boxes of each second-level box carry a numbering 0 to 31; entry s of row b is the box of b's second-level box whose number is b's number ^ m_s, with 4 distinct nonzero masks m_s common to that second-level box; so b' stands at position s of row b exactly when b stands at position s of row b'. cell_coupling[b', s] is the transpose of cell_coupling[b, s] where b' = cell_lists[b, s]. box_coupling[g ^ (s + 1), s] is the transpose of box_coupling[g, s]. top_coupling[t ^ (s + 1), s] is the transpose of top_coupling[t, s].
All inputs are finite; a program needn't handle non-finite values.
Results may differ from a plain program's by a relative error of at most 0.0014.
Values sent between devices are 32-bit elements; how exact they have to be, the bound alone decides.
No kernel may reach another device: no remote copies, remote signals or barrier semaphores. Data moves between devices by JAX's collectives and lax.ppermute only.
A program may use at most 64 MiB of HBM per device.

v0:
```python
import jax
import jax.numpy as jnp
from jax import lax
from jax.sharding import PartitionSpec as P

ITERS = 2


kernel_rate = 3.4641016151377544
near_weight = 0.0625
noise_level = 1.0
exact_solution = lax.Precision.HIGHEST


def swapped(block, axis, distance):
    count = lax.axis_size(axis)
    route = []
    for low in range(count):
        high = low | 1 << distance
        if high != low and high < count:
            route += [(low, high), (high, low)]
    return lax.ppermute(block, axis, route)


def matern(dist_sq):
    scaled = kernel_rate * jnp.sqrt(dist_sq)
    return (1.0 + scaled) * jnp.exp(-scaled)


def pick_rows(list_rows, count, table):
    chooser = (list_rows[:, None] == jnp.arange(count, dtype=jnp.int32)[None, :]).astype(
        jnp.float32
    )
    return jnp.einsum("sb,bkc->skc", chooser, table, precision=exact_solution)


def shards(
    points,
    targets,
    basis,
    leaf_transfer,
    cell_transfer,
    box_parent_transfer,
    cell_coupling,
    box_coupling,
    top_coupling,
    neighbours,
    cell_lists,
):
    own_leaves = basis.shape[0]
    rank_size = basis.shape[1]
    leaf_size = basis.shape[2]
    rhs_count = targets.shape[0]
    group_size = lax.axis_size("gy")
    box_count = lax.axis_size("gx")
    device = lax.axis_index(("gx", "gy"))
    column = lax.axis_index("gx")
    pair_span = 2 * own_leaves
    parity = device % 2
    partner_coords = swapped(points, ("gx", "gy"), 0)
    joined_points = (
        jnp.concatenate([points, partner_coords], axis=1)
        .reshape(3, pair_span, leaf_size)
        .transpose(1, 0, 2)
    )
    local_rows = jnp.bitwise_xor(neighbours % pair_span, own_leaves * parity)
    own_points = joined_points[:own_leaves]
    neighbour_points = jnp.take(joined_points, local_rows, axis=0)

    def squares(values):
        return lax.psum(jnp.sum(values * values, axis=1), ("gx", "gy"))

    solution = jnp.zeros_like(targets)
    residual = targets
    direction = targets
    norm_now = squares(residual)
    for iteration in range(ITERS):
        partner_values = swapped(direction, ("gx", "gy"), 0)
        blocks = jnp.concatenate([direction, partner_values], axis=1).reshape(
            rhs_count, pair_span, leaf_size
        )

        def one_leaf(leaf_item):
            own_cell, near_points, near_rows = leaf_item

            def add_slot(running, slot_item):
                slot_points, slot_row = slot_item
                chosen = lax.dynamic_index_in_dim(blocks, slot_row, 1, keepdims=False)
                dist_sq = jnp.zeros((leaf_size, leaf_size), jnp.float32)
                for coordinate in range(3):
                    offset = slot_points[coordinate, :, None] - own_cell[coordinate, None, :]
                    dist_sq = dist_sq + offset * offset
                return (running + jnp.dot(chosen, matern(dist_sq), precision=exact_solution), None)

            running, unused = lax.scan(
                add_slot, jnp.zeros((rhs_count, leaf_size), jnp.float32), (near_points, near_rows)
            )
            return running

        result = lax.map(one_leaf, (own_points, neighbour_points, local_rows))
        vectors = direction.reshape(rhs_count, own_leaves, leaf_size)
        leaf_moments = jnp.einsum("akj,caj->akc", basis, vectors, precision=exact_solution)
        cell_moment = jnp.einsum(
            "akl,akc->lc", leaf_transfer, leaf_moments, precision=exact_solution
        )
        lifted = jnp.einsum("kl,kc->lc", cell_transfer[0], cell_moment, precision=exact_solution)
        group_cells = lax.all_gather(cell_moment[None], "gy", axis=0, tiled=True)
        group_lifted = lax.all_gather(lifted[None], "gy", axis=0, tiled=True)
        box_moment = jnp.sum(group_lifted, axis=0)
        every_box_index = lax.all_gather(box_moment[None], "gx", axis=0, tiled=True)
        top_count = box_count // 2
        top_length = top_coupling.shape[1]
        box_length = box_coupling.shape[1]
        coarse_moments = (
            jnp.einsum(
                "qpf,qpj->qfj", box_parent_transfer, every_box_index, precision=exact_solution
            )
            .reshape(top_count, 2, rank_size, rhs_count)
            .sum(axis=1)
        )
        top_index = column // 2
        top_row = jnp.bitwise_xor(top_index, jnp.arange(1, top_length + 1, dtype=jnp.int32))
        top_terms = lax.dynamic_index_in_dim(top_coupling, top_index, 0, keepdims=False)
        coarse_local = jnp.einsum(
            "skl,slc->kc",
            top_terms,
            pick_rows(top_row, top_count, coarse_moments),
            precision=exact_solution,
        )
        box_row = jnp.bitwise_xor(column, jnp.arange(1, box_length + 1, dtype=jnp.int32))
        box_terms = lax.dynamic_index_in_dim(box_coupling, column, 0, keepdims=False)
        own_transfer = lax.dynamic_index_in_dim(box_parent_transfer, column, 0, keepdims=False)
        box_local_terms = jnp.einsum(
            "kl,lc->kc", own_transfer, coarse_local, precision=exact_solution
        )
        box_local_terms = box_local_terms + jnp.einsum(
            "skl,slc->kc",
            box_terms,
            pick_rows(box_row, box_count, every_box_index),
            precision=exact_solution,
        )
        cell_row = cell_lists[0] - column * group_size
        cell_local = jnp.einsum(
            "kl,lc->kc", cell_transfer[0], box_local_terms, precision=exact_solution
        )
        cell_local = cell_local + jnp.einsum(
            "skl,slc->kc",
            cell_coupling[0],
            pick_rows(cell_row, group_size, group_cells),
            precision=exact_solution,
        )
        leaf_local = jnp.einsum("akl,lc->akc", leaf_transfer, cell_local, precision=exact_solution)
        image = (
            noise_level * direction
            + near_weight * result.transpose(1, 0, 2).reshape(rhs_count, own_leaves * leaf_size)
            + jnp.einsum("akj,akc->caj", basis, leaf_local, precision=exact_solution).reshape(
                rhs_count, own_leaves * leaf_size
            )
        )
        curvature = lax.psum(jnp.sum(direction * image, axis=1), ("gx", "gy"))
        alpha = norm_now / curvature
        solution = solution + alpha[:, None] * direction
        residual = residual - alpha[:, None] * image
        if iteration + 1 < ITERS:
            norm_next = squares(residual)
            direction = residual + (norm_next / norm_now)[:, None] * direction
            norm_now = norm_next
    return (solution, residual)


def solution(mesh):
    return jax.shard_map(
        shards,
        mesh=mesh,
        in_specs=(
            P(None, ("gx", "gy")),
            P(None, ("gx", "gy")),
            P(("gx", "gy"), None, None),
            P(("gx", "gy"), None, None),
            P(("gx", "gy"), None, None),
            P(),
            P(("gx", "gy"), None, None, None),
            P(),
            P(),
            P(("gx", "gy"), None),
            P(("gx", "gy"), None),
        ),
        out_specs=(P(None, ("gx", "gy")), P(None, ("gx", "gy"))),
        check_vma=False,
    )
```

profile of v0, /device:TPU:1, one launch (start us, length us, event | category | flops | bytes accessed | tf_op | source)
XLA Modules:
  0.0 783.4 jit_solution(14811608208693633472)
XLA Ops:
  0.7 8.9 %collective-permute-start = (f32[3,2048]{1,0:T(4,128)}, f32[3,2048]{1,0:T(4,128)S(1)}, u32[]{:S(2)}, u32[]{:S(2)}) collective-permute-start(f32[3,2048]{1,0:T(4,128)} %param.19), channel_id=1, source_target_pairs={{0,1},{1,0},{2,3},{3,2},{4,5},{5,4},{6,7},{7,6},{8,9},{9,8},{10,11... | collective-permute-start | bytes 73736 | tf_op jit(solution)/shard_map/ppermute | solution.py:22
  9.6 1.9 collective-permute-start.1
  13.6 1.8 fusion.62
  17.0 34.0 %all-gather = f32[2048,64]{1,0:T(8,128)S(1)} all-gather(f32[64,64]{1,0:T(8,128)S(1)} %copy.49), channel_id=2, replica_groups=mesh['gx'=16,'gy'=32] {'gy'}, dimensions={0}, use_global_device_ids=true | all-gather | bytes 540672 | tf_op jit(solution)/shard_map/all_gather | solution.py:108
  51.1 19.1 %all-gather.1 = f32[1024,64]{1,0:T(8,128)S(1)} all-gather(f32[64,64]{1,0:T(8,128)S(1)} %reduce_sum.73), channel_id=3, replica_groups=mesh['gx'=16,'gy'=32] {'gx'}, dimensions={0}, use_global_device_ids=true | all-gather | bytes 278528 | tf_op jit(solution)/shard_map/all_gather | solution.py:110
  72.8 38.0 %all-gather.2 = f32[2048,64]{1,0:T(8,128)} all-gather(f32[64,64]{1,0:T(8,128)S(1)} %copy.56), channel_id=4, replica_groups=mesh['gx'=16,'gy'=32] {'gy'}, dimensions={0}, use_global_device_ids=true | all-gather | bytes 540672 | tf_op jit(solution)/shard_map/all_gather | solution.py:107
  112.8 2.2 fusion.58
  121.8 128.0 %while.43 = (s32[]{:T(128)}, f32[4,64,512]{2,1,0:T(8,128)}, f32[4,6,3,512]{3,2,1,0:T(4,128)}, s32[4,6]{1,0:T(4,128)}, f32[4,3,512]{2,1,0:T(4,128)S(1)}, /*index=...) while((s32[]{:T(128)}, f32[4,64,512]{2,1,0:T(8,128)}, ...), condition=%wide.region_5.6_spmd, body=%wide.region_2.5_spmd.sunk | while | flops 204537856 | bytes 1041382 | solution.py:100
  123.8 29.3 %while.46 = (s32[]{:T(128)}, f32[64,512]{1,0:T(8,128)S(1)}, s32[6]{0:T(128)}, f32[64,8,512]{2,1,0:T(8,128)S(1)}, f32[6,3,512]{2,1,0:T(4,128)S(1)}, /*index=5*/f3...) while((s32[]{:T(128)}, f32[64,512]{1,0:T(8,128)S(1)}, ...), condition=%wide.region_4.4_spmd.clone, body=%wide.region_3.3_spmd.clone.sunk | while | flops 204537856 | bytes 692429 | solution.py:95
  155.8 29.3 %while.46 = (s32[]{:T(128)}, f32[64,512]{1,0:T(8,128)S(1)}, s32[6]{0:T(128)}, f32[64,8,512]{2,1,0:T(8,128)S(1)}, f32[6,3,512]{2,1,0:T(4,128)S(1)}, /*index=5*/f3...) while((s32[]{:T(128)}, f32[64,512]{1,0:T(8,128)S(1)}, ...), condition=%wide.region_4.4_spmd.clone, body=%wide.region_3.3_spmd.clone.sunk | while | flops 204537856 | bytes 692429 | solution.py:95
  164.0 1.5 convolution_add_fusion.9
  187.8 29.3 %while.46 = (s32[]{:T(128)}, f32[64,512]{1,0:T(8,128)S(1)}, s32[6]{0:T(128)}, f32[64,8,512]{2,1,0:T(8,128)S(1)}, f32[6,3,512]{2,1,0:T(4,128)S(1)}, /*index=5*/f3...) while((s32[]{:T(128)}, f32[64,512]{1,0:T(8,128)S(1)}, ...), condition=%wide.region_4.4_spmd.clone, body=%wide.region_3.3_spmd.clone.sunk | while | flops 204537856 | bytes 692429 | solution.py:95
  196.0 1.5 convolution_add_fusion.9
  219.7 29.3 %while.46 = (s32[]{:T(128)}, f32[64,512]{1,0:T(8,128)S(1)}, s32[6]{0:T(128)}, f32[64,8,512]{2,1,0:T(8,128)S(1)}, f32[6,3,512]{2,1,0:T(4,128)S(1)}, /*index=5*/f3...) while((s32[]{:T(128)}, f32[64,512]{1,0:T(8,128)S(1)}, ...), condition=%wide.region_4.4_spmd.clone, body=%wide.region_3.3_spmd.clone.sunk | while | flops 204537856 | bytes 692429 | solution.py:95
  228.0 1.5 convolution_add_fusion.9
  251.1 100.0 %all-reduce = (f32[64]{0:T(128)S(1)}, f32[64]{0:T(128)S(1)}) all-reduce(f32[64]{0:T(128)S(1)} %get-tuple-element.175, f32[64]{0:T(128)S(1)} %get-tuple-element.174), channel_id=1, replica_groups=mesh['gx'=16,'gy'=32] {'gx','gy'}, use_global_device_ids=true, to_apply=%region_1.2 | all-reduce | flops 128 | bytes 1024 | tf_op jit(solution)/shard_map/psum | solution.py:71
  351.2 2.1 multiply_reduce_fusion.1
  353.3 99.5 %psum.30 = f32[64]{0:T(128)S(1)} all-reduce(f32[64]{0:T(128)S(1)} %get-tuple-element.226), channel_id=1, replica_groups=mesh['gx'=16,'gy'=32] {'gx','gy'}, use_global_device_ids=true, to_apply=%region_11.12 | all-reduce | flops 64 | bytes 512 | tf_op jit(solution)/shard_map/psum | solution.py:71
  454.0 2.8 collective-permute-start.2
  458.0 34.0 %all-gather.3 = f32[2048,64]{1,0:T(8,128)} all-gather(f32[64,64]{1,0:T(8,128)S(1)} %copy.63), channel_id=5, replica_groups=mesh['gx'=16,'gy'=32] {'gy'}, dimensions={0}, use_global_device_ids=true | all-gather | bytes 540672 | tf_op jit(solution)/shard_map/all_gather | solution.py:108
  493.3 18.1 %all-gather.4 = f32[1024,64]{1,0:T(8,128)S(1)} all-gather(f32[64,64]{1,0:T(8,128)S(1)} %reduce_sum.77), channel_id=6, replica_groups=mesh['gx'=16,'gy'=32] {'gx'}, dimensions={0}, use_global_device_ids=true | all-gather | bytes 278528 | tf_op jit(solution)/shard_map/all_gather | solution.py:110
  511.4 2.1 bitcast_reduce_fusion
  520.2 34.8 %all-gather.5 = f32[2048,64]{1,0:T(8,128)S(1)} all-gather(f32[64,64]{1,0:T(8,128)S(1)} %copy.70), channel_id=7, replica_groups=mesh['gx'=16,'gy'=32] {'gy'}, dimensions={0}, use_global_device_ids=true | all-gather | bytes 540672 | tf_op jit(solution)/shard_map/all_gather | solution.py:107
  562.1 116.6 %while.45 = (s32[]{:T(128)}, f32[4,64,512]{2,1,0:T(8,128)}, f32[4,6,3,512]{3,2,1,0:T(4,128)}, s32[4,6]{1,0:T(4,128)}, f32[4,3,512]{2,1,0:T(4,128)}, /*index=5*/f...) while((s32[]{:T(128)}, f32[4,64,512]{2,1,0:T(8,128)}, ...), condition=%wide.region_15.16_spmd, body=%wide.region_12.15_spmd.sunk | while | flops 204537856 | bytes 1041382 | solution.py:100
  564.3 26.3 %while.47 = (s32[]{:T(128)}, f32[64,512]{1,0:T(8,128)S(1)}, s32[6]{0:T(128)S(1)}, f32[64,8,512]{2,1,0:T(8,128)S(1)}, f32[6,3,512]{2,1,0:T(4,128)S(1)}, /*index=5...) while((s32[]{:T(128)}, f32[64,512]{1,0:T(8,128)S(1)}, ...), condition=%wide.region_14.14_spmd.clone, body=%wide.region_13.13_spmd.clone.sunk | while | flops 204537856 | bytes 692429 | solution.py:95
  593.5 26.3 %while.47 = (s32[]{:T(128)}, f32[64,512]{1,0:T(8,128)S(1)}, s32[6]{0:T(128)S(1)}, f32[64,8,512]{2,1,0:T(8,128)S(1)}, f32[6,3,512]{2,1,0:T(4,128)S(1)}, /*index=5...) while((s32[]{:T(128)}, f32[64,512]{1,0:T(8,128)S(1)}, ...), condition=%wide.region_14.14_spmd.clone, body=%wide.region_13.13_spmd.clone.sunk | while | flops 204537856 | bytes 692429 | solution.py:95
  622.6 26.3 %while.47 = (s32[]{:T(128)}, f32[64,512]{1,0:T(8,128)S(1)}, s32[6]{0:T(128)S(1)}, f32[64,8,512]{2,1,0:T(8,128)S(1)}, f32[6,3,512]{2,1,0:T(4,128)S(1)}, /*index=5...) while((s32[]{:T(128)}, f32[64,512]{1,0:T(8,128)S(1)}, ...), condition=%wide.region_14.14_spmd.clone, body=%wide.region_13.13_spmd.clone.sunk | while | flops 204537856 | bytes 692429 | solution.py:95
  625.5 1.5 convolution_add_fusion.8
  651.8 26.3 %while.47 = (s32[]{:T(128)}, f32[64,512]{1,0:T(8,128)S(1)}, s32[6]{0:T(128)S(1)}, f32[64,8,512]{2,1,0:T(8,128)S(1)}, f32[6,3,512]{2,1,0:T(4,128)S(1)}, /*index=5...) while((s32[]{:T(128)}, f32[64,512]{1,0:T(8,128)S(1)}, ...), condition=%wide.region_14.14_spmd.clone, body=%wide.region_13.13_spmd.clone.sunk | while | flops 204537856 | bytes 692429 | solution.py:95
  654.6 1.5 convolution_add_fusion.8
  680.9 100.1 %psum.31 = f32[64]{0:T(128)S(1)} all-reduce(f32[64]{0:T(128)S(1)} %multiply_reduce_fusion), channel_id=1, replica_groups=mesh['gx'=16,'gy'=32] {'gx','gy'}, use_global_device_ids=true, to_apply=%region_19.20 | all-reduce | flops 64 | bytes 512 | tf_op jit(solution)/shard_map/psum | solution.py:160
  781.0 2.4 multiply_subtract_fusion
  (400 shorter events, 175.9 us)
Async XLA Ops:
  0.6 111.7 %copy-start = (f32[16,3,64,64]{3,2,1,0:T(8,128)S(1)}, f32[16,3,64,64]{3,2,1,0:T(8,128)}, u32[]{:S(2)}) copy-start(f32[16,3,64,64]{3,2,1,0:T(8,128)} %param.26) | copy-start | bytes 2359300
  0.6 16.1 %copy-start.15 = (f32[1,64,64]{2,1,0:T(8,128)S(1)}, f32[1,64,64]{2,1,0:T(8,128)}, u32[]{:S(2)}) copy-start(f32[1,64,64]{2,1,0:T(8,128)} %param.23) | copy-start | bytes 49156
  0.7 117.0 %collective-permute-start = (f32[3,2048]{1,0:T(4,128)}, f32[3,2048]{1,0:T(4,128)S(1)}, u32[]{:S(2)}, u32[]{:S(2)}) collective-permute-start(f32[3,2048]{1,0:T(4,128)} %param.19), channel_id=1, source_target_pairs={{0,1},{1,0},{2,3},{3,2},{4,5},{5,4},{6,7},{7,6},{8,9},{9,8},{10,11... | collective-permute-start | bytes 73736 | tf_op jit(solution)/shard_map/ppermute | solution.py:22
  9.6 109.6 %collective-permute-start.1 = (f32[64,2048]{1,0:T(8,128)}, f32[64,2048]{1,0:T(8,128)}, u32[]{:S(2)}, u32[]{:S(2)}) collective-permute-start(f32[64,2048]{1,0:T(8,128)} %param.20), channel_id=1, source_target_pairs={{0,1},{1,0},{2,3},{3,2},{4,5},{5,4},{6,7},{7,6},{8,9},{9,8},{10,11... | collective-permute-start | bytes 1572872 | tf_op jit(solution)/shard_map/ppermute | solution.py:22
  11.5 99.3 %copy-start.21 = (s32[4]{0:T(128)}, s32[4]{0:T(128)S(1)}, u32[]{:S(2)}) copy-start(s32[4]{0:T(128)S(1)} %add_xor_fusion.1) | copy-start | bytes 52
  11.6 59.8 %copy-start.25 = (s32[3]{0:T(128)}, s32[3]{0:T(128)S(1)}, u32[]{:S(2)}) copy-start(s32[3]{0:T(128)S(1)} %add_xor_fusion) | copy-start | bytes 40
  15.5 54.7 %copy-start.10 = (f32[16,64,64]{2,1,0:T(8,128)S(1)}, f32[16,64,64]{2,1,0:T(8,128)}, u32[]{:S(2)}) copy-start(f32[16,64,64]{2,1,0:T(8,128)} %param.24) | copy-start | bytes 786436
  51.1 21.5 %copy-start.27 = (s32[1,4]{1,0:T(1,128)S(1)}, s32[1,4]{1,0:T(1,128)}, u32[]{:S(2)}) copy-start(s32[1,4]{1,0:T(1,128)} %param.29) | copy-start | bytes 52
  72.7 39.7 %copy-start.18 = (f32[3,64,64]{2,0,1:T(4,128)S(1)}, f32[3,64,64]{2,0,1:T(4,128)}, u32[]{:S(2)}) copy-start(f32[3,64,64]{2,0,1:T(4,128)} %fusion.67) | copy-start | bytes 147460
  72.7 42.4 %copy-start.23 = (s32[4]{0:T(128)}, s32[4]{0:T(128)S(1)}, u32[]{:S(2)}) copy-start(s32[4]{0:T(128)S(1)} %subtract_bitcast_fusion) | copy-start | bytes 52
  72.7 42.3 %copy-start.13 = (f32[1,4,64,64]{3,2,1,0:T(8,128)S(1)}, f32[1,4,64,64]{3,2,1,0:T(8,128)}, u32[]{:S(2)}) copy-start(f32[1,4,64,64]{3,2,1,0:T(8,128)} %param.25) | copy-start | bytes 196612
  110.8 4.9 copy-start.11
  110.8 5.4 copy-start.4
  115.1 2.6 copy-start.20
  116.2 2.9 copy-start.1
  249.7 1.4 copy-start.17
  249.7 1.2 copy-start.8
  250.9 100.3 %copy-start.9 = (f32[4,8,8,512]{3,2,0,1:T(8,128)}, f32[4,8,8,512]{3,2,0,1:T(8,128)S(1)}, u32[]{:S(2)}) copy-start(f32[4,8,8,512]{3,2,0,1:T(8,128)S(1)} %copy.90) | copy-start | bytes 1572868
  351.2 105.6 %copy-start.5 = (f32[4,64,512]{2,1,0:T(8,128)S(1)}, f32[4,64,512]{2,1,0:T(8,128)}, u32[]{:S(2)}) copy-start(f32[4,64,512]{2,1,0:T(8,128)} %param.21) | copy-start | bytes 1572868
  353.3 104.1 %copy-start.12 = (f32[4,64,64]{2,1,0:T(8,128)S(1)}, f32[4,64,64]{2,1,0:T(8,128)}, u32[]{:S(2)}) copy-start(f32[4,64,64]{2,1,0:T(8,128)} %param.22) | copy-start | bytes 196612
  452.8 5.1 copy-start.28
  454.0 105.6 %copy-start.2 = (f32[64,2048]{1,0:T(8,128)}, f32[64,2048]{1,0:T(8,128)S(1)}, u32[]{:S(2)}) copy-start(f32[64,2048]{1,0:T(8,128)S(1)} %multiply_add_fusion.1) | copy-start | bytes 1572868
  454.0 105.5 %collective-permute-start.2 = (f32[64,2048]{1,0:T(8,128)S(1)}, f32[64,2048]{1,0:T(8,128)}, u32[]{:S(2)}, u32[]{:S(2)}) collective-permute-start(f32[64,2048]{1,0:T(8,128)S(1)} %multiply_add_fusion.1), channel_id=1, source_target_pairs={{0,1},{1,0},{2,3},{3,2},{4,5},{5,4},{6,7},{7,6},{8,9},{9,8},{10,11... | collective-permute-start | bytes 1572872 | tf_op jit(solution)/shard_map/ppermute | solution.py:22
  457.7 53.7 %copy-start.19 = (f32[64,64,1]{1,0,2:T(8,128)}, f32[64,64,1]{1,0,2:T(8,128)S(1)}, u32[]{:S(2)}) copy-start(f32[64,64,1]{1,0,2:T(8,128)S(1)} %fusion.124) | copy-start | bytes 49156
  492.0 21.5 %copy-start.26 = (s32[3]{0:T(128)S(1)}, s32[3]{0:T(128)}, u32[]{:S(2)}) copy-start(s32[3]{0:T(128)} %copy-done.25) | copy-start | bytes 40
  493.3 22.3 %copy-start.22 = (s32[4]{0:T(128)S(1)}, s32[4]{0:T(128)}, u32[]{:S(2)}) copy-start(s32[4]{0:T(128)} %copy-done.21) | copy-start | bytes 52
  513.5 41.5 %copy-start.24 = (s32[4]{0:T(128)S(1)}, s32[4]{0:T(128)}, u32[]{:S(2)}) copy-start(s32[4]{0:T(128)} %copy-done.23) | copy-start | bytes 52
  516.9 40.1 %copy-start.14 = (f32[1,4,64,64]{3,2,1,0:T(8,128)S(1)}, f32[1,4,64,64]{3,2,1,0:T(8,128)}, u32[]{:S(2)}) copy-start(f32[1,4,64,64]{3,2,1,0:T(8,128)} %param.25) | copy-start | bytes 196612
  516.9 40.5 %copy-start.16 = (f32[1,64,64]{2,1,0:T(8,128)S(1)}, f32[1,64,64]{2,1,0:T(8,128)}, u32[]{:S(2)}) copy-start(f32[1,64,64]{2,1,0:T(8,128)} %param.23) | copy-start | bytes 49156
  678.7 2.0 copy-start.3
  678.7 2.0 copy-start.6
  679.9 101.1 %copy-start.29 = (f32[64]{0:T(128)S(1)}, f32[64]{0:T(128)}, u32[]{:S(2)}) copy-start(f32[64]{0:T(128)} %copy-done.28) | copy-start | bytes 772
  (1 other events, 0.8 us)
where the time goes:
time: 787 us; the launch traced here: 783 us
  blocking collectives  478 us (61%)
  matrix products  96.7 us (12%)
  loops' own time  96.7 us (12%)
  local copies, waits for them, and re-layouts  82.7 us (11%)
  other arithmetic  14.8 us (2%)
  starting transfers between devices  13.6 us (2%)
    psum x2, blocking collectives, squares(): return lax.psum(jnp.sum(values * values, axis=1), ('gx', 'gy'))  200 us
    psum x1, blocking collectives, shards(): curvature = lax.psum(jnp.sum(direction * image, axis=1), ('gx', 'gy'))  100 us
    another operation x8, loops' own time, one_leaf(): lax.scan(add_slot, jnp.zeros((rhs_count, leaf_size), jnp.float32), (near_...  96.6 us
    dot_general x48, matrix products, add_slot(): jnp.dot(chosen, matern(dist_sq), precision=exact_solution)  73.6 us
    all_gather x2, blocking collectives, shards(): group_cells = lax.all_gather(cell_moment[None], 'gy', axis=0, tiled=True)  72.9 us
    all_gather x2, blocking collectives, shards(): group_lifted = lax.all_gather(lifted[None], 'gy', axis=0, tiled=True)  68 us
    dynamic_slice x48, local copies, waits for them, and re-layouts, one_leaf(): lax.scan(add_slot, jnp.zeros((rhs_count, leaf_size), jnp.float32), (near_...  45.6 us
    all_gather x2, blocking collectives, shards(): every_box_index = lax.all_gather(box_moment[None], 'gx', axis=0, tiled=True)  37.2 us
  transfers between devices with their start and end apart: 3, of which 0 were waited for; matrix products, arithmetic and copies ran while one was open for 4% of the time, Pallas kernels for 0%

commit v1 on v0

v1 whole, which is shorter than its diff:
```python
import functools
import math

import jax
import jax.numpy as jnp
from jax import lax
from jax.experimental import pallas as pl
from jax.experimental.pallas import tpu as pltpu
from jax.sharding import PartitionSpec as P

RANK = 64
ROWS = 64
LEAF = 512
OWN = 4
SLOTS = 6
FEATURES = 32
BOX_SPAN = 9
GROUP = 32
LIST = 4

UNIT = 2.0 * math.sqrt(3.0)
NEAR_WEIGHT = 0.0625

EXACT = lax.Precision.HIGHEST
VMEM = pl.BlockSpec(memory_space=pltpu.VMEM)
SMEM = pl.BlockSpec(memory_space=pltpu.SMEM)
ANY = pl.BlockSpec(memory_space=pl.ANY)

NN = (((1,), (0,)), ((), ()))
NT = (((1,), (1,)), ((), ()))
TN = (((0,), (0,)), ((), ()))


def mm(a, b, dims=NN):
    return lax.dot_general(a, b, dims, precision=EXACT, preferred_element_type=jnp.float32)


def mm16(a, b, dims=NN):
    return lax.dot_general(a, b, dims, preferred_element_type=jnp.float32)


def split2(value):
    high = value.astype(jnp.bfloat16)
    return high, (value - high.astype(jnp.float32)).astype(jnp.bfloat16)


def split3(value):
    first = value.astype(jnp.bfloat16).astype(jnp.float32)
    rest = value - first
    second = rest.astype(jnp.bfloat16).astype(jnp.float32)
    return first, second, rest - second


def params(mib=32):
    return pltpu.CompilerParams(vmem_limit_bytes=mib * 1024 * 1024)


def cost(flops, moved, special=0):
    return pl.CostEstimate(flops=flops, bytes_accessed=moved, transcendentals=special)


def shape(*dims, dtype=jnp.float32):
    return jax.ShapeDtypeStruct(dims, dtype)


def packed_rows(table):
    return jnp.concatenate([table[: ROWS // 2], table[ROWS // 2 :]], axis=1)


def unpacked_rows(table):
    return jnp.concatenate([table[:, :RANK], table[:, RANK:]], axis=0)


def fetch(pairs, sems):
    copies = [
        pltpu.make_async_copy(source, target, sems.at[k])
        for k, (source, target) in enumerate(pairs)
    ]
    for copy in copies:
        copy.start()
    return copies


def up_body(
    basis, leaf_transfer, cell_transfer, lists, vector, lifts, message, cell, b, t, c, v, sems
):
    copies = fetch(
        ((leaf_transfer, t), (basis, b), (vector, v), (cell_transfer, c)), sems
    )
    for copy in copies:
        copy.wait()
    total = jnp.zeros((ROWS, RANK), jnp.float32)
    for a in range(OWN):
        lift = mm(t[a], b[a], TN)
        lifts[:, a * LEAF : (a + 1) * LEAF] = lift
        total = total + mm(v[:, a * LEAF : (a + 1) * LEAF], lift, NT)
    message[:, 0, 0:128] = packed_rows(total)
    message[:, 0, 128:256] = packed_rows(mm(total, c[0]))
    lane = lax.broadcasted_iota(jnp.int32, (GROUP, 128), 1)
    table = jnp.zeros((GROUP, 128), jnp.int32)
    for k in range(LIST):
        table = jnp.where(lane == k, lists[0, k] & (GROUP - 1), table)
    message[:, 0, 256:384] = table.astype(jnp.float32)
    cell[:, :RANK] = c[0]
    cell[:, RANK:] = c[0]


def up(basis, leaf_transfer, cell_transfer, cell_lists, vector):
    return pl.pallas_call(
        up_body,
        out_shape=(
            shape(RANK, OWN * LEAF),
            shape(GROUP, 1, 384),
            shape(RANK, 2 * RANK),
        ),
        in_specs=[ANY] * 3 + [SMEM, ANY],
        out_specs=[VMEM] * 3,
        scratch_shapes=[
            pltpu.VMEM((OWN, RANK, LEAF), jnp.float32),
            pltpu.VMEM((OWN, RANK, RANK), jnp.float32),
            pltpu.VMEM((1, RANK, RANK), jnp.float32),
            pltpu.VMEM((ROWS, OWN * LEAF), jnp.float32),
            pltpu.SemaphoreType.DMA((4,)),
        ],
        compiler_params=params(60),
        cost_estimate=cost(60_000_000, 2_000_000),
        name="up",
    )(basis, leaf_transfer, cell_transfer, cell_lists, vector)


def coarse_body(parent_ref, box_ref, top_ref, out, parent, box_coupling, top_coupling, sems):
    g = lax.axis_index("gx")
    t = g // 2
    copies = fetch(
        (
            (parent_ref, parent),
            (box_ref.at[g], box_coupling),
            (top_ref.at[t], top_coupling),
        ),
        sems,
    )
    out[...] = jnp.zeros_like(out)
    for copy in copies:
        copy.wait()
    for m in range(1, BOX_SPAN + 1):
        if m >= 2:
            if m % 2 == 0:
                through = mm(parent[g], top_coupling[m // 2 - 1])
            value = mm(parent[jnp.bitwise_xor(g, m)], through, NT)
        if m <= 3:
            direct = box_coupling[m - 1].T
            value = direct if m == 1 else value + direct
        low = (m - 1) * 128
        out[low : low + 64, 0:64] = value
        out[low + 64 : low + 128, 64:128] = value


def coarse(parent, box_coupling, top_coupling):
    return pl.pallas_call(
        coarse_body,
        out_shape=shape(BOX_SPAN * 128, 128),
        in_specs=[ANY] * 3,
        out_specs=VMEM,
        scratch_shapes=[
            pltpu.VMEM((16, RANK, RANK), jnp.float32),
            pltpu.VMEM((3, RANK, RANK), jnp.float32),
            pltpu.VMEM((4, RANK, RANK), jnp.float32),
            pltpu.SemaphoreType.DMA((3,)),
        ],
        compiler_params=params(60),
        cost_estimate=cost(50_000_000, 2_000_000),
        name="coarse",
    )(parent, box_coupling, top_coupling)


def route_body(received, box, picked):
    chunk = jnp.sum(received[:, 0, 128:256], axis=0, keepdims=True)
    box[...] = jnp.broadcast_to(chunk[None], box.shape)
    cells = received[:, 0, 0:128]
    numbers = received[:, 0, 256:384]
    member = lax.broadcasted_iota(jnp.int32, (GROUP, GROUP), 1).astype(jnp.float32)
    for k in range(LIST):
        chooser = (numbers[:, k : k + 1] == member).astype(jnp.float32)
        picked[:, k * 128 : (k + 1) * 128] = mm(chooser, cells)


def route(received):
    return pl.pallas_call(
        route_body,
        out_shape=(shape(16, 1, 128), shape(GROUP, LIST * 128)),
        in_specs=[VMEM],
        out_specs=[VMEM] * 2,
        compiler_params=params(),
        cost_estimate=cost(4_000_000, 200_000),
        name="route",
    )(received)


def boxes_body(received, maps, picked, message):
    g = lax.axis_index("gx")
    row = jnp.concatenate(
        [received[jnp.bitwise_xor(g, m)] for m in range(1, BOX_SPAN + 1)], axis=1
    )
    local = mm(row, maps[...])
    message[:, 0, 0:128] = jnp.broadcast_to(local, (GROUP, 128))
    message[:, 0, 128:640] = picked[...]


def boxes(received, maps, picked):
    return pl.pallas_call(
        boxes_body,
        out_shape=shape(GROUP, 1, 640),
        in_specs=[VMEM] * 3,
        out_specs=VMEM,
        compiler_params=params(),
        cost_estimate=cost(4_000_000, 200_000),
        name="boxes",
    )(received, maps, picked)


def sum_rows(columns):
    lane = lax.broadcasted_iota(jnp.int32, (ROWS, 128), 1)
    table = jnp.zeros((ROWS, 128), jnp.float32)
    for k, column in columns:
        table = jnp.where(lane == k, column, table)
    table = table.T
    upper = jnp.concatenate([table[0:1], table[1:2]], axis=1)
    lower = jnp.concatenate([table[2:3], table[3:4]], axis=1)
    return jnp.concatenate([upper, lower], axis=0)


def tally_body(
    lists, received, cells, couplings, moment, dots, image, near, box, local, sums
):
    total = mm(received[...], cells[:, :RANK], TN)
    box[...] = jnp.broadcast_to(packed_rows(total)[None], box.shape)
    expansion = jnp.zeros((RANK, ROWS), jnp.float32)
    for k in range(LIST):
        low = pl.multiple_of((lists[0, k] & (GROUP - 1)) * RANK, RANK)
        expansion = expansion + mm(couplings[0, k], received[pl.ds(low, RANK), :])
    local[...] = expansion
    square = dots[:, 2:3]
    cubic = square
    for a in range(OWN):
        part = slice(a * LEAF, (a + 1) * LEAF)
        cubic = cubic + jnp.sum(image[:, part] * near[:, part], axis=1, keepdims=True)
    rows = sum_rows(((0, dots[:, 0:1]), (1, dots[:, 1:2]), (2, square), (3, cubic)))
    far = jnp.sum(moment[...] * expansion, axis=0, keepdims=True)
    blank = jnp.zeros((1, RANK), jnp.float32)
    rows = rows + jnp.concatenate(
        [jnp.zeros((1, 128), jnp.float32), jnp.concatenate([blank, far], axis=1)], axis=0
    )
    sums[...] = jnp.broadcast_to(rows[None], sums.shape)


def tally(lists, received, cells, couplings, moment, dots, image, near):
    return pl.pallas_call(
        tally_body,
        out_shape=(shape(16, 32, 128), shape(RANK, ROWS), shape(GROUP, 2, 128)),
        in_specs=[SMEM] + [VMEM] * 7,
        out_specs=[VMEM] * 3,
        compiler_params=params(),
        cost_estimate=cost(4_000_000, 2_500_000),
        name="tally",
    )(lists, received, cells, couplings, moment, dots, image, near)


def spread_body(received, extra, sums):
    total = jnp.sum(received[...], axis=0, keepdims=True) + extra[...][None]
    sums[...] = jnp.broadcast_to(total, sums.shape)


def spread(received, extra):
    return pl.pallas_call(
        spread_body,
        out_shape=shape(16, 2, 128),
        in_specs=[VMEM] * 2,
        out_specs=VMEM,
        compiler_params=params(),
        cost_estimate=cost(10_000, 50_000),
        name="spread",
    )(received, extra)


def features_body(own, partner, left, right, rows):
    block = lax.axis_index("gx") * (lax.axis_size("gy") // 2) + lax.axis_index("gy") // 2
    axis_id = lax.broadcasted_iota(jnp.int32, (3, OWN * LEAF), 0)
    centre = jnp.zeros((3, OWN * LEAF), jnp.int32)
    for axis in range(3):
        place = 1
        for depth in range(1, 11):
            place = place + ((block >> (3 * (depth - 1) + axis)) & 1) * (1 << depth)
        centre = jnp.where(axis_id == axis, place, centre)
    centre = centre.astype(jnp.float32)
    ones = jnp.ones((3, OWN * LEAF), jnp.float32)
    for half, source in enumerate((own, partner)):
        local = (source[...] - centre) * UNIT
        one, two, three = split3(local)
        square = jnp.sum(local * local, axis=0, keepdims=True)
        squares = split3(square)
        rows[24:32, :] = jnp.zeros((8, OWN * LEAF), jnp.float32)
        for place, piece in enumerate((one, one, two, one, two, three)):
            rows[3 * place : 3 * place + 3, :] = -2.0 * piece
        for place, piece in enumerate(squares):
            rows[18 + place : 19 + place, :] = piece
        rows[21:24, :] = ones
        for a in range(OWN):
            left[half * OWN + a] = rows[:, a * LEAF : (a + 1) * LEAF].T.astype(jnp.bfloat16)
        if half == 0:
            for place, piece in enumerate((one, two, one, three, two, one)):
                rows[3 * place : 3 * place + 3, :] = piece
            rows[18:21, :] = ones
            for place, piece in enumerate(squares):
                rows[21 + place : 22 + place, :] = piece
            for a in range(OWN):
                right[a] = rows[:, a * LEAF : (a + 1) * LEAF].astype(jnp.bfloat16)


def features(own, partner):
    return pl.pallas_call(
        features_body,
        out_shape=(
            shape(2 * OWN, LEAF, FEATURES, dtype=jnp.bfloat16),
            shape(OWN, FEATURES, LEAF, dtype=jnp.bfloat16),
        ),
        in_specs=[VMEM] * 2,
        out_specs=[VMEM] * 2,
        scratch_shapes=[pltpu.VMEM((FEATURES, OWN * LEAF), jnp.float32)],
        compiler_params=params(),
        cost_estimate=cost(1_000_000, 400_000),
        name="features",
    )(own, partner)


def joined_body(own, partner, out):
    for half, source in enumerate((own, partner)):
        for a in range(OWN):
            high, low = split2(source[:, a * LEAF : (a + 1) * LEAF])
            out[half * OWN + a, :ROWS, :] = high
            out[half * OWN + a, ROWS:, :] = low


def joined(own, partner):
    return pl.pallas_call(
        joined_body,
        out_shape=shape(2 * OWN, 2 * ROWS, LEAF, dtype=jnp.bfloat16),
        in_specs=[VMEM] * 2,
        out_specs=VMEM,
        compiler_params=params(),
        cost_estimate=cost(1_000_000, 2_000_000),
        name="joined",
    )(own, partner)


def neighbour_row(neighbours, leaf, n):
    parity = lax.axis_index("gy") % 2
    return jnp.bitwise_xor(neighbours[leaf, n] & (2 * OWN - 1), OWN * parity)


def tiles_body(neighbours, left, right, vectors, tiles, out, square):
    leaf = pl.program_id(0)
    target = right[leaf]
    rows = [neighbour_row(neighbours, leaf, n) for n in range(SLOTS)]
    wide = jnp.zeros((2 * ROWS, LEAF), jnp.float32)
    narrow = jnp.zeros((ROWS, LEAF), jnp.float32)
    step = 32

    def measure(n):
        square[n % 2] = mm16(left[rows[n]], target)

    def apply(n, wide, narrow):
        wide = wide + mm16(vectors[rows[n]], tiles[0, n, 0])
        narrow = narrow + mm16(vectors[rows[n], :ROWS, :], tiles[0, n, 1])
        return wide, narrow

    measure(0)
    for n in range(SLOTS):
        if n + 1 < SLOTS:
            measure(n + 1)
        if n > 0:
            wide, narrow = apply(n - 1, wide, narrow)
        for low in range(0, LEAF, step):
            part = jnp.maximum(square[n % 2, low : low + step, :], 1e-12)
            u = part * lax.rsqrt(part)
            kernel = jnp.exp(-u) * (1.0 + u)
            high, rest = split2(kernel)
            tiles[0, n, 0, low : low + step, :] = high
            tiles[0, n, 1, low : low + step, :] = rest
    wide, narrow = apply(SLOTS - 1, wide, narrow)
    out[...] = NEAR_WEIGHT * (wide[:ROWS] + wide[ROWS:] + narrow)


def near_tiles(neighbours, left, right, vectors):
    tile = shape(OWN, SLOTS, 2, LEAF, LEAF, dtype=jnp.bfloat16)
    block = pl.BlockSpec((1, SLOTS, 2, LEAF, LEAF), lambda a: (a, 0, 0, 0, 0))
    return pl.pallas_call(
        tiles_body,
        grid=(OWN,),
        out_shape=(tile, shape(ROWS, OWN * LEAF)),
        in_specs=[SMEM] + [VMEM] * 3,
        out_specs=[block, pl.BlockSpec((ROWS, LEAF), lambda a: (0, a))],
        scratch_shapes=[pltpu.VMEM((2, LEAF, LEAF), jnp.float32)],
        compiler_params=params(40),
        cost_estimate=cost(8_000_000_000, 30_000_000, 12_000_000),
        name="near_tiles",
    )(neighbours, left, right, vectors)


def again_body(neighbours, vectors, high_tiles, low_tiles, out):
    leaf = pl.program_id(0)
    wide = jnp.zeros((2 * ROWS, LEAF), jnp.float32)
    narrow = jnp.zeros((ROWS, LEAF), jnp.float32)
    for n in range(SLOTS // 2):
        row = neighbour_row(neighbours, leaf, pl.program_id(1) * (SLOTS // 2) + n)
        wide = wide + mm16(vectors[row], high_tiles[0, n, 0])
        narrow = narrow + mm16(vectors[row, :ROWS, :], low_tiles[0, n, 0])
    value = NEAR_WEIGHT * (wide[:ROWS] + wide[ROWS:] + narrow)

    @pl.when(pl.program_id(1) == 0)
    def first():
        out[...] = value

    @pl.when(pl.program_id(1) > 0)
    def later():
        out[...] += value


def near_again(neighbours, vectors, tiles):
    half = (1, SLOTS // 2, 1, LEAF, LEAF)
    high = pl.BlockSpec(half, lambda a, h: (a, h, 0, 0, 0))
    low = pl.BlockSpec(half, lambda a, h: (a, h, 1, 0, 0))
    return pl.pallas_call(
        again_body,
        grid=(OWN, 2),
        out_shape=shape(ROWS, OWN * LEAF),
        in_specs=[SMEM, VMEM, high, low],
        out_specs=pl.BlockSpec((ROWS, LEAF), lambda a, h: (0, a)),
        compiler_params=params(40),
        cost_estimate=cost(6_000_000_000, 30_000_000),
        name="near_again",
    )(neighbours, vectors, tiles, tiles)


def box_local(maps, boxes):
    g = lax.axis_index("gx")
    row = jnp.concatenate(
        [boxes[jnp.bitwise_xor(g, m)] for m in range(1, BOX_SPAN + 1)], axis=1
    )
    return mm(row, maps[...])


def cell_local(couplings, cell_transfer, received):
    local = mm(unpacked_rows(received[:, 0, 0:128]), cell_transfer[0], NT)
    for s in range(LIST):
        low = 128 * (s + 1)
        local = local + mm(
            unpacked_rows(received[:, 0, low : low + 128]), couplings[0, s], NT
        )
    return local


def middle_body(
    couplings, cell_transfer, lifts, vector, near, received, image, moment, dots
):
    local = cell_local(couplings, cell_transfer, received)
    total = jnp.zeros((RANK, ROWS), jnp.float32)
    sums = [jnp.zeros((ROWS, 1), jnp.float32)] * 3
    for a in range(OWN):
        part = slice(a * LEAF, (a + 1) * LEAF)
        lift = lifts[:, part]
        value = vector[:, part]
        result = value + near[:, part] + mm(local, lift)
        image[:, part] = result
        total = total + mm(lift, result, NT)
        for k, product in enumerate((value * value, value * result, result * result)):
            sums[k] = sums[k] + jnp.sum(product, axis=1, keepdims=True)
    moment[...] = total
    lane = lax.broadcasted_iota(jnp.int32, (ROWS, 128), 1)
    table = jnp.zeros((ROWS, 128), jnp.float32)
    for k, column in enumerate(sums):
        table = jnp.where(lane == k, column, table)
    dots[...] = table


def middle(couplings, cell_transfer, lifts, vector, near, received):
    return pl.pallas_call(
        middle_body,
        out_shape=(shape(ROWS, OWN * LEAF), shape(RANK, ROWS), shape(ROWS, 128)),
        in_specs=[VMEM] * 6,
        out_specs=[VMEM] * 3,
        compiler_params=params(),
        cost_estimate=cost(80_000_000, 3_000_000),
        name="middle",
    )(couplings, cell_transfer, lifts, vector, near, received)


def last_body(cell_transfer, maps, local, lifts, vector, near, boxes, image, extra):
    row = box_local(maps, boxes)
    product = unpacked_rows(row * boxes[lax.axis_index("gx")])
    extra[...] = sum_rows(((3, jnp.sum(product, axis=1, keepdims=True)),))
    expansion = local[...] + mm(cell_transfer[0], unpacked_rows(row), NT)
    for a in range(OWN):
        part = slice(a * LEAF, (a + 1) * LEAF)
        image[:, part] = vector[:, part] + near[:, part] + mm(expansion, lifts[:, part], TN)


def last(cell_transfer, maps, local, lifts, vector, near, boxes):
    return pl.pallas_call(
        last_body,
        out_shape=(shape(ROWS, OWN * LEAF), shape(2, 128)),
        in_specs=[VMEM] * 7,
        out_specs=[VMEM] * 2,
        compiler_params=params(),
        cost_estimate=cost(40_000_000, 3_000_000),
        name="last",
    )(cell_transfer, maps, local, lifts, vector, near, boxes)


def finish_body(received, vector, first, second, iterate, residual):
    table = jnp.sum(received[...], axis=0)
    table = jnp.concatenate([table, jnp.zeros((6, 128), jnp.float32)], axis=0).T
    norm = table[:ROWS, 0:1]
    lean = table[ROWS:, 0:1]
    square = table[:ROWS, 1:2]
    cubic = table[ROWS:, 1:2]
    alpha0 = norm / lean
    norm1 = alpha0 * (alpha0 * square - lean)
    beta = norm1 / norm
    grow = 1.0 + beta
    curve = grow * (grow * lean - 2.0 * alpha0 * square) + alpha0 * alpha0 * cubic
    alpha1 = norm1 / curve
    iterate[...] = (alpha0 + alpha1 * grow) * vector[...] - (alpha1 * alpha0) * first[...]
    residual[...] = (
        vector[...]
        - (alpha0 + alpha1 * grow) * first[...]
        + (alpha1 * alpha0) * second[...]
    )


def finish(received, vector, first, second):
    return pl.pallas_call(
        finish_body,
        out_shape=(shape(ROWS, OWN * LEAF), shape(ROWS, OWN * LEAF)),
        in_specs=[VMEM] * 4,
        out_specs=[VMEM] * 2,
        compiler_params=params(),
        cost_estimate=cost(1_000_000, 3_000_000),
        name="finish",
    )(received, vector, first, second)


def exchange(block, axis, mask):
    count = lax.axis_size(axis)
    return lax.ppermute(block, axis, [(i, i ^ mask) for i in range(count)])


def turn(block, axis):
    return lax.all_to_all(block, axis, 0, 0, tiled=True)


def gathered(block):
    return lax.all_gather(block, "gy", axis=0, tiled=True)


def shards(
    points,
    targets,
    basis,
    leaf_transfer,
    cell_transfer,
    box_parent_transfer,
    cell_coupling,
    box_coupling,
    top_coupling,
    neighbours,
    cell_lists,
):
    partner_points = exchange(points, "gy", 1)
    partner_targets = exchange(targets, "gy", 1)
    lifts, message, cell = up(basis, leaf_transfer, cell_transfer, cell_lists, targets)
    cells = gathered(cell)
    maps = coarse(box_parent_transfer, box_coupling, top_coupling)
    left, right = features(points, partner_points)
    vectors = joined(targets, partner_targets)
    tiles, near = near_tiles(neighbours, left, right, vectors)
    box, picked = route(turn(message, "gy"))
    message = boxes(turn(box, "gx"), maps, picked)
    first, moment, dots = middle(
        cell_coupling, cell_transfer, lifts, targets, near, turn(message, "gy")
    )

    partner_first = exchange(first, "gy", 1)
    received = gathered(moment)
    near = near_again(neighbours, joined(first, partner_first), tiles)
    box, local, sums = tally(
        cell_lists, received, cells, cell_coupling, moment, dots, first, near
    )
    sums = turn(sums, "gy")
    second, extra = last(cell_transfer, maps, local, lifts, first, near, turn(box, "gx"))
    return finish(turn(spread(sums, extra), "gx"), targets, first, second)


def solution(mesh):
    both = ("gx", "gy")
    return jax.shard_map(
        shards,
        mesh=mesh,
        in_specs=(
            P(None, both),
            P(None, both),
            P(both, None, None),
            P(both, None, None),
            P(both, None, None),
            P(),
            P(both, None, None, None),
            P(),
            P(),
            P(both, None),
            P(both, None),
        ),
        out_specs=(P(None, both), P(None, both)),
        check_vma=False,
    )
```

time: 787 us -> 193 us (0.25)
  blocking collectives: 478 us -> 55.3 us
  matrix products: 96.7 us -> 0 us
  loops' own time: 96.7 us -> 0 us
  local copies, waits for them, and re-layouts: 82.7 us -> 8.02 us
  Pallas kernels: 0 us -> 46.7 us
  starting transfers between devices: 13.6 us -> 46.9 us
  waiting for transfers between devices: 0.01 us -> 20.9 us
  other arithmetic: 14.8 us -> 0 us
  between operations: 1.28 us -> 14.3 us
    psum x3 -> x0, blocking collectives: 300 us -> none  [the longest x2 200 us: squares(): return lax.psum(jnp.sum(values * values, axis=1), ('gx', 'gy'))]
    all_gather x6 -> x1, blocking collectives: 178 us -> 33.2 us  [gathered(): return lax.all_gather(block, 'gy', axis=0, tiled=True)]
    dot_general x76 -> x0, matrix products: 96.7 us -> none  [the longest x48 73.6 us: add_slot(): jnp.dot(chosen, matern(dist_sq), precision=exact_solution)]
    another operation x10 -> x0, loops' own time: 96.7 us -> none  [the longest x8 96.6 us: one_leaf(): lax.scan(add_slot, jnp.zeros((rhs_count, leaf_size), jnp.float32), (near_...]
    dynamic_slice x96 -> x0, local copies, waits for them, and re-layouts: 51 us -> none  [the longest x48 45.6 us: one_leaf(): lax.scan(add_slot, jnp.zeros((rhs_count, leaf_size), jnp.float32), (near_...]
    pallas_call x0 -> x14, Pallas kernels: none -> 46.7 us  [the longest x1 17.6 us: near_tiles(): pl.pallas_call(tiles_body, grid=(OWN,), out_shape=(tile, shape(ROWS, OWN...]
    all_to_all x0 -> x4, starting transfers between devices: none -> 33.5 us  [turn(): return lax.all_to_all(block, axis, 0, 0, tiled=True)]
    all_to_all x0 -> x2, blocking collectives: none -> 22.1 us  [turn(): return lax.all_to_all(block, axis, 0, 0, tiled=True)]
  transfers between devices with their start and end apart: 3 -> 8, of which waited for: 0 -> 3; matrix products, arithmetic and copies ran while one was open for 4% -> 0% of each run, Pallas kernels for 0% -> 22%
where the time goes in v1:
time: 193 us; the launch traced here: 192 us
  blocking collectives  55.3 us (29%)
  starting transfers between devices  46.9 us (24%)
  Pallas kernels  46.7 us (24%)
  waiting for transfers between devices  20.9 us (11%)
  between operations  14.3 us (7%)
  local copies, waits for them, and re-layouts  8.02 us (4%)
    all_to_all x4, starting transfers between devices, turn(): return lax.all_to_all(block, axis, 0, 0, tiled=True)  33.5 us
    all_gather x1, blocking collectives, gathered(): return lax.all_gather(block, 'gy', axis=0, tiled=True)  33.2 us
    all_to_all x2, blocking collectives, turn(): return lax.all_to_all(block, axis, 0, 0, tiled=True)  22.1 us
    all_to_all x4, waiting for transfers between devices, turn(): return lax.all_to_all(block, axis, 0, 0, tiled=True)  20.2 us
    pallas_call x1, Pallas kernels, near_tiles(): pl.pallas_call(tiles_body, grid=(OWN,), out_shape=(tile, shape(ROWS, OWN...  17.6 us
    ppermute x3, starting transfers between devices, exchange(): return lax.ppermute(block, axis, [(i, i ^ mask) for i in range(count)])  13.3 us
    pallas_call x1, Pallas kernels, near_again(): pl.pallas_call(again_body, grid=(OWN, 2), out_shape=shape(ROWS, OWN * LEA...  11.9 us
    unnamed x30, local copies, waits for them, and re-layouts  8.02 us
  transfers between devices with their start and end apart: 8, of which 3 were waited for; matrix products, arithmetic and copies ran while one was open for 0% of the time, Pallas kernels for 22%

profile of v1, /device:TPU:1, one launch (start us, length us, event | category | flops | bytes accessed | tf_op | source)
XLA Modules:
  0.0 192.1 jit_solution(6645119097915901066)
XLA Ops:
  7.2 8.9 %collective-permute-start.1 = (f32[64,2048]{1,0:T(8,128)}, f32[64,2048]{1,0:T(8,128)S(1)}, u32[]{:S(2)}, u32[]{:S(2)}) collective-permute-start(f32[64,2048]{1,0:T(8,128)} %vector.5), channel_id=1, source_target_pairs={{0,1},{1,0},{2,3},{3,2},{4,5},{5,4},{6,7},{7,6},{8,9},{9,8},{10,11... | collective-permute-start | bytes 1572872 | tf_op jit(solution)/shard_map/ppermute | solution.py:554
  16.1 4.2 %up.1 = (f32[64,2048]{1,0:T(8,128)}, f32[32,1,384]{2,1,0:T(1,128)}, f32[64,128]{1,0:T(8,128)}) custom-call(f32[4,64,512]{2,1,0:T(8,128)} %basis.1, f32[4,64,64]{2,1,0:T(8,128)} %leaf_transfer.1, f32[1,64,64]{2,1,0:T(8,128)} %cell_transfer.5, s32[1,4]{1,0:T(1,128)} %lists.3, f32[64,2048]{1,0:T(8,128)} %vector.5), custom_call_target="tpu_custom_call" | custom-call | flops 60000000 | bytes 2000000 | tf_op jit(solution)/shard_map/up/pallas_call | solution.py:109
  20.4 10.1 %all-to-all-start = ((f32[32,1,384]{2,1,0:T(1,128)}), f32[32,1,384]{2,1,0:T(1,128)S(1)}, u32[]{:S(2)}, u32[]{:S(2)}) async-start(f32[32,1,384]{2,1,0:T(1,128)} %get-tuple-element.23), calls=%async_computation | async-start | bytes 98304 | tf_op jit(solution)/shard_map/all_to_all | solution.py:558
  30.6 0.7 all-gather.2.cloned.1.call-update
  31.3 2.1 %collective-permute-start = (f32[3,2048]{1,0:T(4,128)}, f32[3,2048]{1,0:T(4,128)S(1)}, u32[]{:S(2)}, u32[]{:S(2)}) collective-permute-start(f32[3,2048]{1,0:T(4,128)} %own.2), channel_id=1, source_target_pairs={{0,1},{1,0},{2,3},{3,2},{4,5},{5,4},{6,7},{7,6},{8,9},{9,8},{10,11... | collective-permute-start | bytes 73736 | tf_op jit(solution)/shard_map/ppermute | solution.py:554
  33.4 9.6 %all-to-all-done.received = f32[32,1,384]{2,1,0:T(1,128)S(1)} async-done(((f32[32,1,384]{2,1,0:T(1,128)}), f32[32,1,384]{2,1,0:T(1,128)S(1)}, u32[]{:S(2)}, u32[]{:S(2)}) %all-to-all-start) | async-done | bytes 49184 | tf_op jit(solution)/shard_map/all_to_all | solution.py:558
  43.0 0.9 route.1
  44.0 6.8 %all-to-all-start.1 = ((f32[16,1,128]{2,1,0:T(1,128)}), f32[16,1,128]{2,1,0:T(1,128)S(1)}, u32[]{:S(2)}, u32[]{:S(2)}) async-start(f32[16,1,128]{2,1,0:T(1,128)} %get-tuple-element.24), calls=%async_computation.1 | async-start | bytes 16384 | tf_op jit(solution)/shard_map/all_to_all | solution.py:558
  50.7 3.2 %coarse.1.maps = f32[1152,128]{1,0:T(8,128)} custom-call(f32[16,64,64]{2,1,0:T(8,128)} %parent_ref.1, f32[16,3,64,64]{3,2,1,0:T(8,128)} %box_ref.1, f32[8,4,64,64]{3,2,1,0:T(8,128)} %top_ref.1), custom_call_target="tpu_custom_call" | custom-call | flops 50000000 | bytes 2000000 | tf_op jit(solution)/shard_map/coarse/pallas_call | solution.py:159
  54.0 0.7 copy-done.9
  55.2 1.0 copy-done.13
  56.2 0.8 all-to-all-done.1.received
  57.0 1.1 copy-done.2
  58.1 1.0 boxes.1
  59.1 6.4 %all-to-all-start.2 = ((f32[32,1,640]{2,1,0:T(1,128)}), f32[32,1,640]{2,1,0:T(1,128)S(1)}, u32[]{:S(2)}, u32[]{:S(2)}) async-start(f32[32,1,640]{2,1,0:T(1,128)} %boxes.1), calls=%async_computation.2 | async-start | bytes 163840 | tf_op jit(solution)/shard_map/all_to_all | solution.py:558
  65.6 1.0 copy-done
  66.7 0.7 copy-done.10
  67.4 1.2 copy-done.14
  68.6 17.6 %near_tiles.1 = (bf16[4,6,2,512,512]{4,3,2,1,0:T(8,128)(2,1)}, f32[64,2048]{1,0:T(8,128)S(1)}) custom-call(s32[4,6]{1,0:T(4,128)S(1)} %copy-done.10, bf16[8,512,32]{2,1,0:T(8,128)(2,1)S(1)} %copy-done.14, bf16[4,32,512]{2,1,0:T(8,128)(2,1)S(1)} %get-tuple-element.21.right, bf16[8,128,512]{2,1,0:T(8,128)(2,1)S(1)} %joined.2.vectors), custom_call_target="tpu_custom_call" | custom-call | flops 8000000000 | bytes 30000000 | tf_op jit(solution)/shard_map/near_tiles/pallas_call | solution.py:396
  86.3 2.0 %middle.1 = (f32[64,2048]{1,0:T(8,128)S(1)}, f32[64,64]{1,0:T(8,128)S(1)}, f32[64,128]{1,0:T(8,128)S(1)}) custom-call(f32[1,4,64,64]{3,2,1,0:T(8,128)S(1)} %copy-done.7, f32[1,64,64]{2,1,0:T(8,128)S(1)} %copy-done.8, f32[64,2048]{1,0:T(8,128)S(1)} %copy-done.4, f32[64,2048]{1,0:T(8,128)S(1)} %copy-done.1, f32[64,2048]{1,0:T(8,128)S(1)} %get-tuple-element.22.near, ...), custom_call_target="tpu_custom_call" | custom-call | flops 80000000 | bytes 3000000 | tf_op jit(solution)/shard_map/middle/pallas_call | solution.py:486
  88.3 2.3 %collective-permute-start.2 = (f32[64,2048]{1,0:T(8,128)S(1)}, f32[64,2048]{1,0:T(8,128)S(1)}, u32[]{:S(2)}, u32[]{:S(2)}) collective-permute-start(f32[64,2048]{1,0:T(8,128)S(1)} %get-tuple-element.29.own.image.vector.first), channel_id=1, source_target_pairs={{0,1},{1,0},{2,3},{3,2},{4,5},{5,4},{6,7},{7,6},{8,9},{9,8},{10,11... | collective-permute-start | bytes 1572872 | tf_op jit(solution)/shard_map/ppermute | solution.py:554
  90.5 33.2 %all_gather.6.received = f32[2048,64]{1,0:T(8,128)S(1)} all-gather(f32[64,64]{1,0:T(8,128)S(1)} %get-tuple-element.26.moment), channel_id=1, replica_groups=mesh['gx'=16,'gy'=32] {'gy'}, dimensions={0}, use_global_device_ids=true | all-gather | bytes 540672 | tf_op jit(solution)/shard_map/all_gather | solution.py:562
  123.9 11.9 %near_again.1.near = f32[64,2048]{1,0:T(8,128)S(1)} custom-call(s32[4,6]{1,0:T(4,128)S(1)} %copy-done.11, bf16[8,128,512]{2,1,0:T(8,128)(2,1)S(1)} %joined.3.vectors, bf16[4,6,2,512,512]{4,3,2,1,0:T(8,128)(2,1)} %get-tuple-element.30.high_tiles.low_tiles, bf16[4,6,2,512,512]{4,3,2,1,0:T(8,128)(2,1)} %get-tuple-element.30.high_tiles.low_tiles), custom_call_target="tpu_custom_call" | custom-call | flops 6000000000 | bytes 30000000 | tf_op jit(solution)/shard_map/near_again/pallas_call | solution.py:432
  135.8 1.2 copy-done.6
  137.1 2.3 %tally.1 = (f32[16,32,128]{2,1,0:T(8,128)S(1)}, f32[64,64]{1,0:T(8,128)S(1)}, f32[32,2,128]{2,1,0:T(2,128)}) custom-call(s32[1,4]{1,0:T(1,128)S(1)} %copy-done.12, f32[2048,64]{1,0:T(8,128)S(1)} %all_gather.6.received, f32[2048,128]{1,0:T(8,128)S(1)} %copy-done.6, f32[1,4,64,64]{3,2,1,0:T(8,128)S(1)} %copy-done.7, f32[64,64]{1,0:T(8,128)S(1)} %get-tuple-element.26.moment, ...), custom_call_target="tpu_custom_call" | custom-call | flops 4000000 | bytes 2500000 | tf_op jit(solution)/shard_map/tally/pallas_call | solution.py:257
  139.3 13.1 %all_to_all.30.boxes = f32[16,32,128]{2,1,0:T(8,128)S(1)} all-to-all(f32[16,32,128]{2,1,0:T(8,128)S(1)} %get-tuple-element.33), channel_id=1, replica_groups=mesh['gx'=16,'gy'=32] {'gx'}, dimensions={0} | all-to-all | bytes 524288 | tf_op jit(solution)/shard_map/all_to_all | solution.py:558
  152.4 10.3 %all-to-all-start.3 = ((f32[32,2,128]{2,1,0:T(2,128)}), f32[32,2,128]{2,1,0:T(2,128)S(1)}, u32[]{:S(2)}, u32[]{:S(2)}) async-start(f32[32,2,128]{2,1,0:T(2,128)} %get-tuple-element.31), calls=%async_computation.3 | async-start | bytes 65536 | tf_op jit(solution)/shard_map/all_to_all | solution.py:558
  162.7 1.0 copy-done.5
  163.7 1.3 last.1
  165.1 9.7 %all-to-all-done.3.received = f32[32,2,128]{2,1,0:T(2,128)S(1)} async-done(((f32[32,2,128]{2,1,0:T(2,128)}), f32[32,2,128]{2,1,0:T(2,128)S(1)}, u32[]{:S(2)}, u32[]{:S(2)}) %all-to-all-start.3) | async-done | bytes 32800 | tf_op jit(solution)/shard_map/all_to_all | solution.py:558
  174.8 9.1 %all_to_all.31.received = f32[16,2,128]{2,1,0:T(2,128)S(1)} all-to-all(f32[16,2,128]{2,1,0:T(2,128)S(1)} %spread.1), channel_id=1, replica_groups=mesh['gx'=16,'gy'=32] {'gx'}, dimensions={0} | all-to-all | bytes 32768 | tf_op jit(solution)/shard_map/all_to_all | solution.py:558
  183.9 1.4 finish.1
  (32 shorter events, 0.9 us)
Async XLA Ops:
  7.2 79.1 %copy-start.1 = (f32[64,2048]{1,0:T(8,128)S(1)}, f32[64,2048]{1,0:T(8,128)}, u32[]{:S(2)}) copy-start(f32[64,2048]{1,0:T(8,128)} %vector.5) | copy-start | bytes 1572868
  7.2 79.1 %copy-start.8 = (f32[1,64,64]{2,1,0:T(8,128)S(1)}, f32[1,64,64]{2,1,0:T(8,128)}, u32[]{:S(2)}) copy-start(f32[1,64,64]{2,1,0:T(8,128)} %cell_transfer.5) | copy-start | bytes 49156
  7.2 116.7 %copy-start.11 = (s32[4,6]{1,0:T(4,128)S(1)}, s32[4,6]{1,0:T(4,128)}, u32[]{:S(2)}) copy-start(s32[4,6]{1,0:T(4,128)} %neighbours.3) | copy-start | bytes 292
  7.2 79.1 %copy-start.7 = (f32[1,4,64,64]{3,2,1,0:T(8,128)S(1)}, f32[1,4,64,64]{3,2,1,0:T(8,128)}, u32[]{:S(2)}) copy-start(f32[1,4,64,64]{3,2,1,0:T(8,128)} %couplings.3) | copy-start | bytes 196612
  7.2 58.3 %collective-permute-start.1 = (f32[64,2048]{1,0:T(8,128)}, f32[64,2048]{1,0:T(8,128)S(1)}, u32[]{:S(2)}, u32[]{:S(2)}) collective-permute-start(f32[64,2048]{1,0:T(8,128)} %vector.5), channel_id=1, source_target_pairs={{0,1},{1,0},{2,3},{3,2},{4,5},{5,4},{6,7},{7,6},{8,9},{9,8},{10,11... | collective-permute-start | bytes 1572872 | tf_op jit(solution)/shard_map/ppermute | solution.py:554
  20.4 65.9 %copy-start.4 = (f32[64,2048]{1,0:T(8,128)S(1)}, f32[64,2048]{1,0:T(8,128)}, u32[]{:S(2)}) copy-start(f32[64,2048]{1,0:T(8,128)} %get-tuple-element.19.lifts) | copy-start | bytes 1572868
  20.4 22.6 %all-to-all-start = ((f32[32,1,384]{2,1,0:T(1,128)}), f32[32,1,384]{2,1,0:T(1,128)S(1)}, u32[]{:S(2)}, u32[]{:S(2)}) async-start(f32[32,1,384]{2,1,0:T(1,128)} %get-tuple-element.23), calls=%async_computation | async-start | bytes 98304 | tf_op jit(solution)/shard_map/all_to_all | solution.py:558
  30.5 105.3 %all-gather.2.cloned.1.call-start = ((), (), s32[]{:S(2)}) async-start(), calls=%async_computation.6 | async-start | bytes 1081344 | tf_op jit(solution)/shard_map/all_gather | solution.py:562
  31.3 22.7 %collective-permute-start = (f32[3,2048]{1,0:T(4,128)}, f32[3,2048]{1,0:T(4,128)S(1)}, u32[]{:S(2)}, u32[]{:S(2)}) collective-permute-start(f32[3,2048]{1,0:T(4,128)} %own.2), channel_id=1, source_target_pairs={{0,1},{1,0},{2,3},{3,2},{4,5},{5,4},{6,7},{7,6},{8,9},{9,8},{10,11... | collective-permute-start | bytes 73736 | tf_op jit(solution)/shard_map/ppermute | solution.py:554
  44.0 13.1 %all-to-all-start.1 = ((f32[16,1,128]{2,1,0:T(1,128)}), f32[16,1,128]{2,1,0:T(1,128)S(1)}, u32[]{:S(2)}, u32[]{:S(2)}) async-start(f32[16,1,128]{2,1,0:T(1,128)} %get-tuple-element.24), calls=%async_computation.1 | async-start | bytes 16384 | tf_op jit(solution)/shard_map/all_to_all | solution.py:558
  54.0 0.8 copy-start.9
  55.2 1.0 copy-start.13
  57.0 1.1 copy-start.2
  59.1 27.1 %all-to-all-start.2 = ((f32[32,1,640]{2,1,0:T(1,128)}), f32[32,1,640]{2,1,0:T(1,128)S(1)}, u32[]{:S(2)}, u32[]{:S(2)}) async-start(f32[32,1,640]{2,1,0:T(1,128)} %boxes.1), calls=%async_computation.2 | async-start | bytes 163840 | tf_op jit(solution)/shard_map/all_to_all | solution.py:558
  65.6 1.0 copy-start
  66.7 0.7 copy-start.10
  67.4 1.2 copy-start.14
  88.3 35.5 %collective-permute-start.2 = (f32[64,2048]{1,0:T(8,128)S(1)}, f32[64,2048]{1,0:T(8,128)S(1)}, u32[]{:S(2)}, u32[]{:S(2)}) collective-permute-start(f32[64,2048]{1,0:T(8,128)S(1)} %get-tuple-element.29.own.image.vector.first), channel_id=1, source_target_pairs={{0,1},{1,0},{2,3},{3,2},{4,5},{5,4},{6,7},{7,6},{8,9},{9,8},{10,11... | collective-permute-start | bytes 1572872 | tf_op jit(solution)/shard_map/ppermute | solution.py:554
  123.9 11.9 %copy-start.12 = (s32[1,4]{1,0:T(1,128)S(1)}, s32[1,4]{1,0:T(1,128)}, u32[]{:S(2)}) copy-start(s32[1,4]{1,0:T(1,128)} %lists.3) | copy-start | bytes 52
  123.9 38.8 %copy-start.3 = (f32[1152,128]{1,0:T(8,128)S(1)}, f32[1152,128]{1,0:T(8,128)}, u32[]{:S(2)}) copy-start(f32[1152,128]{1,0:T(8,128)} %coarse.1.maps) | copy-start | bytes 1769476
  135.8 1.2 copy-start.6
  152.4 22.4 %all-to-all-start.3 = ((f32[32,2,128]{2,1,0:T(2,128)}), f32[32,2,128]{2,1,0:T(2,128)S(1)}, u32[]{:S(2)}, u32[]{:S(2)}) async-start(f32[32,2,128]{2,1,0:T(2,128)} %get-tuple-element.31), calls=%async_computation.3 | async-start | bytes 65536 | tf_op jit(solution)/shard_map/all_to_all | solution.py:558
  162.7 1.0 copy-start.5
Sparse Core Ops, SparseCore 0:
  33.5 72.3 all-gather.1

commit v2 on v1

--- a/solution.py
+++ b/solution.py
@@ -81,11 +81,23 @@
     return copies
 
 
+def send_moments(message, moment, cell_transfer):
+    message[:, 0, 0:128] = packed_rows(moment)
+    message[:, 0, 128:256] = packed_rows(mm(moment, cell_transfer))
+
+
 def up_body(
-    basis, leaf_transfer, cell_transfer, lists, vector, lifts, message, cell, b, t, c, v, sems
+    basis, leaf_transfer, cell_transfer, lists, vector, points, lifts, message, v, p, b, t, c, sems
 ):
     copies = fetch(
-        ((leaf_transfer, t), (basis, b), (vector, v), (cell_transfer, c)), sems
+        (
+            (leaf_transfer, t),
+            (basis, b),
+            (vector, v),
+            (cell_transfer, c),
+            (points, p),
+        ),
+        sems,
     )
     for copy in copies:
         copy.wait()
@@ -94,38 +106,35 @@
         lift = mm(t[a], b[a], TN)
         lifts[:, a * LEAF : (a + 1) * LEAF] = lift
         total = total + mm(v[:, a * LEAF : (a + 1) * LEAF], lift, NT)
-    message[:, 0, 0:128] = packed_rows(total)
-    message[:, 0, 128:256] = packed_rows(mm(total, c[0]))
+    send_moments(message, total, c[0])
     lane = lax.broadcasted_iota(jnp.int32, (GROUP, 128), 1)
     table = jnp.zeros((GROUP, 128), jnp.int32)
     for k in range(LIST):
         table = jnp.where(lane == k, lists[0, k] & (GROUP - 1), table)
     message[:, 0, 256:384] = table.astype(jnp.float32)
-    cell[:, :RANK] = c[0]
-    cell[:, RANK:] = c[0]
-
-
-def up(basis, leaf_transfer, cell_transfer, cell_lists, vector):
+
+
+def up(basis, leaf_transfer, cell_transfer, cell_lists, vector, points):
     return pl.pallas_call(
         up_body,
         out_shape=(
             shape(RANK, OWN * LEAF),
             shape(GROUP, 1, 384),
-            shape(RANK, 2 * RANK),
+            shape(ROWS, OWN * LEAF),
+            shape(3, OWN * LEAF),
         ),
-        in_specs=[ANY] * 3 + [SMEM, ANY],
-        out_specs=[VMEM] * 3,
+        in_specs=[ANY] * 3 + [SMEM, ANY, ANY],
+        out_specs=[VMEM] * 4,
         scratch_shapes=[
             pltpu.VMEM((OWN, RANK, LEAF), jnp.float32),
             pltpu.VMEM((OWN, RANK, RANK), jnp.float32),
             pltpu.VMEM((1, RANK, RANK), jnp.float32),
-            pltpu.VMEM((ROWS, OWN * LEAF), jnp.float32),
-            pltpu.SemaphoreType.DMA((4,)),
+            pltpu.SemaphoreType.DMA((5,)),
         ],
         compiler_params=params(60),
         cost_estimate=cost(60_000_000, 2_000_000),
         name="up",
-    )(basis, leaf_transfer, cell_transfer, cell_lists, vector)
+    )(basis, leaf_transfer, cell_transfer, cell_lists, vector, points)
 
 
 def coarse_body(parent_ref, box_ref, top_ref, out, parent, box_coupling, top_coupling, sems):
@@ -173,27 +182,39 @@
     )(parent, box_coupling, top_coupling)
 
 
-def route_body(received, box, picked):
+def route_body(with_lists, received, lists, *outs):
+    box, picked = outs[0], outs[1]
     chunk = jnp.sum(received[:, 0, 128:256], axis=0, keepdims=True)
     box[...] = jnp.broadcast_to(chunk[None], box.shape)
     cells = received[:, 0, 0:128]
-    numbers = received[:, 0, 256:384]
+    numbers = received[:, 0, 256:384] if with_lists else lists[...]
     member = lax.broadcasted_iota(jnp.int32, (GROUP, GROUP), 1).astype(jnp.float32)
-    for k in range(LIST):
-        chooser = (numbers[:, k : k + 1] == member).astype(jnp.float32)
-        picked[:, k * 128 : (k + 1) * 128] = mm(chooser, cells)
-
-
-def route(received):
-    return pl.pallas_call(
-        route_body,
-        out_shape=(shape(16, 1, 128), shape(GROUP, LIST * 128)),
-        in_specs=[VMEM],
-        out_specs=[VMEM] * 2,
+    for s in range(LIST):
+        chooser = (numbers[:, s : s + 1] == member).astype(jnp.float32)
+        picked[:, 0, s * 128 : (s + 1) * 128] = mm(chooser, cells)
+    if with_lists:
+        outs[2][...] = numbers
+
+
+def route(received, lists=None):
+    first = lists is None
+    outs = (shape(16, 1, 128), shape(GROUP, 1, LIST * 128))
+    if first:
+        body = lambda received, *outs: route_body(True, received, None, *outs)
+        outs = outs + (shape(GROUP, 128),)
+        operands = (received,)
+    else:
+        body = functools.partial(route_body, False)
+        operands = (received, lists)
+    return pl.pallas_call(
+        body,
+        out_shape=outs,
+        in_specs=[VMEM] * len(operands),
+        out_specs=[VMEM] * len(outs),
         compiler_params=params(),
         cost_estimate=cost(4_000_000, 200_000),
         name="route",
-    )(received)
+    )(*operands)
 
 
 def boxes_body(received, maps, picked, message):
@@ -203,7 +224,7 @@
     )
     local = mm(row, maps[...])
     message[:, 0, 0:128] = jnp.broadcast_to(local, (GROUP, 128))
-    message[:, 0, 128:640] = picked[...]
+    message[:, 0, 128:640] = picked[:, 0, :]
 
 
 def boxes(received, maps, picked):
@@ -230,56 +251,60 @@
 
 
 def tally_body(
-    lists, received, cells, couplings, moment, dots, image, near, box, local, sums
+    couplings, maps, moment, dots, image, near, picked, received, local, chunk, sums
 ):
-    total = mm(received[...], cells[:, :RANK], TN)
-    box[...] = jnp.broadcast_to(packed_rows(total)[None], box.shape)
-    expansion = jnp.zeros((RANK, ROWS), jnp.float32)
+    expansion = jnp.zeros((ROWS, RANK), jnp.float32)
     for k in range(LIST):
-        low = pl.multiple_of((lists[0, k] & (GROUP - 1)) * RANK, RANK)
-        expansion = expansion + mm(couplings[0, k], received[pl.ds(low, RANK), :])
+        part = unpacked_rows(picked[:, 0, k * 128 : (k + 1) * 128])
+        expansion = expansion + mm(part, couplings[0, k], NT)
     local[...] = expansion
     square = dots[:, 2:3]
-    cubic = square
+    cubic = square + jnp.sum(moment[...] * expansion, axis=1, keepdims=True)
     for a in range(OWN):
         part = slice(a * LEAF, (a + 1) * LEAF)
         cubic = cubic + jnp.sum(image[:, part] * near[:, part], axis=1, keepdims=True)
     rows = sum_rows(((0, dots[:, 0:1]), (1, dots[:, 1:2]), (2, square), (3, cubic)))
-    far = jnp.sum(moment[...] * expansion, axis=0, keepdims=True)
-    blank = jnp.zeros((1, RANK), jnp.float32)
-    rows = rows + jnp.concatenate(
-        [jnp.zeros((1, 128), jnp.float32), jnp.concatenate([blank, far], axis=1)], axis=0
-    )
+    row = box_local(maps, received)
+    chunk[...] = row
+    product = row * received[lax.axis_index("gx")]
+    place = lax.broadcasted_iota(jnp.int32, (2, 128), 0) * 128
+    place = place + lax.broadcasted_iota(jnp.int32, (2, 128), 1)
+    column = 128 + RANK + lax.axis_index("gy")
+    for half in range(2):
+        term = jnp.sum(product[:, half * RANK : (half + 1) * RANK], axis=1, keepdims=True)
+        rows = rows + jnp.where(place == column + half * (ROWS // 2), term, 0.0)
     sums[...] = jnp.broadcast_to(rows[None], sums.shape)
 
 
-def tally(lists, received, cells, couplings, moment, dots, image, near):
+def tally(couplings, maps, moment, dots, image, near, picked, received):
     return pl.pallas_call(
         tally_body,
-        out_shape=(shape(16, 32, 128), shape(RANK, ROWS), shape(GROUP, 2, 128)),
-        in_specs=[SMEM] + [VMEM] * 7,
+        out_shape=(shape(ROWS, RANK), shape(1, 128), shape(16, 2, 128)),
+        in_specs=[VMEM] * 8,
         out_specs=[VMEM] * 3,
         compiler_params=params(),
         cost_estimate=cost(4_000_000, 2_500_000),
         name="tally",
-    )(lists, received, cells, couplings, moment, dots, image, near)
-
-
-def spread_body(received, extra, sums):
-    total = jnp.sum(received[...], axis=0, keepdims=True) + extra[...][None]
-    sums[...] = jnp.broadcast_to(total, sums.shape)
-
-
-def spread(received, extra):
+    )(couplings, maps, moment, dots, image, near, picked, received)
+
+
+def spread_body(received, chunk, message):
+    total = jnp.sum(received[...], axis=0)
+    message[:, 0, 0:128] = jnp.broadcast_to(total[0:1], (GROUP, 128))
+    message[:, 0, 128:256] = jnp.broadcast_to(total[1:2], (GROUP, 128))
+    message[:, 0, 256:384] = jnp.broadcast_to(chunk[...], (GROUP, 128))
+
+
+def spread(received, chunk):
     return pl.pallas_call(
         spread_body,
-        out_shape=shape(16, 2, 128),
+        out_shape=shape(GROUP, 1, 384),
         in_specs=[VMEM] * 2,
         out_specs=VMEM,
         compiler_params=params(),
         cost_estimate=cost(10_000, 50_000),
         name="spread",
-    )(received, extra)
+    )(received, chunk)
 
 
 def features_body(own, partner, left, right, rows):
@@ -406,7 +431,8 @@
     )(neighbours, left, right, vectors)
 
 
-def again_body(neighbours, vectors, high_tiles, low_tiles, out):
+def again_body(neighbours, vectors, high_tiles, low_tiles, box, out, box_out):
+    box_out[...] = box[...]
     leaf = pl.program_id(0)
     wide = jnp.zeros((2 * ROWS, LEAF), jnp.float32)
     narrow = jnp.zeros((ROWS, LEAF), jnp.float32)
@@ -425,20 +451,20 @@
         out[...] += value
 
 
-def near_again(neighbours, vectors, tiles):
+def near_again(neighbours, vectors, tiles, box):
     half = (1, SLOTS // 2, 1, LEAF, LEAF)
     high = pl.BlockSpec(half, lambda a, h: (a, h, 0, 0, 0))
     low = pl.BlockSpec(half, lambda a, h: (a, h, 1, 0, 0))
     return pl.pallas_call(
         again_body,
         grid=(OWN, 2),
-        out_shape=shape(ROWS, OWN * LEAF),
-        in_specs=[SMEM, VMEM, high, low],
-        out_specs=pl.BlockSpec((ROWS, LEAF), lambda a, h: (0, a)),
+        out_shape=(shape(ROWS, OWN * LEAF), shape(*box.shape)),
+        in_specs=[SMEM, VMEM, high, low, VMEM],
+        out_specs=[pl.BlockSpec((ROWS, LEAF), lambda a, h: (0, a)), VMEM],
         compiler_params=params(40),
         cost_estimate=cost(6_000_000_000, 30_000_000),
         name="near_again",
-    )(neighbours, vectors, tiles, tiles)
+    )(neighbours, vectors, tiles, tiles, box)
 
 
 def box_local(maps, boxes):
@@ -460,10 +486,10 @@
 
 
 def middle_body(
-    couplings, cell_transfer, lifts, vector, near, received, image, moment, dots
+    couplings, cell_transfer, lifts, vector, near, received, image, message, moment, dots
 ):
     local = cell_local(couplings, cell_transfer, received)
-    total = jnp.zeros((RANK, ROWS), jnp.float32)
+    total = jnp.zeros((ROWS, RANK), jnp.float32)
     sums = [jnp.zeros((ROWS, 1), jnp.float32)] * 3
     for a in range(OWN):
         part = slice(a * LEAF, (a + 1) * LEAF)
@@ -471,9 +497,10 @@
         value = vector[:, part]
         result = value + near[:, part] + mm(local, lift)
         image[:, part] = result
-        total = total + mm(lift, result, NT)
+        total = total + mm(result, lift, NT)
         for k, product in enumerate((value * value, value * result, result * result)):
             sums[k] = sums[k] + jnp.sum(product, axis=1, keepdims=True)
+    send_moments(message, total, cell_transfer[0])
     moment[...] = total
     lane = lax.broadcasted_iota(jnp.int32, (ROWS, 128), 1)
     table = jnp.zeros((ROWS, 128), jnp.float32)
@@ -485,68 +512,52 @@
 def middle(couplings, cell_transfer, lifts, vector, near, received):
     return pl.pallas_call(
         middle_body,
-        out_shape=(shape(ROWS, OWN * LEAF), shape(RANK, ROWS), shape(ROWS, 128)),
+        out_shape=(shape(ROWS, OWN * LEAF), shape(GROUP, 1, 256), shape(ROWS, RANK), shape(ROWS, 128)),
         in_specs=[VMEM] * 6,
-        out_specs=[VMEM] * 3,
+        out_specs=[VMEM] * 4,
         compiler_params=params(),
         cost_estimate=cost(80_000_000, 3_000_000),
         name="middle",
     )(couplings, cell_transfer, lifts, vector, near, received)
 
 
-def last_body(cell_transfer, maps, local, lifts, vector, near, boxes, image, extra):
-    row = box_local(maps, boxes)
-    product = unpacked_rows(row * boxes[lax.axis_index("gx")])
-    extra[...] = sum_rows(((3, jnp.sum(product, axis=1, keepdims=True)),))
-    expansion = local[...] + mm(cell_transfer[0], unpacked_rows(row), NT)
-    for a in range(OWN):
-        part = slice(a * LEAF, (a + 1) * LEAF)
-        image[:, part] = vector[:, part] + near[:, part] + mm(expansion, lifts[:, part], TN)
-
-
-def last(cell_transfer, maps, local, lifts, vector, near, boxes):
-    return pl.pallas_call(
-        last_body,
-        out_shape=(shape(ROWS, OWN * LEAF), shape(2, 128)),
-        in_specs=[VMEM] * 7,
-        out_specs=[VMEM] * 2,
-        compiler_params=params(),
-        cost_estimate=cost(40_000_000, 3_000_000),
-        name="last",
-    )(cell_transfer, maps, local, lifts, vector, near, boxes)
-
-
-def finish_body(received, vector, first, second, iterate, residual):
-    table = jnp.sum(received[...], axis=0)
-    table = jnp.concatenate([table, jnp.zeros((6, 128), jnp.float32)], axis=0).T
+def finish_body(cell_transfer, lifts, local, near, vector, first, received, iterate, residual):
+    expansion = local[...] + mm(
+        unpacked_rows(received[:, 0, 256:384]), cell_transfer[0], NT
+    )
+    table = jnp.sum(received[:, 0, 0:256], axis=0, keepdims=True)
+    table = jnp.concatenate([table, jnp.zeros((7, 256), jnp.float32)], axis=0).T
     norm = table[:ROWS, 0:1]
-    lean = table[ROWS:, 0:1]
-    square = table[:ROWS, 1:2]
-    cubic = table[ROWS:, 1:2]
+    lean = table[ROWS : 2 * ROWS, 0:1]
+    square = table[2 * ROWS : 3 * ROWS, 0:1]
+    cubic = table[3 * ROWS :, 0:1]
     alpha0 = norm / lean
     norm1 = alpha0 * (alpha0 * square - lean)
     beta = norm1 / norm
     grow = 1.0 + beta
     curve = grow * (grow * lean - 2.0 * alpha0 * square) + alpha0 * alpha0 * cubic
     alpha1 = norm1 / curve
-    iterate[...] = (alpha0 + alpha1 * grow) * vector[...] - (alpha1 * alpha0) * first[...]
-    residual[...] = (
-        vector[...]
-        - (alpha0 + alpha1 * grow) * first[...]
-        + (alpha1 * alpha0) * second[...]
-    )
-
-
-def finish(received, vector, first, second):
+    both = alpha0 + alpha1 * grow
+    cross = alpha1 * alpha0
+    for a in range(OWN):
+        part = slice(a * LEAF, (a + 1) * LEAF)
+        start = vector[:, part]
+        image = first[:, part]
+        second = image + near[:, part] + mm(expansion, lifts[:, part])
+        iterate[:, part] = both * start - cross * image
+        residual[:, part] = start - both * image + cross * second
+
+
+def finish(cell_transfer, lifts, local, near, vector, first, received):
     return pl.pallas_call(
         finish_body,
         out_shape=(shape(ROWS, OWN * LEAF), shape(ROWS, OWN * LEAF)),
-        in_specs=[VMEM] * 4,
+        in_specs=[VMEM] * 7,
         out_specs=[VMEM] * 2,
         compiler_params=params(),
-        cost_estimate=cost(1_000_000, 3_000_000),
+        cost_estimate=cost(20_000_000, 3_000_000),
         name="finish",
-    )(received, vector, first, second)
+    )(cell_transfer, lifts, local, near, vector, first, received)
 
 
 def exchange(block, axis, mask):
@@ -556,10 +567,6 @@
 
 def turn(block, axis):
     return lax.all_to_all(block, axis, 0, 0, tiled=True)
-
-
-def gathered(block):
-    return lax.all_gather(block, "gy", axis=0, tiled=True)
 
 
 def shards(
@@ -575,29 +582,30 @@
     neighbours,
     cell_lists,
 ):
+    lifts, message, targets, points = up(
+        basis, leaf_transfer, cell_transfer, cell_lists, targets, points
+    )
     partner_points = exchange(points, "gy", 1)
     partner_targets = exchange(targets, "gy", 1)
-    lifts, message, cell = up(basis, leaf_transfer, cell_transfer, cell_lists, targets)
-    cells = gathered(cell)
     maps = coarse(box_parent_transfer, box_coupling, top_coupling)
     left, right = features(points, partner_points)
     vectors = joined(targets, partner_targets)
     tiles, near = near_tiles(neighbours, left, right, vectors)
-    box, picked = route(turn(message, "gy"))
+    box, picked, lists = route(turn(message, "gy"))
     message = boxes(turn(box, "gx"), maps, picked)
-    first, moment, dots = middle(
+    first, message, moment, dots = middle(
         cell_coupling, cell_transfer, lifts, targets, near, turn(message, "gy")
     )
 
     partner_first = exchange(first, "gy", 1)
-    received = gathered(moment)
-    near = near_again(neighbours, joined(first, partner_first), tiles)
-    box, local, sums = tally(
-        cell_lists, received, cells, cell_coupling, moment, dots, first, near
-    )
-    sums = turn(sums, "gy")
-    second, extra = last(cell_transfer, maps, local, lifts, first, near, turn(box, "gx"))
-    return finish(turn(spread(sums, extra), "gx"), targets, first, second)
+    box, picked = route(turn(message, "gy"), lists)
+    picked = turn(picked, "gy")
+    near, box = near_again(neighbours, joined(first, partner_first), tiles, box)
+    local, chunk, sums = tally(
+        cell_coupling, maps, moment, dots, first, near, picked, turn(box, "gx")
+    )
+    message = turn(spread(turn(sums, "gx"), chunk), "gy")
+    return finish(cell_transfer, lifts, local, near, targets, first, message)
 
 
 def solution(mesh):

time: 193 us -> 177 us (0.917)
  blocking collectives: 55.3 us -> 70.8 us
  between operations: 14.3 us -> 0.88 us
  waiting for transfers between devices: 20.9 us -> 12 us
  starting transfers between devices: 46.9 us -> 41.2 us
  local copies, waits for them, and re-layouts: 8.02 us -> 5.77 us
    all_to_all x2 -> x4, blocking collectives: 22.1 us -> 70.8 us  [turn(): return lax.all_to_all(block, axis, 0, 0, tiled=True)]
    all_gather x1 -> x0, blocking collectives: 33.2 us -> none  [gathered(): return lax.all_gather(block, 'gy', axis=0, tiled=True)]
    all_to_all x4, waiting for transfers between devices: 20.2 us -> 12 us  [turn(): return lax.all_to_all(block, axis, 0, 0, tiled=True)]
    all_to_all x4, starting transfers between devices: 33.5 us -> 27.9 us  [turn(): return lax.all_to_all(block, axis, 0, 0, tiled=True)]
    unnamed x30 -> x24, local copies, waits for them, and re-layouts: 8.02 us -> 5.77 us
  transfers between devices with their start and end apart: 8 -> 7, of which waited for: 3 -> 3; matrix products, arithmetic and copies ran while one was open for 0% -> 0% of each run, Pallas kernels for 22% -> 21%
where the time goes in v2:
time: 177 us
  blocking collectives  70.8 us (40%)
  Pallas kernels  46 us (26%)
  starting transfers between devices  41.2 us (23%)
  waiting for transfers between devices  12 us (7%)
  local copies, waits for them, and re-layouts  5.77 us (3%)
    all_to_all x4, blocking collectives, turn(): return lax.all_to_all(block, axis, 0, 0, tiled=True)  70.8 us
    all_to_all x4, starting transfers between devices, turn(): return lax.all_to_all(block, axis, 0, 0, tiled=True)  27.9 us
    pallas_call x1, Pallas kernels, near_tiles(): pl.pallas_call(tiles_body, grid=(OWN,), out_shape=(tile, shape(ROWS, OWN...  17.7 us
    ppermute x3, starting transfers between devices, exchange(): return lax.ppermute(block, axis, [(i, i ^ mask) for i in range(count)])  13.3 us
    all_to_all x4, waiting for transfers between devices, turn(): return lax.all_to_all(block, axis, 0, 0, tiled=True)  12 us
    pallas_call x1, Pallas kernels, near_again(): pl.pallas_call(again_body, grid=(OWN, 2), out_shape=(shape(ROWS, OWN * LE...  11.9 us
    unnamed x24, local copies, waits for them, and re-layouts  5.77 us
    pallas_call x1, Pallas kernels, up(): pl.pallas_call(up_body, out_shape=(shape(RANK, OWN * LEAF), shape(GROUP,...  4.56 us
  transfers between devices with their start and end apart: 7, of which 3 were waited for; matrix products, arithmetic and copies ran while one was open for 0% of the time, Pallas kernels for 21%

profile of v2, /device:TPU:1, one launch (start us, length us, event | category | flops | bytes accessed | tf_op | source)
XLA Modules:
  0.0 176.6 jit_solution(14152539666415191524)
XLA Ops:
  0.7 4.6 %up.1 = (f32[64,2048]{1,0:T(8,128)}, f32[32,1,384]{2,1,0:T(1,128)}, f32[64,2048]{1,0:T(8,128)}, f32[3,2048]{1,0:T(4,128)}) custom-call(f32[4,64,512]{2,1,0:T(8,128)} %basis.1, f32[4,64,64]{2,1,0:T(8,128)} %leaf_transfer.1, f32[1,64,64]{2,1,0:T(8,128)} %cell_transfer.5, s32[1,4]{1,0:T(1,128)} %lists.1, f32[64,2048]{1,0:T(8,128)} %vector.1, f32[3,2048]{1,0:T(4,128)} %points.1), custom_call_target="tpu_custom_call" | custom-call | flops 60000000 | bytes 2000000 | tf_op jit(solution)/shard_map/up/pallas_call | solution.py:118
  5.3 8.9 %collective-permute-start.1 = (f32[64,2048]{1,0:T(8,128)}, f32[64,2048]{1,0:T(8,128)S(1)}, u32[]{:S(2)}, u32[]{:S(2)}) collective-permute-start(f32[64,2048]{1,0:T(8,128)} %get-tuple-element.25.own.vector), channel_id=1, source_target_pairs={{0,1},{1,0},{2,3},{3,2},{4,5},{5,4},{6,7},{7,6},{8,9},{9,8},{10,11... | collective-permute-start | bytes 1572872 | tf_op jit(solution)/shard_map/ppermute | solution.py:565
  14.2 10.0 %all-to-all-start = ((f32[32,1,384]{2,1,0:T(1,128)}), f32[32,1,384]{2,1,0:T(1,128)S(1)}, u32[]{:S(2)}, u32[]{:S(2)}) async-start(f32[32,1,384]{2,1,0:T(1,128)} %get-tuple-element.30), calls=%async_computation | async-start | bytes 98304 | tf_op jit(solution)/shard_map/all_to_all | solution.py:569
  24.2 2.1 %collective-permute-start = (f32[3,2048]{1,0:T(4,128)}, f32[3,2048]{1,0:T(4,128)S(1)}, u32[]{:S(2)}, u32[]{:S(2)}) collective-permute-start(f32[3,2048]{1,0:T(4,128)} %get-tuple-element.26.own), channel_id=1, source_target_pairs={{0,1},{1,0},{2,3},{3,2},{4,5},{5,4},{6,7},{7,6},{8,9},{9,8},{10,11... | collective-permute-start | bytes 73736 | tf_op jit(solution)/shard_map/ppermute | solution.py:565
  26.3 10.4 %all-to-all-done.received = f32[32,1,384]{2,1,0:T(1,128)S(1)} async-done(((f32[32,1,384]{2,1,0:T(1,128)}), f32[32,1,384]{2,1,0:T(1,128)S(1)}, u32[]{:S(2)}, u32[]{:S(2)}) %all-to-all-start) | async-done | bytes 49184 | tf_op jit(solution)/shard_map/all_to_all | solution.py:569
  36.7 0.9 route.2
  37.6 6.8 %all-to-all-start.1 = ((f32[16,1,128]{2,1,0:T(1,128)}), f32[16,1,128]{2,1,0:T(1,128)S(1)}, u32[]{:S(2)}, u32[]{:S(2)}) async-start(f32[16,1,128]{2,1,0:T(1,128)} %get-tuple-element.31), calls=%async_computation.1 | async-start | bytes 16384 | tf_op jit(solution)/shard_map/all_to_all | solution.py:569
  44.4 3.3 %coarse.1.maps = f32[1152,128]{1,0:T(8,128)} custom-call(f32[16,64,64]{2,1,0:T(8,128)} %parent_ref.1, f32[16,3,64,64]{3,2,1,0:T(8,128)} %box_ref.1, f32[8,4,64,64]{3,2,1,0:T(8,128)} %top_ref.1), custom_call_target="tpu_custom_call" | custom-call | flops 50000000 | bytes 2000000 | tf_op jit(solution)/shard_map/coarse/pallas_call | solution.py:168
  47.7 0.7 copy-done.7
  48.5 0.5 features.1
  49.0 1.0 copy-done.10
  50.0 0.7 all-to-all-done.1.received
  50.6 1.1 copy-done
  51.7 1.0 boxes.1
  52.7 6.5 %all-to-all-start.2 = ((f32[32,1,640]{2,1,0:T(1,128)}), f32[32,1,640]{2,1,0:T(1,128)S(1)}, u32[]{:S(2)}, u32[]{:S(2)}) async-start(f32[32,1,640]{2,1,0:T(1,128)} %boxes.1), calls=%async_computation.2 | async-start | bytes 163840 | tf_op jit(solution)/shard_map/all_to_all | solution.py:569
  59.3 1.0 copy-done.2
  60.5 0.7 copy-done.8
  61.1 1.2 copy-done.11
  62.4 17.7 %near_tiles.1 = (bf16[4,6,2,512,512]{4,3,2,1,0:T(8,128)(2,1)}, f32[64,2048]{1,0:T(8,128)S(1)}) custom-call(s32[4,6]{1,0:T(4,128)S(1)} %copy-done.8, bf16[8,512,32]{2,1,0:T(8,128)(2,1)S(1)} %copy-done.11, bf16[4,32,512]{2,1,0:T(8,128)(2,1)S(1)} %get-tuple-element.28.right, bf16[8,128,512]{2,1,0:T(8,128)(2,1)S(1)} %joined.2.vectors), custom_call_target="tpu_custom_call" | custom-call | flops 8000000000 | bytes 30000000 | tf_op jit(solution)/shard_map/near_tiles/pallas_call | solution.py:421
  80.1 2.2 %middle.1 = (f32[64,2048]{1,0:T(8,128)S(1)}, f32[32,1,256]{2,1,0:T(1,128)S(1)}, f32[64,64]{1,0:T(8,128)S(1)}, f32[64,128]{1,0:T(8,128)S(1)}) custom-call(f32[1,4,64,64]{3,2,1,0:T(8,128)S(1)} %copy-done.5, f32[1,64,64]{2,1,0:T(8,128)S(1)} %copy-done.6, f32[64,2048]{1,0:T(8,128)S(1)} %copy-done.4, f32[64,2048]{1,0:T(8,128)S(1)} %copy-done.3, ...), custom_call_target="tpu_custom_call" | custom-call | flops 80000000 | bytes 3000000 | tf_op jit(solution)/shard_map/middle/pallas_call | solution.py:513
  82.3 2.3 %collective-permute-start.2 = (f32[64,2048]{1,0:T(8,128)S(1)}, f32[64,2048]{1,0:T(8,128)S(1)}, u32[]{:S(2)}, u32[]{:S(2)}) collective-permute-start(f32[64,2048]{1,0:T(8,128)S(1)} %get-tuple-element.35.own.image.first), channel_id=1, source_target_pairs={{0,1},{1,0},{2,3},{3,2},{4,5},{5,4},{6,7},{7,6},{8,9},{9,8},{10,11... | collective-permute-start | bytes 1572872 | tf_op jit(solution)/shard_map/ppermute | solution.py:565
  84.5 24.0 %all_to_all.40.received = f32[32,1,256]{2,1,0:T(1,128)S(1)} all-to-all(f32[32,1,256]{2,1,0:T(1,128)S(1)} %get-tuple-element.37), channel_id=1, replica_groups=mesh['gx'=16,'gy'=32] {'gy'}, dimensions={0} | all-to-all | bytes 65536 | tf_op jit(solution)/shard_map/all_to_all | solution.py:569
  108.5 0.9 route.3
  109.5 4.6 %all-to-all-start.4 = ((f32[32,1,512]{2,1,0:T(1,128)}), f32[32,1,512]{2,1,0:T(1,128)S(1)}, u32[]{:S(2)}, u32[]{:S(2)}) async-start(f32[32,1,512]{2,1,0:T(1,128)} %get-tuple-element.41), calls=%async_computation.4 | async-start | bytes 131072 | tf_op jit(solution)/shard_map/all_to_all | solution.py:569
  114.1 0.1 joined.3.vectors
  114.3 11.9 %near_again.1 = (f32[64,2048]{1,0:T(8,128)S(1)}, f32[16,1,128]{2,1,0:T(1,128)S(1)}) custom-call(s32[4,6]{1,0:T(4,128)S(1)} %copy-done.9, bf16[8,128,512]{2,1,0:T(8,128)(2,1)S(1)} %joined.3.vectors, bf16[4,6,2,512,512]{4,3,2,1,0:T(8,128)(2,1)} %get-tuple-element.36.high_tiles.low_tiles, bf16[4,6,2,512,512]{4,3,2,1,0:T(8,128)(2,1)} %get-tuple-element.36.high_tiles.low_tiles, ...), custom_call_target="tpu_custom_call" | custom-call | flops 6000000000 | bytes 30000000 | tf_op jit(solution)/shard_map/near_again/pallas_call | solution.py:458
  126.2 1.0 all-to-all-done.4.picked
  127.2 11.2 %all_to_all.41.received = f32[16,1,128]{2,1,0:T(1,128)S(1)} all-to-all(f32[16,1,128]{2,1,0:T(1,128)S(1)} %get-tuple-element.42), channel_id=1, replica_groups=mesh['gx'=16,'gy'=32] {'gx'}, dimensions={0} | all-to-all | bytes 16384 | tf_op jit(solution)/shard_map/all_to_all | solution.py:569
  138.3 0.9 tally.1
  139.2 9.1 %all_to_all.42.received = f32[16,2,128]{2,1,0:T(2,128)S(1)} all-to-all(f32[16,2,128]{2,1,0:T(2,128)S(1)} %get-tuple-element.44), channel_id=1, replica_groups=mesh['gx'=16,'gy'=32] {'gx'}, dimensions={0} | all-to-all | bytes 32768 | tf_op jit(solution)/shard_map/all_to_all | solution.py:569
  148.4 26.4 %all_to_all.43.received = f32[32,1,384]{2,1,0:T(1,128)S(1)} all-to-all(f32[32,1,384]{2,1,0:T(1,128)S(1)} %spread.1), channel_id=1, replica_groups=mesh['gx'=16,'gy'=32] {'gy'}, dimensions={0} | all-to-all | bytes 98304 | tf_op jit(solution)/shard_map/all_to_all | solution.py:569
  174.9 1.7 finish.1
  (24 shorter events, 0.2 us)
Async XLA Ops:
  0.6 79.4 %copy-start.6 = (f32[1,64,64]{2,1,0:T(8,128)S(1)}, f32[1,64,64]{2,1,0:T(8,128)}, u32[]{:S(2)}) copy-start(f32[1,64,64]{2,1,0:T(8,128)} %cell_transfer.5) | copy-start | bytes 49156
  0.6 113.6 %copy-start.9 = (s32[4,6]{1,0:T(4,128)S(1)}, s32[4,6]{1,0:T(4,128)}, u32[]{:S(2)}) copy-start(s32[4,6]{1,0:T(4,128)} %neighbours.3) | copy-start | bytes 292
  0.7 79.4 %copy-start.5 = (f32[1,4,64,64]{3,2,1,0:T(8,128)S(1)}, f32[1,4,64,64]{3,2,1,0:T(8,128)}, u32[]{:S(2)}) copy-start(f32[1,4,64,64]{3,2,1,0:T(8,128)} %couplings.3) | copy-start | bytes 196612
  5.2 74.8 %copy-start.3 = (f32[64,2048]{1,0:T(8,128)S(1)}, f32[64,2048]{1,0:T(8,128)}, u32[]{:S(2)}) copy-start(f32[64,2048]{1,0:T(8,128)} %get-tuple-element.25.own.vector) | copy-start | bytes 1572868
  5.2 74.8 %copy-start.4 = (f32[64,2048]{1,0:T(8,128)S(1)}, f32[64,2048]{1,0:T(8,128)}, u32[]{:S(2)}) copy-start(f32[64,2048]{1,0:T(8,128)} %get-tuple-element.24.lifts) | copy-start | bytes 1572868
  5.3 54.0 %collective-permute-start.1 = (f32[64,2048]{1,0:T(8,128)}, f32[64,2048]{1,0:T(8,128)S(1)}, u32[]{:S(2)}, u32[]{:S(2)}) collective-permute-start(f32[64,2048]{1,0:T(8,128)} %get-tuple-element.25.own.vector), channel_id=1, source_target_pairs={{0,1},{1,0},{2,3},{3,2},{4,5},{5,4},{6,7},{7,6},{8,9},{9,8},{10,11... | collective-permute-start | bytes 1572872 | tf_op jit(solution)/shard_map/ppermute | solution.py:565
  14.2 22.5 %all-to-all-start = ((f32[32,1,384]{2,1,0:T(1,128)}), f32[32,1,384]{2,1,0:T(1,128)S(1)}, u32[]{:S(2)}, u32[]{:S(2)}) async-start(f32[32,1,384]{2,1,0:T(1,128)} %get-tuple-element.30), calls=%async_computation | async-start | bytes 98304 | tf_op jit(solution)/shard_map/all_to_all | solution.py:569
  24.2 23.5 %collective-permute-start = (f32[3,2048]{1,0:T(4,128)}, f32[3,2048]{1,0:T(4,128)S(1)}, u32[]{:S(2)}, u32[]{:S(2)}) collective-permute-start(f32[3,2048]{1,0:T(4,128)} %get-tuple-element.26.own), channel_id=1, source_target_pairs={{0,1},{1,0},{2,3},{3,2},{4,5},{5,4},{6,7},{7,6},{8,9},{9,8},{10,11... | collective-permute-start | bytes 73736 | tf_op jit(solution)/shard_map/ppermute | solution.py:565
  37.6 13.0 %all-to-all-start.1 = ((f32[16,1,128]{2,1,0:T(1,128)}), f32[16,1,128]{2,1,0:T(1,128)S(1)}, u32[]{:S(2)}, u32[]{:S(2)}) async-start(f32[16,1,128]{2,1,0:T(1,128)} %get-tuple-element.31), calls=%async_computation.1 | async-start | bytes 16384 | tf_op jit(solution)/shard_map/all_to_all | solution.py:569
  47.7 0.8 copy-start.7
  49.0 1.0 copy-start.10
  50.6 1.1 copy-start
  52.7 27.3 %all-to-all-start.2 = ((f32[32,1,640]{2,1,0:T(1,128)}), f32[32,1,640]{2,1,0:T(1,128)S(1)}, u32[]{:S(2)}, u32[]{:S(2)}) async-start(f32[32,1,640]{2,1,0:T(1,128)} %boxes.1), calls=%async_computation.2 | async-start | bytes 163840 | tf_op jit(solution)/shard_map/all_to_all | solution.py:569
  59.3 1.0 copy-start.2
  60.5 0.7 copy-start.8
  61.1 1.2 copy-start.11
  82.3 31.8 %collective-permute-start.2 = (f32[64,2048]{1,0:T(8,128)S(1)}, f32[64,2048]{1,0:T(8,128)S(1)}, u32[]{:S(2)}, u32[]{:S(2)}) collective-permute-start(f32[64,2048]{1,0:T(8,128)S(1)} %get-tuple-element.35.own.image.first), channel_id=1, source_target_pairs={{0,1},{1,0},{2,3},{3,2},{4,5},{5,4},{6,7},{7,6},{8,9},{9,8},{10,11... | collective-permute-start | bytes 1572872 | tf_op jit(solution)/shard_map/ppermute | solution.py:565
  109.5 17.7 %all-to-all-start.4 = ((f32[32,1,512]{2,1,0:T(1,128)}), f32[32,1,512]{2,1,0:T(1,128)S(1)}, u32[]{:S(2)}, u32[]{:S(2)}) async-start(f32[32,1,512]{2,1,0:T(1,128)} %get-tuple-element.41), calls=%async_computation.4 | async-start | bytes 131072 | tf_op jit(solution)/shard_map/all_to_all | solution.py:569
  114.2 24.1 %copy-start.1 = (f32[1152,128]{1,0:T(8,128)S(1)}, f32[1152,128]{1,0:T(8,128)}, u32[]{:S(2)}) copy-start(f32[1152,128]{1,0:T(8,128)} %coarse.1.maps) | copy-start | bytes 1769476

commit v3 on v2

--- a/solution.py
+++ b/solution.py
@@ -182,39 +182,37 @@
     )(parent, box_coupling, top_coupling)
 
 
-def route_body(with_lists, received, lists, *outs):
-    box, picked = outs[0], outs[1]
+def route_body(with_lists, received, *refs):
     chunk = jnp.sum(received[:, 0, 128:256], axis=0, keepdims=True)
+    cells = received[:, 0, 0:128]
+    if with_lists:
+        box, picked, lists = refs[-3:]
+        numbers = received[:, 0, 256:384]
+        lists[...] = numbers
+    else:
+        box, picked = refs[-2:]
+        numbers = refs[0][...]
     box[...] = jnp.broadcast_to(chunk[None], box.shape)
-    cells = received[:, 0, 0:128]
-    numbers = received[:, 0, 256:384] if with_lists else lists[...]
     member = lax.broadcasted_iota(jnp.int32, (GROUP, GROUP), 1).astype(jnp.float32)
     for s in range(LIST):
         chooser = (numbers[:, s : s + 1] == member).astype(jnp.float32)
         picked[:, 0, s * 128 : (s + 1) * 128] = mm(chooser, cells)
-    if with_lists:
-        outs[2][...] = numbers
-
-
-def route(received, lists=None):
-    first = lists is None
-    outs = (shape(16, 1, 128), shape(GROUP, 1, LIST * 128))
-    if first:
-        body = lambda received, *outs: route_body(True, received, None, *outs)
+
+
+def route(received, lists, after):
+    outs = (shape(16 if lists is None else 1, 1, 128), shape(GROUP, 1, LIST * 128))
+    operands = (received,) + (() if lists is None else (lists,))
+    if lists is None:
         outs = outs + (shape(GROUP, 128),)
-        operands = (received,)
-    else:
-        body = functools.partial(route_body, False)
-        operands = (received, lists)
-    return pl.pallas_call(
-        body,
+    return pl.pallas_call(
+        functools.partial(route_body, lists is None),
         out_shape=outs,
-        in_specs=[VMEM] * len(operands),
+        in_specs=[VMEM] * len(operands) + [ANY] * len(after),
         out_specs=[VMEM] * len(outs),
-        compiler_params=params(),
+        compiler_params=params(8),
         cost_estimate=cost(4_000_000, 200_000),
         name="route",
-    )(*operands)
+    )(*operands, *after)
 
 
 def boxes_body(received, maps, picked, message):
@@ -251,7 +249,22 @@
 
 
 def tally_body(
-    couplings, maps, moment, dots, image, near, picked, received, local, chunk, sums
+    couplings,
+    maps,
+    moment,
+    dots,
+    image,
+    near0,
+    near1,
+    picked,
+    own,
+    one,
+    two,
+    four,
+    eight,
+    local,
+    chunk,
+    sums,
 ):
     expansion = jnp.zeros((ROWS, RANK), jnp.float32)
     for k in range(LIST):
@@ -262,11 +275,13 @@
     cubic = square + jnp.sum(moment[...] * expansion, axis=1, keepdims=True)
     for a in range(OWN):
         part = slice(a * LEAF, (a + 1) * LEAF)
-        cubic = cubic + jnp.sum(image[:, part] * near[:, part], axis=1, keepdims=True)
+        near = near_of(near0, near1, a)
+        cubic = cubic + jnp.sum(image[:, part] * near, axis=1, keepdims=True)
     rows = sum_rows(((0, dots[:, 0:1]), (1, dots[:, 1:2]), (2, square), (3, cubic)))
-    row = box_local(maps, received)
+    others = [ref[k] for ref in (one, two, four, eight) for k in range(ref.shape[0])]
+    row = mm(jnp.concatenate(others, axis=1), maps[...])
     chunk[...] = row
-    product = row * received[lax.axis_index("gx")]
+    product = row * own[0]
     place = lax.broadcasted_iota(jnp.int32, (2, 128), 0) * 128
     place = place + lax.broadcasted_iota(jnp.int32, (2, 128), 1)
     column = 128 + RANK + lax.axis_index("gy")
@@ -276,16 +291,16 @@
     sums[...] = jnp.broadcast_to(rows[None], sums.shape)
 
 
-def tally(couplings, maps, moment, dots, image, near, picked, received):
+def tally(couplings, maps, moment, dots, image, near0, near1, picked, boxes):
     return pl.pallas_call(
         tally_body,
         out_shape=(shape(ROWS, RANK), shape(1, 128), shape(16, 2, 128)),
-        in_specs=[VMEM] * 8,
+        in_specs=[VMEM] * 13,
         out_specs=[VMEM] * 3,
         compiler_params=params(),
         cost_estimate=cost(4_000_000, 2_500_000),
         name="tally",
-    )(couplings, maps, moment, dots, image, near, picked, received)
+    )(couplings, maps, moment, dots, image, near0, near1, picked, *boxes)
 
 
 def spread_body(received, chunk, message):
@@ -382,8 +397,9 @@
     return jnp.bitwise_xor(neighbours[leaf, n] & (2 * OWN - 1), OWN * parity)
 
 
-def tiles_body(neighbours, left, right, vectors, tiles, out, square):
-    leaf = pl.program_id(0)
+def tiles_body(first_leaf, neighbours, left, right, vectors, *refs):
+    tiles, out, square = refs[-3:]
+    leaf = pl.program_id(0) + first_leaf
     target = right[leaf]
     rows = [neighbour_row(neighbours, leaf, n) for n in range(SLOTS)]
     wide = jnp.zeros((2 * ROWS, LEAF), jnp.float32)
@@ -415,25 +431,26 @@
     out[...] = NEAR_WEIGHT * (wide[:ROWS] + wide[ROWS:] + narrow)
 
 
-def near_tiles(neighbours, left, right, vectors):
-    tile = shape(OWN, SLOTS, 2, LEAF, LEAF, dtype=jnp.bfloat16)
+def near_tiles(leaves, neighbours, left, right, vectors, after=()):
+    tile = shape(len(leaves), SLOTS, 2, LEAF, LEAF, dtype=jnp.bfloat16)
     block = pl.BlockSpec((1, SLOTS, 2, LEAF, LEAF), lambda a: (a, 0, 0, 0, 0))
     return pl.pallas_call(
-        tiles_body,
-        grid=(OWN,),
-        out_shape=(tile, shape(ROWS, OWN * LEAF)),
-        in_specs=[SMEM] + [VMEM] * 3,
+        functools.partial(tiles_body, leaves[0]),
+        grid=(len(leaves),),
+        out_shape=(tile, shape(ROWS, len(leaves) * LEAF)),
+        in_specs=[SMEM] + [VMEM] * 3 + [ANY] * len(after),
         out_specs=[block, pl.BlockSpec((ROWS, LEAF), lambda a: (0, a))],
         scratch_shapes=[pltpu.VMEM((2, LEAF, LEAF), jnp.float32)],
         compiler_params=params(40),
-        cost_estimate=cost(8_000_000_000, 30_000_000, 12_000_000),
+        cost_estimate=cost(
+            2_000_000_000 * len(leaves), 7_000_000 * len(leaves), 3_000_000 * len(leaves)
+        ),
         name="near_tiles",
-    )(neighbours, left, right, vectors)
-
-
-def again_body(neighbours, vectors, high_tiles, low_tiles, box, out, box_out):
-    box_out[...] = box[...]
-    leaf = pl.program_id(0)
+    )(neighbours, left, right, vectors, *after)
+
+
+def again_body(first_leaf, neighbours, vectors, high_tiles, low_tiles, out):
+    leaf = pl.program_id(0) + first_leaf
     wide = jnp.zeros((2 * ROWS, LEAF), jnp.float32)
     narrow = jnp.zeros((ROWS, LEAF), jnp.float32)
     for n in range(SLOTS // 2):
@@ -451,28 +468,24 @@
         out[...] += value
 
 
-def near_again(neighbours, vectors, tiles, box):
+def near_again(leaves, neighbours, vectors, tiles):
     half = (1, SLOTS // 2, 1, LEAF, LEAF)
     high = pl.BlockSpec(half, lambda a, h: (a, h, 0, 0, 0))
     low = pl.BlockSpec(half, lambda a, h: (a, h, 1, 0, 0))
     return pl.pallas_call(
-        again_body,
-        grid=(OWN, 2),
-        out_shape=(shape(ROWS, OWN * LEAF), shape(*box.shape)),
-        in_specs=[SMEM, VMEM, high, low, VMEM],
-        out_specs=[pl.BlockSpec((ROWS, LEAF), lambda a, h: (0, a)), VMEM],
+        functools.partial(again_body, leaves[0]),
+        grid=(len(leaves), 2),
+        out_shape=shape(ROWS, len(leaves) * LEAF),
+        in_specs=[SMEM, VMEM, high, low],
+        out_specs=pl.BlockSpec((ROWS, LEAF), lambda a, h: (0, a)),
         compiler_params=params(40),
-        cost_estimate=cost(6_000_000_000, 30_000_000),
+        cost_estimate=cost(1_500_000_000 * len(leaves), 7_000_000 * len(leaves)),
         name="near_again",
-    )(neighbours, vectors, tiles, tiles, box)
-
-
-def box_local(maps, boxes):
-    g = lax.axis_index("gx")
-    row = jnp.concatenate(
-        [boxes[jnp.bitwise_xor(g, m)] for m in range(1, BOX_SPAN + 1)], axis=1
-    )
-    return mm(row, maps[...])
+    )(neighbours, vectors, tiles, tiles)
+
+
+def near_of(near0, near1, a):
+    return near0[...] if a == 0 else near1[:, (a - 1) * LEAF : a * LEAF]
 
 
 def cell_local(couplings, cell_transfer, received):
@@ -486,7 +499,7 @@
 
 
 def middle_body(
-    couplings, cell_transfer, lifts, vector, near, received, image, message, moment, dots
+    couplings, cell_transfer, lifts, vector, near0, near1, received, image, message, moment, dots
 ):
     local = cell_local(couplings, cell_transfer, received)
     total = jnp.zeros((ROWS, RANK), jnp.float32)
@@ -495,7 +508,7 @@
         part = slice(a * LEAF, (a + 1) * LEAF)
         lift = lifts[:, part]
         value = vector[:, part]
-        result = value + near[:, part] + mm(local, lift)
+        result = value + near_of(near0, near1, a) + mm(local, lift)
         image[:, part] = result
         total = total + mm(result, lift, NT)
         for k, product in enumerate((value * value, value * result, result * result)):
@@ -509,19 +522,21 @@
     dots[...] = table
 
 
-def middle(couplings, cell_transfer, lifts, vector, near, received):
+def middle(couplings, cell_transfer, lifts, vector, near0, near1, received):
     return pl.pallas_call(
         middle_body,
         out_shape=(shape(ROWS, OWN * LEAF), shape(GROUP, 1, 256), shape(ROWS, RANK), shape(ROWS, 128)),
-        in_specs=[VMEM] * 6,
+        in_specs=[VMEM] * 7,
         out_specs=[VMEM] * 4,
         compiler_params=params(),
         cost_estimate=cost(80_000_000, 3_000_000),
         name="middle",
-    )(couplings, cell_transfer, lifts, vector, near, received)
-
-
-def finish_body(cell_transfer, lifts, local, near, vector, first, received, iterate, residual):
+    )(couplings, cell_transfer, lifts, vector, near0, near1, received)
+
+
+def finish_body(
+    cell_transfer, lifts, local, near0, near1, vector, first, received, iterate, residual
+):
     expansion = local[...] + mm(
         unpacked_rows(received[:, 0, 256:384]), cell_transfer[0], NT
     )
@@ -543,21 +558,22 @@
         part = slice(a * LEAF, (a + 1) * LEAF)
         start = vector[:, part]
         image = first[:, part]
-        second = image + near[:, part] + mm(expansion, lifts[:, part])
+        near = near_of(near0, near1, a)
+        second = image + near + mm(expansion, lifts[:, part])
         iterate[:, part] = both * start - cross * image
         residual[:, part] = start - both * image + cross * second
 
 
-def finish(cell_transfer, lifts, local, near, vector, first, received):
+def finish(cell_transfer, lifts, local, near0, near1, vector, first, received):
     return pl.pallas_call(
         finish_body,
         out_shape=(shape(ROWS, OWN * LEAF), shape(ROWS, OWN * LEAF)),
-        in_specs=[VMEM] * 7,
+        in_specs=[VMEM] * 8,
         out_specs=[VMEM] * 2,
         compiler_params=params(),
         cost_estimate=cost(20_000_000, 3_000_000),
         name="finish",
-    )(cell_transfer, lifts, local, near, vector, first, received)
+    )(cell_transfer, lifts, local, near0, near1, vector, first, received)
 
 
 def exchange(block, axis, mask):
@@ -590,22 +606,38 @@
     maps = coarse(box_parent_transfer, box_coupling, top_coupling)
     left, right = features(points, partner_points)
     vectors = joined(targets, partner_targets)
-    tiles, near = near_tiles(neighbours, left, right, vectors)
-    box, picked, lists = route(turn(message, "gy"))
+    tiles0, near0 = near_tiles((0,), neighbours, left, right, vectors)
+    box, picked, lists = route(turn(message, "gy"), None, (near0,))
     message = boxes(turn(box, "gx"), maps, picked)
+    tiles1, near1 = near_tiles((1, 2, 3), neighbours, left, right, vectors, (message,))
     first, message, moment, dots = middle(
-        cell_coupling, cell_transfer, lifts, targets, near, turn(message, "gy")
+        cell_coupling, cell_transfer, lifts, targets, near0, near1, turn(message, "gy")
     )
 
     partner_first = exchange(first, "gy", 1)
-    box, picked = route(turn(message, "gy"), lists)
+    vectors = joined(first, partner_first)
+    near1 = near_again((1, 2, 3), neighbours, vectors, tiles1)
+    box, picked = route(turn(message, "gy"), lists, (near1,))
     picked = turn(picked, "gy")
-    near, box = near_again(neighbours, joined(first, partner_first), tiles, box)
+    near0 = near_again((0,), neighbours, vectors, tiles0)
+    one = exchange(box, "gx", 1)
+    pair = jnp.concatenate([box, one], axis=0)
+    two = exchange(pair, "gx", 2)
+    eight = exchange(pair, "gx", 8)
+    four = exchange(jnp.concatenate([pair, two], axis=0), "gx", 4)
     local, chunk, sums = tally(
-        cell_coupling, maps, moment, dots, first, near, picked, turn(box, "gx")
+        cell_coupling,
+        maps,
+        moment,
+        dots,
+        first,
+        near0,
+        near1,
+        picked,
+        (box, one, two, four, eight),
     )
     message = turn(spread(turn(sums, "gx"), chunk), "gy")
-    return finish(cell_transfer, lifts, local, near, targets, first, message)
+    return finish(cell_transfer, lifts, local, near0, near1, targets, first, message)
 
 
 def solution(mesh):

time: 177 us -> 180 us (1.017)
  starting transfers between devices: 41.2 us -> 74.6 us
  blocking collectives: 70.8 us -> 38.1 us
  local copies, waits for them, and re-layouts: 5.77 us -> 11.7 us
  waiting for transfers between devices: 12 us -> 7.82 us
    all_to_all x4 -> x2, blocking collectives: 70.8 us -> 38.1 us  [turn(): return lax.all_to_all(block, axis, 0, 0, tiled=True)]
    all_to_all x4 -> x5, starting transfers between devices: 27.9 us -> 50.5 us  [turn(): return lax.all_to_all(block, axis, 0, 0, tiled=True)]
    ppermute x3 -> x7, starting transfers between devices: 13.3 us -> 24.2 us  [exchange(): return lax.ppermute(block, axis, [(i, i ^ mask) for i in range(count)])]
    unnamed x24 -> x31, local copies, waits for them, and re-layouts: 5.77 us -> 11.7 us
    all_to_all x4 -> x5, waiting for transfers between devices: 12 us -> 7.8 us  [turn(): return lax.all_to_all(block, axis, 0, 0, tiled=True)]
    pallas_call x4 -> x6, Pallas kernels: 31.4 us -> 31.2 us  [the longest x2 18.2 us: near_tiles(): pl.pallas_call(functools.partial(tiles_body, leaves[0]), grid=(len(leaves...]
  transfers between devices with their start and end apart: 7 -> 12, of which waited for: 3 -> 3; matrix products, arithmetic and copies ran while one was open for 0% -> 0% of each run, Pallas kernels for 21% -> 19%
where the time goes in v3:
time: 180 us; the launch traced here: 179 us
  starting transfers between devices  74.6 us (41%)
  Pallas kernels  46.1 us (26%)
  blocking collectives  38.1 us (21%)
  local copies, waits for them, and re-layouts  11.7 us (6%)
  waiting for transfers between devices  7.82 us (4%)
    all_to_all x5, starting transfers between devices, turn(): return lax.all_to_all(block, axis, 0, 0, tiled=True)  50.5 us
    all_to_all x2, blocking collectives, turn(): return lax.all_to_all(block, axis, 0, 0, tiled=True)  38.1 us
    ppermute x7, starting transfers between devices, exchange(): return lax.ppermute(block, axis, [(i, i ^ mask) for i in range(count)])  24.2 us
    pallas_call x2, Pallas kernels, near_tiles(): pl.pallas_call(functools.partial(tiles_body, leaves[0]), grid=(len(leaves...  18.2 us
    unnamed x31, local copies, waits for them, and re-layouts  11.7 us
    pallas_call x2, Pallas kernels, near_again(): pl.pallas_call(functools.partial(again_body, leaves[0]), grid=(len(leaves...  11.2 us
    all_to_all x5, waiting for transfers between devices, turn(): return lax.all_to_all(block, axis, 0, 0, tiled=True)  7.8 us
    pallas_call x1, Pallas kernels, up(): pl.pallas_call(up_body, out_shape=(shape(RANK, OWN * LEAF), shape(GROUP,...  4.43 us
  transfers between devices with their start and end apart: 12, of which 3 were waited for; matrix products, arithmetic and copies ran while one was open for 0% of the time, Pallas kernels for 19%

profile of v3, /device:TPU:1, one launch (start us, length us, event | category | flops | bytes accessed | tf_op | source)
XLA Modules:
  0.0 179.4 jit_solution(8366293442854465287)
XLA Ops:
  0.6 4.4 %up.1 = (f32[64,2048]{1,0:T(8,128)}, f32[32,1,384]{2,1,0:T(1,128)}, f32[64,2048]{1,0:T(8,128)}, f32[3,2048]{1,0:T(4,128)}) custom-call(f32[4,64,512]{2,1,0:T(8,128)} %basis.1, f32[4,64,64]{2,1,0:T(8,128)} %leaf_transfer.1, f32[1,64,64]{2,1,0:T(8,128)} %cell_transfer.5, s32[1,4]{1,0:T(1,128)} %lists.1, f32[64,2048]{1,0:T(8,128)} %vector.1, f32[3,2048]{1,0:T(4,128)} %points.1), custom_call_target="tpu_custom_call" | custom-call | flops 60000000 | bytes 2000000 | tf_op jit(solution)/shard_map/up/pallas_call | solution.py:118
  5.1 8.8 %collective-permute-start.1 = (f32[64,2048]{1,0:T(8,128)}, f32[64,2048]{1,0:T(8,128)S(1)}, u32[]{:S(2)}, u32[]{:S(2)}) collective-permute-start(f32[64,2048]{1,0:T(8,128)} %get-tuple-element.25.own.vector), channel_id=1, source_target_pairs={{0,1},{1,0},{2,3},{3,2},{4,5},{5,4},{6,7},{7,6},{8,9},{9,8},{10,11... | collective-permute-start | bytes 1572872 | tf_op jit(solution)/shard_map/ppermute | solution.py:581
  13.9 1.9 %collective-permute-start = (f32[3,2048]{1,0:T(4,128)}, f32[3,2048]{1,0:T(4,128)S(1)}, u32[]{:S(2)}, u32[]{:S(2)}) collective-permute-start(f32[3,2048]{1,0:T(4,128)} %get-tuple-element.26.own), channel_id=1, source_target_pairs={{0,1},{1,0},{2,3},{3,2},{4,5},{5,4},{6,7},{7,6},{8,9},{9,8},{10,11... | collective-permute-start | bytes 73736 | tf_op jit(solution)/shard_map/ppermute | solution.py:581
  15.8 10.4 %all-to-all-start = ((f32[32,1,384]{2,1,0:T(1,128)}), f32[32,1,384]{2,1,0:T(1,128)S(1)}, u32[]{:S(2)}, u32[]{:S(2)}) async-start(f32[32,1,384]{2,1,0:T(1,128)} %get-tuple-element.30), calls=%async_computation | async-start | bytes 98304 | tf_op jit(solution)/shard_map/all_to_all | solution.py:585
  27.5 1.4 copy-done.4
  29.8 4.3 %near_tiles.2 = (bf16[1,6,2,512,512]{4,3,2,1,0:T(8,128)(2,1)S(1)}, f32[64,512]{1,0:T(8,128)S(1)}) custom-call(s32[4,6]{1,0:T(4,128)S(1)} %copy-done.11, bf16[8,512,32]{2,1,0:T(8,128)(2,1)S(1)} %get-tuple-element.27.left, bf16[4,32,512]{2,1,0:T(8,128)(2,1)S(1)} %get-tuple-element.28.right, bf16[8,128,512]{2,1,0:T(8,128)(2,1)S(1)} %joined.2.vectors), custom_call_target="tpu_custom_call" | custom-call | flops 2000000000 | bytes 7000000 | tf_op jit(solution)/shard_map/near_tiles/pallas_call | solution.py:437
  34.1 2.6 %copy-done = bf16[1,6,2,512,512]{4,3,2,1,0:T(8,128)(2,1)} copy-done((bf16[1,6,2,512,512]{4,3,2,1,0:T(8,128)(2,1)}, bf16[1,6,2,512,512]{4,3,2,1,0:T(8,128)(2,1)S(1)}, u32[]{:S(2)}) %copy-start) | copy-done | bytes 6291480
  36.7 2.0 %all-to-all-done.received = f32[32,1,384]{2,1,0:T(1,128)S(1)} async-done(((f32[32,1,384]{2,1,0:T(1,128)}), f32[32,1,384]{2,1,0:T(1,128)S(1)}, u32[]{:S(2)}, u32[]{:S(2)}) %all-to-all-start) | async-done | bytes 49184 | tf_op jit(solution)/shard_map/all_to_all | solution.py:585
  39.6 6.8 %all-to-all-start.1 = ((f32[16,1,128]{2,1,0:T(1,128)}), f32[16,1,128]{2,1,0:T(1,128)S(1)}, u32[]{:S(2)}, u32[]{:S(2)}) async-start(f32[16,1,128]{2,1,0:T(1,128)} %get-tuple-element.31), calls=%async_computation.1 | async-start | bytes 16384 | tf_op jit(solution)/shard_map/all_to_all | solution.py:585
  46.4 3.3 %coarse.1.maps = f32[1152,128]{1,0:T(8,128)} custom-call(f32[16,64,64]{2,1,0:T(8,128)} %parent_ref.1, f32[16,3,64,64]{3,2,1,0:T(8,128)} %box_ref.1, f32[8,4,64,64]{3,2,1,0:T(8,128)} %top_ref.1), custom_call_target="tpu_custom_call" | custom-call | flops 50000000 | bytes 2000000 | tf_op jit(solution)/shard_map/coarse/pallas_call | solution.py:168
  49.7 3.0 %all-to-all-done.1.received = f32[16,1,128]{2,1,0:T(1,128)S(1)} async-done(((f32[16,1,128]{2,1,0:T(1,128)}), f32[16,1,128]{2,1,0:T(1,128)S(1)}, u32[]{:S(2)}, u32[]{:S(2)}) %all-to-all-start.1) | async-done | bytes 8224 | tf_op jit(solution)/shard_map/all_to_all | solution.py:585
  52.6 1.1 copy-done.2
  53.7 1.0 boxes.1.refs_0_
  54.7 11.8 %all-to-all-start.2 = ((f32[32,1,640]{2,1,0:T(1,128)}), f32[32,1,640]{2,1,0:T(1,128)S(1)}, u32[]{:S(2)}, u32[]{:S(2)}) async-start(f32[32,1,640]{2,1,0:T(1,128)} %boxes.1.refs_0_), calls=%async_computation.2 | async-start | bytes 163840 | tf_op jit(solution)/shard_map/all_to_all | solution.py:585
  66.5 1.2 copy-done.14
  67.8 13.9 %near_tiles.3 = (bf16[3,6,2,512,512]{4,3,2,1,0:T(8,128)(2,1)}, f32[64,1536]{1,0:T(8,128)S(1)}) custom-call(s32[4,6]{1,0:T(4,128)S(1)} %copy-done.12, bf16[8,512,32]{2,1,0:T(8,128)(2,1)S(1)} %copy-done.14, bf16[4,32,512]{2,1,0:T(8,128)(2,1)S(1)} %get-tuple-element.28.right, bf16[8,128,512]{2,1,0:T(8,128)(2,1)S(1)} %joined.2.vectors, f32[32,1,640]{2,1,0:T(1,128)} %boxes.1.refs_0_), custom_call_target="tpu_custom_call" | custom-call | flops 6000000000 | bytes 21000000 | tf_op jit(solution)/shard_map/near_tiles/pallas_call | solution.py:437
  81.7 2.8 %middle.1 = (f32[64,2048]{1,0:T(8,128)S(1)}, f32[32,1,256]{2,1,0:T(1,128)}, f32[64,64]{1,0:T(8,128)S(1)}, f32[64,128]{1,0:T(8,128)S(1)}) custom-call(f32[1,4,64,64]{3,2,1,0:T(8,128)S(1)} %copy-done.8, f32[1,64,64]{2,1,0:T(8,128)S(1)} %copy-done.9, f32[64,2048]{1,0:T(8,128)S(1)} %copy-done.6, f32[64,2048]{1,0:T(8,128)S(1)} %copy-done.5, ...), custom_call_target="tpu_custom_call" | custom-call | flops 80000000 | bytes 3000000 | tf_op jit(solution)/shard_map/middle/pallas_call | solution.py:526
  84.5 2.3 %collective-permute-start.2 = (f32[64,2048]{1,0:T(8,128)S(1)}, f32[64,2048]{1,0:T(8,128)S(1)}, u32[]{:S(2)}, u32[]{:S(2)}) collective-permute-start(f32[64,2048]{1,0:T(8,128)S(1)} %get-tuple-element.36.own.image.first), channel_id=1, source_target_pairs={{0,1},{1,0},{2,3},{3,2},{4,5},{5,4},{6,7},{7,6},{8,9},{9,8},{10,11... | collective-permute-start | bytes 1572872 | tf_op jit(solution)/shard_map/ppermute | solution.py:581
  86.8 11.9 %all-to-all-start.3 = ((f32[32,1,256]{2,1,0:T(1,128)}), f32[32,1,256]{2,1,0:T(1,128)S(1)}, u32[]{:S(2)}, u32[]{:S(2)}) async-start(f32[32,1,256]{2,1,0:T(1,128)} %get-tuple-element.39), calls=%async_computation.3 | async-start | bytes 65536 | tf_op jit(solution)/shard_map/all_to_all | solution.py:585
  98.9 9.1 %near_again.3.refs_1_.near1 = f32[64,1536]{1,0:T(8,128)S(1)} custom-call(s32[4,6]{1,0:T(4,128)S(1)} %copy-done.12, bf16[8,128,512]{2,1,0:T(8,128)(2,1)S(1)} %joined.3.vectors, bf16[3,6,2,512,512]{4,3,2,1,0:T(8,128)(2,1)} %get-tuple-element.38.high_tiles.low_tiles, bf16[3,6,2,512,512]{4,3,2,1,0:T(8,128)(2,1)} %get-tuple-element.38.high_tiles.low_tiles), custom_call_target="tpu_custom_call" | custom-call | flops 4499999744 | bytes 21000000 | tf_op jit(solution)/shard_map/near_again/pallas_call | solution.py:475
  108.0 2.9 %all-to-all-done.3.received = f32[32,1,256]{2,1,0:T(1,128)S(1)} async-done(((f32[32,1,256]{2,1,0:T(1,128)}), f32[32,1,256]{2,1,0:T(1,128)S(1)}, u32[]{:S(2)}, u32[]{:S(2)}) %all-to-all-start.3) | async-done | bytes 32800 | tf_op jit(solution)/shard_map/all_to_all | solution.py:585
  111.8 2.0 %collective-permute-start.3 = (f32[1,1,128]{2,1,0:T(1,128)S(1)}, f32[1,1,128]{2,1,0:T(1,128)S(1)}, u32[]{:S(2)}, u32[]{:S(2)}) collective-permute-start(f32[1,1,128]{2,1,0:T(1,128)S(1)} %get-tuple-element.42.own), channel_id=1, source_target_pairs={{0,32},{32,0},{64,96},{96,64},{128,160},{160,128},{192,224},{224,1... | collective-permute-start | bytes 1544 | tf_op jit(solution)/shard_map/ppermute | solution.py:581
  113.8 9.6 %all-to-all-start.4 = ((f32[32,1,512]{2,1,0:T(1,128)}), f32[32,1,512]{2,1,0:T(1,128)S(1)}, u32[]{:S(2)}, u32[]{:S(2)}) async-start(f32[32,1,512]{2,1,0:T(1,128)} %get-tuple-element.41), calls=%async_computation.4 | async-start | bytes 131072 | tf_op jit(solution)/shard_map/all_to_all | solution.py:585
  123.5 3.9 %collective-permute-start.4 = (f32[2,1,128]{2,1,0:T(1,128)S(1)}, f32[2,1,128]{2,1,0:T(1,128)S(1)}, u32[]{:S(2)}, u32[]{:S(2)}) collective-permute-start(f32[2,1,128]{2,1,0:T(1,128)S(1)} %constant_dynamic-update-slice_fusion), channel_id=1, source_target_pairs={{0,64},{32,96},{64,0},{96,32},{128,192},{160,224},{192,128},{224,1... | collective-permute-start | bytes 3080 | tf_op jit(solution)/shard_map/ppermute | solution.py:581
  127.4 2.8 %collective-permute-start.6 = (f32[2,1,128]{2,1,0:T(1,128)S(1)}, f32[2,1,128]{2,1,0:T(1,128)S(1)}, u32[]{:S(2)}, u32[]{:S(2)}) collective-permute-start(f32[2,1,128]{2,1,0:T(1,128)S(1)} %constant_dynamic-update-slice_fusion), channel_id=1, source_target_pairs={{0,256},{32,288},{64,320},{96,352},{128,384},{160,416},{192,448},{... | collective-permute-start | bytes 3080 | tf_op jit(solution)/shard_map/ppermute | solution.py:581
  130.2 2.5 %collective-permute-start.5 = (f32[4,1,128]{2,1,0:T(1,128)S(1)}, f32[4,1,128]{2,1,0:T(1,128)S(1)}, u32[]{:S(2)}, u32[]{:S(2)}) collective-permute-start(f32[4,1,128]{2,1,0:T(1,128)S(1)} %pad_maximum_fusion), channel_id=1, source_target_pairs={{0,128},{32,160},{64,192},{96,224},{128,0},{160,32},{192,64},{224,... | collective-permute-start | bytes 6152 | tf_op jit(solution)/shard_map/ppermute | solution.py:581
  132.7 2.8 %copy-done.1 = bf16[1,6,2,512,512]{4,3,2,1,0:T(8,128)(2,1)S(1)} copy-done((bf16[1,6,2,512,512]{4,3,2,1,0:T(8,128)(2,1)S(1)}, bf16[1,6,2,512,512]{4,3,2,1,0:T(8,128)(2,1)}, u32[]{:S(2)}) %copy-start.1) | copy-done | bytes 6291480
  135.5 2.1 %near_again.2.near0 = f32[64,512]{1,0:T(8,128)S(1)} custom-call(s32[4,6]{1,0:T(4,128)S(1)} %copy-done.12, bf16[8,128,512]{2,1,0:T(8,128)(2,1)S(1)} %joined.3.vectors, bf16[1,6,2,512,512]{4,3,2,1,0:T(8,128)(2,1)S(1)} %copy-done.1, bf16[1,6,2,512,512]{4,3,2,1,0:T(8,128)(2,1)S(1)} %copy-done.1), custom_call_target="tpu_custom_call" | custom-call | flops 1500000000 | bytes 7000000 | tf_op jit(solution)/shard_map/near_again/pallas_call | solution.py:475
  138.5 11.4 %all_to_all.35.received = f32[16,2,128]{2,1,0:T(2,128)S(1)} all-to-all(f32[16,2,128]{2,1,0:T(2,128)S(1)} %get-tuple-element.44), channel_id=1, replica_groups=mesh['gx'=16,'gy'=32] {'gx'}, dimensions={0} | all-to-all | bytes 32768 | tf_op jit(solution)/shard_map/all_to_all | solution.py:585
  149.9 26.7 %all_to_all.36.received = f32[32,1,384]{2,1,0:T(1,128)S(1)} all-to-all(f32[32,1,384]{2,1,0:T(1,128)S(1)} %spread.1), channel_id=1, replica_groups=mesh['gx'=16,'gy'=32] {'gy'}, dimensions={0} | all-to-all | bytes 98304 | tf_op jit(solution)/shard_map/all_to_all | solution.py:585
  176.6 1.0 copy-done.7
  177.7 1.7 finish.1
  (43 shorter events, 5.1 us)
Async XLA Ops:
  5.1 22.4 %collective-permute-start.1 = (f32[64,2048]{1,0:T(8,128)}, f32[64,2048]{1,0:T(8,128)S(1)}, u32[]{:S(2)}, u32[]{:S(2)}) collective-permute-start(f32[64,2048]{1,0:T(8,128)} %get-tuple-element.25.own.vector), channel_id=1, source_target_pairs={{0,1},{1,0},{2,3},{3,2},{4,5},{5,4},{6,7},{7,6},{8,9},{9,8},{10,11... | collective-permute-start | bytes 1572872 | tf_op jit(solution)/shard_map/ppermute | solution.py:581
  13.9 12.3 %collective-permute-start = (f32[3,2048]{1,0:T(4,128)}, f32[3,2048]{1,0:T(4,128)S(1)}, u32[]{:S(2)}, u32[]{:S(2)}) collective-permute-start(f32[3,2048]{1,0:T(4,128)} %get-tuple-element.26.own), channel_id=1, source_target_pairs={{0,1},{1,0},{2,3},{3,2},{4,5},{5,4},{6,7},{7,6},{8,9},{9,8},{10,11... | collective-permute-start | bytes 73736 | tf_op jit(solution)/shard_map/ppermute | solution.py:581
  15.8 22.9 %all-to-all-start = ((f32[32,1,384]{2,1,0:T(1,128)}), f32[32,1,384]{2,1,0:T(1,128)S(1)}, u32[]{:S(2)}, u32[]{:S(2)}) async-start(f32[32,1,384]{2,1,0:T(1,128)} %get-tuple-element.30), calls=%async_computation | async-start | bytes 98304 | tf_op jit(solution)/shard_map/all_to_all | solution.py:585
  26.2 0.8 copy-start.10
  27.5 1.6 copy-start.13
  27.5 1.4 copy-start.4
  29.0 37.5 %copy-start.12 = (s32[4,6]{1,0:T(4,128)S(1)}, s32[4,6]{1,0:T(4,128)}, u32[]{:S(2)}) copy-start(s32[4,6]{1,0:T(4,128)} %neighbours.7) | copy-start | bytes 292
  29.0 0.7 copy-start.11
  34.1 2.7 %copy-start = (bf16[1,6,2,512,512]{4,3,2,1,0:T(8,128)(2,1)}, bf16[1,6,2,512,512]{4,3,2,1,0:T(8,128)(2,1)S(1)}, u32[]{:S(2)}) copy-start(bf16[1,6,2,512,512]{4,3,2,1,0:T(8,128)(2,1)S(1)} %get-tuple-element.37.high_tiles.low_tiles) | copy-start | bytes 18874372
  39.6 13.0 %all-to-all-start.1 = ((f32[16,1,128]{2,1,0:T(1,128)}), f32[16,1,128]{2,1,0:T(1,128)S(1)}, u32[]{:S(2)}, u32[]{:S(2)}) async-start(f32[16,1,128]{2,1,0:T(1,128)} %get-tuple-element.31), calls=%async_computation.1 | async-start | bytes 16384 | tf_op jit(solution)/shard_map/all_to_all | solution.py:585
  52.6 1.1 copy-start.2
  54.7 26.9 %all-to-all-start.2 = ((f32[32,1,640]{2,1,0:T(1,128)}), f32[32,1,640]{2,1,0:T(1,128)S(1)}, u32[]{:S(2)}, u32[]{:S(2)}) async-start(f32[32,1,640]{2,1,0:T(1,128)} %boxes.1.refs_0_), calls=%async_computation.2 | async-start | bytes 163840 | tf_op jit(solution)/shard_map/all_to_all | solution.py:585
  66.5 1.2 copy-start.14
  67.8 13.9 %copy-start.5 = (f32[64,2048]{1,0:T(8,128)S(1)}, f32[64,2048]{1,0:T(8,128)}, u32[]{:S(2)}) copy-start(f32[64,2048]{1,0:T(8,128)} %get-tuple-element.25.own.vector) | copy-start | bytes 1572868
  67.8 13.9 %copy-start.6 = (f32[64,2048]{1,0:T(8,128)S(1)}, f32[64,2048]{1,0:T(8,128)}, u32[]{:S(2)}) copy-start(f32[64,2048]{1,0:T(8,128)} %get-tuple-element.24.lifts) | copy-start | bytes 1572868
  67.8 13.9 %copy-start.8 = (f32[1,4,64,64]{3,2,1,0:T(8,128)S(1)}, f32[1,4,64,64]{3,2,1,0:T(8,128)}, u32[]{:S(2)}) copy-start(f32[1,4,64,64]{3,2,1,0:T(8,128)} %couplings.3) | copy-start | bytes 196612
  67.8 13.9 %copy-start.9 = (f32[1,64,64]{2,1,0:T(8,128)S(1)}, f32[1,64,64]{2,1,0:T(8,128)}, u32[]{:S(2)}) copy-start(f32[1,64,64]{2,1,0:T(8,128)} %cell_transfer.5) | copy-start | bytes 49156
  84.5 14.3 %collective-permute-start.2 = (f32[64,2048]{1,0:T(8,128)S(1)}, f32[64,2048]{1,0:T(8,128)S(1)}, u32[]{:S(2)}, u32[]{:S(2)}) collective-permute-start(f32[64,2048]{1,0:T(8,128)S(1)} %get-tuple-element.36.own.image.first), channel_id=1, source_target_pairs={{0,1},{1,0},{2,3},{3,2},{4,5},{5,4},{6,7},{7,6},{8,9},{9,8},{10,11... | collective-permute-start | bytes 1572872 | tf_op jit(solution)/shard_map/ppermute | solution.py:581
  86.8 24.1 %all-to-all-start.3 = ((f32[32,1,256]{2,1,0:T(1,128)}), f32[32,1,256]{2,1,0:T(1,128)S(1)}, u32[]{:S(2)}, u32[]{:S(2)}) async-start(f32[32,1,256]{2,1,0:T(1,128)} %get-tuple-element.39), calls=%async_computation.3 | async-start | bytes 65536 | tf_op jit(solution)/shard_map/all_to_all | solution.py:585
  111.8 11.7 %collective-permute-start.3 = (f32[1,1,128]{2,1,0:T(1,128)S(1)}, f32[1,1,128]{2,1,0:T(1,128)S(1)}, u32[]{:S(2)}, u32[]{:S(2)}) collective-permute-start(f32[1,1,128]{2,1,0:T(1,128)S(1)} %get-tuple-element.42.own), channel_id=1, source_target_pairs={{0,32},{32,0},{64,96},{96,64},{128,160},{160,128},{192,224},{224,1... | collective-permute-start | bytes 1544 | tf_op jit(solution)/shard_map/ppermute | solution.py:581
  113.8 23.7 %all-to-all-start.4 = ((f32[32,1,512]{2,1,0:T(1,128)}), f32[32,1,512]{2,1,0:T(1,128)S(1)}, u32[]{:S(2)}, u32[]{:S(2)}) async-start(f32[32,1,512]{2,1,0:T(1,128)} %get-tuple-element.41), calls=%async_computation.4 | async-start | bytes 131072 | tf_op jit(solution)/shard_map/all_to_all | solution.py:585
  123.5 6.7 %collective-permute-start.4 = (f32[2,1,128]{2,1,0:T(1,128)S(1)}, f32[2,1,128]{2,1,0:T(1,128)S(1)}, u32[]{:S(2)}, u32[]{:S(2)}) collective-permute-start(f32[2,1,128]{2,1,0:T(1,128)S(1)} %constant_dynamic-update-slice_fusion), channel_id=1, source_target_pairs={{0,64},{32,96},{64,0},{96,32},{128,192},{160,224},{192,128},{224,1... | collective-permute-start | bytes 3080 | tf_op jit(solution)/shard_map/ppermute | solution.py:581
  127.4 10.2 %collective-permute-start.6 = (f32[2,1,128]{2,1,0:T(1,128)S(1)}, f32[2,1,128]{2,1,0:T(1,128)S(1)}, u32[]{:S(2)}, u32[]{:S(2)}) collective-permute-start(f32[2,1,128]{2,1,0:T(1,128)S(1)} %constant_dynamic-update-slice_fusion), channel_id=1, source_target_pairs={{0,256},{32,288},{64,320},{96,352},{128,384},{160,416},{192,448},{... | collective-permute-start | bytes 3080 | tf_op jit(solution)/shard_map/ppermute | solution.py:581
  130.2 7.4 %collective-permute-start.5 = (f32[4,1,128]{2,1,0:T(1,128)S(1)}, f32[4,1,128]{2,1,0:T(1,128)S(1)}, u32[]{:S(2)}, u32[]{:S(2)}) collective-permute-start(f32[4,1,128]{2,1,0:T(1,128)S(1)} %pad_maximum_fusion), channel_id=1, source_target_pairs={{0,128},{32,160},{64,192},{96,224},{128,0},{160,32},{192,64},{224,... | collective-permute-start | bytes 6152 | tf_op jit(solution)/shard_map/ppermute | solution.py:581
  132.7 2.8 %copy-start.1 = (bf16[1,6,2,512,512]{4,3,2,1,0:T(8,128)(2,1)S(1)}, bf16[1,6,2,512,512]{4,3,2,1,0:T(8,128)(2,1)}, u32[]{:S(2)}) copy-start(bf16[1,6,2,512,512]{4,3,2,1,0:T(8,128)(2,1)} %copy-done) | copy-start | bytes 18874372
  135.5 2.1 %copy-start.3 = (f32[1152,128]{1,0:T(8,128)S(1)}, f32[1152,128]{1,0:T(8,128)}, u32[]{:S(2)}) copy-start(f32[1152,128]{1,0:T(8,128)} %coarse.1.maps) | copy-start | bytes 1769476
  176.6 1.0 copy-start.7

commit v4 on v3

--- a/solution.py
+++ b/solution.py
@@ -254,8 +254,7 @@
     moment,
     dots,
     image,
-    near0,
-    near1,
+    near,
     picked,
     own,
     one,
@@ -275,8 +274,7 @@
     cubic = square + jnp.sum(moment[...] * expansion, axis=1, keepdims=True)
     for a in range(OWN):
         part = slice(a * LEAF, (a + 1) * LEAF)
-        near = near_of(near0, near1, a)
-        cubic = cubic + jnp.sum(image[:, part] * near, axis=1, keepdims=True)
+        cubic = cubic + jnp.sum(image[:, part] * near[:, part], axis=1, keepdims=True)
     rows = sum_rows(((0, dots[:, 0:1]), (1, dots[:, 1:2]), (2, square), (3, cubic)))
     others = [ref[k] for ref in (one, two, four, eight) for k in range(ref.shape[0])]
     row = mm(jnp.concatenate(others, axis=1), maps[...])
@@ -291,16 +289,16 @@
     sums[...] = jnp.broadcast_to(rows[None], sums.shape)
 
 
-def tally(couplings, maps, moment, dots, image, near0, near1, picked, boxes):
+def tally(couplings, maps, moment, dots, image, near, picked, boxes):
     return pl.pallas_call(
         tally_body,
         out_shape=(shape(ROWS, RANK), shape(1, 128), shape(16, 2, 128)),
-        in_specs=[VMEM] * 13,
+        in_specs=[VMEM] * 12,
         out_specs=[VMEM] * 3,
         compiler_params=params(),
         cost_estimate=cost(4_000_000, 2_500_000),
         name="tally",
-    )(couplings, maps, moment, dots, image, near0, near1, picked, *boxes)
+    )(couplings, maps, moment, dots, image, near, picked, *boxes)
 
 
 def spread_body(received, chunk, message):
@@ -484,10 +482,6 @@
     )(neighbours, vectors, tiles, tiles)
 
 
-def near_of(near0, near1, a):
-    return near0[...] if a == 0 else near1[:, (a - 1) * LEAF : a * LEAF]
-
-
 def cell_local(couplings, cell_transfer, received):
     local = mm(unpacked_rows(received[:, 0, 0:128]), cell_transfer[0], NT)
     for s in range(LIST):
@@ -499,7 +493,7 @@
 
 
 def middle_body(
-    couplings, cell_transfer, lifts, vector, near0, near1, received, image, message, moment, dots
+    couplings, cell_transfer, lifts, vector, near, received, image, message, moment, dots
 ):
     local = cell_local(couplings, cell_transfer, received)
     total = jnp.zeros((ROWS, RANK), jnp.float32)
@@ -508,7 +502,7 @@
         part = slice(a * LEAF, (a + 1) * LEAF)
         lift = lifts[:, part]
         value = vector[:, part]
-        result = value + near_of(near0, near1, a) + mm(local, lift)
+        result = value + near[:, part] + mm(local, lift)
         image[:, part] = result
         total = total + mm(result, lift, NT)
         for k, product in enumerate((value * value, value * result, result * result)):
@@ -522,20 +516,20 @@
     dots[...] = table
 
 
-def middle(couplings, cell_transfer, lifts, vector, near0, near1, received):
+def middle(couplings, cell_transfer, lifts, vector, near, received):
     return pl.pallas_call(
         middle_body,
         out_shape=(shape(ROWS, OWN * LEAF), shape(GROUP, 1, 256), shape(ROWS, RANK), shape(ROWS, 128)),
-        in_specs=[VMEM] * 7,
+        in_specs=[VMEM] * 6,
         out_specs=[VMEM] * 4,
         compiler_params=params(),
         cost_estimate=cost(80_000_000, 3_000_000),
         name="middle",
-    )(couplings, cell_transfer, lifts, vector, near0, near1, received)
+    )(couplings, cell_transfer, lifts, vector, near, received)
 
 
 def finish_body(
-    cell_transfer, lifts, local, near0, near1, vector, first, received, iterate, residual
+    cell_transfer, lifts, local, near, vector, first, received, iterate, residual
 ):
     expansion = local[...] + mm(
         unpacked_rows(received[:, 0, 256:384]), cell_transfer[0], NT
@@ -558,22 +552,21 @@
         part = slice(a * LEAF, (a + 1) * LEAF)
         start = vector[:, part]
         image = first[:, part]
-        near = near_of(near0, near1, a)
-        second = image + near + mm(expansion, lifts[:, part])
+        second = image + near[:, part] + mm(expansion, lifts[:, part])
         iterate[:, part] = both * start - cross * image
         residual[:, part] = start - both * image + cross * second
 
 
-def finish(cell_transfer, lifts, local, near0, near1, vector, first, received):
+def finish(cell_transfer, lifts, local, near, vector, first, received):
     return pl.pallas_call(
         finish_body,
         out_shape=(shape(ROWS, OWN * LEAF), shape(ROWS, OWN * LEAF)),
-        in_specs=[VMEM] * 8,
+        in_specs=[VMEM] * 7,
         out_specs=[VMEM] * 2,
         compiler_params=params(),
         cost_estimate=cost(20_000_000, 3_000_000),
         name="finish",
-    )(cell_transfer, lifts, local, near0, near1, vector, first, received)
+    )(cell_transfer, lifts, local, near, vector, first, received)
 
 
 def exchange(block, axis, mask):
@@ -606,20 +599,17 @@
     maps = coarse(box_parent_transfer, box_coupling, top_coupling)
     left, right = features(points, partner_points)
     vectors = joined(targets, partner_targets)
-    tiles0, near0 = near_tiles((0,), neighbours, left, right, vectors)
-    box, picked, lists = route(turn(message, "gy"), None, (near0,))
+    tiles, near = near_tiles(range(OWN), neighbours, left, right, vectors)
+    box, picked, lists = route(turn(message, "gy"), None, ())
     message = boxes(turn(box, "gx"), maps, picked)
-    tiles1, near1 = near_tiles((1, 2, 3), neighbours, left, right, vectors, (message,))
     first, message, moment, dots = middle(
-        cell_coupling, cell_transfer, lifts, targets, near0, near1, turn(message, "gy")
+        cell_coupling, cell_transfer, lifts, targets, near, turn(message, "gy")
     )
 
     partner_first = exchange(first, "gy", 1)
-    vectors = joined(first, partner_first)
-    near1 = near_again((1, 2, 3), neighbours, vectors, tiles1)
-    box, picked = route(turn(message, "gy"), lists, (near1,))
+    near = near_again(range(OWN), neighbours, joined(first, partner_first), tiles)
+    box, picked = route(turn(message, "gy"), lists, (near,))
     picked = turn(picked, "gy")
-    near0 = near_again((0,), neighbours, vectors, tiles0)
     one = exchange(box, "gx", 1)
     pair = jnp.concatenate([box, one], axis=0)
     two = exchange(pair, "gx", 2)
@@ -631,13 +621,12 @@
         moment,
         dots,
         first,
-        near0,
-        near1,
+        near,
         picked,
         (box, one, two, four, eight),
     )
     message = turn(spread(turn(sums, "gx"), chunk), "gy")
-    return finish(cell_transfer, lifts, local, near0, near1, targets, first, message)
+    return finish(cell_transfer, lifts, local, near, targets, first, message)
 
 
 def solution(mesh):

time: 180 us -> 183 us (1.017)
  waiting for transfers between devices: 7.82 us -> 14.9 us
  local copies, waits for them, and re-layouts: 11.7 us -> 5.77 us
  blocking collectives: 38.1 us -> 40.3 us
    unnamed x31 -> x25, local copies, waits for them, and re-layouts: 11.7 us -> 5.76 us
    ppermute x7, waiting for transfers between devices: 0.02 us -> 3.78 us  [exchange(): return lax.ppermute(block, axis, [(i, i ^ mask) for i in range(count)])]
    all_to_all x5, waiting for transfers between devices: 7.8 us -> 11.1 us  [turn(): return lax.all_to_all(block, axis, 0, 0, tiled=True)]
    all_to_all x5, starting transfers between devices: 50.5 us -> 47.8 us  [turn(): return lax.all_to_all(block, axis, 0, 0, tiled=True)]
    all_to_all x2, blocking collectives: 38.1 us -> 40.3 us  [turn(): return lax.all_to_all(block, axis, 0, 0, tiled=True)]
    ppermute x7, starting transfers between devices: 24.2 us -> 26.1 us  [exchange(): return lax.ppermute(block, axis, [(i, i ^ mask) for i in range(count)])]
    pallas_call x2 -> x1, Pallas kernels: 11.2 us -> 11.9 us  [near_again(): pl.pallas_call(functools.partial(again_body, leaves[0]), grid=(len(leaves...]
    pallas_call x2 -> x1, Pallas kernels: 18.2 us -> 17.6 us  [near_tiles(): pl.pallas_call(functools.partial(tiles_body, leaves[0]), grid=(len(leaves...]
  transfers between devices with their start and end apart: 12 -> 12, of which waited for: 3 -> 4; matrix products, arithmetic and copies ran while one was open for 0% -> 0% of each run, Pallas kernels for 19% -> 19%
where the time goes in v4:
time: 183 us; the launch traced here: 182 us
  starting transfers between devices  73.9 us (40%)
  Pallas kernels  46.4 us (25%)
  blocking collectives  40.3 us (22%)
  waiting for transfers between devices  14.9 us (8%)
  local copies, waits for them, and re-layouts  5.77 us (3%)
    all_to_all x5, starting transfers between devices, turn(): return lax.all_to_all(block, axis, 0, 0, tiled=True)  47.8 us
    all_to_all x2, blocking collectives, turn(): return lax.all_to_all(block, axis, 0, 0, tiled=True)  40.3 us
    ppermute x7, starting transfers between devices, exchange(): return lax.ppermute(block, axis, [(i, i ^ mask) for i in range(count)])  26.1 us
    pallas_call x1, Pallas kernels, near_tiles(): pl.pallas_call(functools.partial(tiles_body, leaves[0]), grid=(len(leaves...  17.6 us
    pallas_call x1, Pallas kernels, near_again(): pl.pallas_call(functools.partial(again_body, leaves[0]), grid=(len(leaves...  11.9 us
    all_to_all x5, waiting for transfers between devices, turn(): return lax.all_to_all(block, axis, 0, 0, tiled=True)  11.1 us
    unnamed x25, local copies, waits for them, and re-layouts  5.76 us
    pallas_call x1, Pallas kernels, up(): pl.pallas_call(up_body, out_shape=(shape(RANK, OWN * LEAF), shape(GROUP,...  4.56 us
  transfers between devices with their start and end apart: 12, of which 4 were waited for; matrix products, arithmetic and copies ran while one was open for 0% of the time, Pallas kernels for 19%

profile of v4, /device:TPU:1, one launch (start us, length us, event | category | flops | bytes accessed | tf_op | source)
XLA Modules:
  0.0 182.2 jit_solution(16941095377947872287)
XLA Ops:
  0.7 4.6 %up.1 = (f32[64,2048]{1,0:T(8,128)}, f32[32,1,384]{2,1,0:T(1,128)}, f32[64,2048]{1,0:T(8,128)}, f32[3,2048]{1,0:T(4,128)}) custom-call(f32[4,64,512]{2,1,0:T(8,128)} %basis.1, f32[4,64,64]{2,1,0:T(8,128)} %leaf_transfer.1, f32[1,64,64]{2,1,0:T(8,128)} %cell_transfer.5, s32[1,4]{1,0:T(1,128)} %lists.1, f32[64,2048]{1,0:T(8,128)} %vector.1, f32[3,2048]{1,0:T(4,128)} %points.1), custom_call_target="tpu_custom_call" | custom-call | flops 60000000 | bytes 2000000 | tf_op jit(solution)/shard_map/up/pallas_call | solution.py:118
  5.3 8.9 %collective-permute-start.1 = (f32[64,2048]{1,0:T(8,128)}, f32[64,2048]{1,0:T(8,128)S(1)}, u32[]{:S(2)}, u32[]{:S(2)}) collective-permute-start(f32[64,2048]{1,0:T(8,128)} %get-tuple-element.23.own.vector), channel_id=1, source_target_pairs={{0,1},{1,0},{2,3},{3,2},{4,5},{5,4},{6,7},{7,6},{8,9},{9,8},{10,11... | collective-permute-start | bytes 1572872 | tf_op jit(solution)/shard_map/ppermute | solution.py:574
  14.2 10.0 %all-to-all-start = ((f32[32,1,384]{2,1,0:T(1,128)}), f32[32,1,384]{2,1,0:T(1,128)S(1)}, u32[]{:S(2)}, u32[]{:S(2)}) async-start(f32[32,1,384]{2,1,0:T(1,128)} %get-tuple-element.28), calls=%async_computation | async-start | bytes 98304 | tf_op jit(solution)/shard_map/all_to_all | solution.py:578
  24.2 2.1 %collective-permute-start = (f32[3,2048]{1,0:T(4,128)}, f32[3,2048]{1,0:T(4,128)S(1)}, u32[]{:S(2)}, u32[]{:S(2)}) collective-permute-start(f32[3,2048]{1,0:T(4,128)} %get-tuple-element.24.own), channel_id=1, source_target_pairs={{0,1},{1,0},{2,3},{3,2},{4,5},{5,4},{6,7},{7,6},{8,9},{9,8},{10,11... | collective-permute-start | bytes 73736 | tf_op jit(solution)/shard_map/ppermute | solution.py:574
  26.3 10.4 %all-to-all-done.received = f32[32,1,384]{2,1,0:T(1,128)S(1)} async-done(((f32[32,1,384]{2,1,0:T(1,128)}), f32[32,1,384]{2,1,0:T(1,128)S(1)}, u32[]{:S(2)}, u32[]{:S(2)}) %all-to-all-start) | async-done | bytes 49184 | tf_op jit(solution)/shard_map/all_to_all | solution.py:578
  36.7 0.9 route.2
  37.6 6.8 %all-to-all-start.1 = ((f32[16,1,128]{2,1,0:T(1,128)}), f32[16,1,128]{2,1,0:T(1,128)S(1)}, u32[]{:S(2)}, u32[]{:S(2)}) async-start(f32[16,1,128]{2,1,0:T(1,128)} %get-tuple-element.29), calls=%async_computation.1 | async-start | bytes 16384 | tf_op jit(solution)/shard_map/all_to_all | solution.py:578
  44.4 3.3 %coarse.1.maps = f32[1152,128]{1,0:T(8,128)} custom-call(f32[16,64,64]{2,1,0:T(8,128)} %parent_ref.1, f32[16,3,64,64]{3,2,1,0:T(8,128)} %box_ref.1, f32[8,4,64,64]{3,2,1,0:T(8,128)} %top_ref.1), custom_call_target="tpu_custom_call" | custom-call | flops 50000000 | bytes 2000000 | tf_op jit(solution)/shard_map/coarse/pallas_call | solution.py:168
  47.7 0.7 copy-done.7
  49.0 1.0 copy-done.10
  50.6 1.1 copy-done
  51.7 1.0 boxes.1
  52.7 6.5 %all-to-all-start.2 = ((f32[32,1,640]{2,1,0:T(1,128)}), f32[32,1,640]{2,1,0:T(1,128)S(1)}, u32[]{:S(2)}, u32[]{:S(2)}) async-start(f32[32,1,640]{2,1,0:T(1,128)} %boxes.1), calls=%async_computation.2 | async-start | bytes 163840 | tf_op jit(solution)/shard_map/all_to_all | solution.py:578
  59.3 1.0 copy-done.2
  61.1 1.2 copy-done.11
  62.3 17.6 %near_tiles.1 = (bf16[4,6,2,512,512]{4,3,2,1,0:T(8,128)(2,1)}, f32[64,2048]{1,0:T(8,128)S(1)}) custom-call(s32[4,6]{1,0:T(4,128)S(1)} %copy-done.8, bf16[8,512,32]{2,1,0:T(8,128)(2,1)S(1)} %copy-done.11, bf16[4,32,512]{2,1,0:T(8,128)(2,1)S(1)} %get-tuple-element.26.right, bf16[8,128,512]{2,1,0:T(8,128)(2,1)S(1)} %joined.2.vectors), custom_call_target="tpu_custom_call" | custom-call | flops 8000000000 | bytes 28000000 | tf_op jit(solution)/shard_map/near_tiles/pallas_call | solution.py:435
  80.0 2.8 %middle.1 = (f32[64,2048]{1,0:T(8,128)S(1)}, f32[32,1,256]{2,1,0:T(1,128)}, f32[64,64]{1,0:T(8,128)S(1)}, f32[64,128]{1,0:T(8,128)S(1)}) custom-call(f32[1,4,64,64]{3,2,1,0:T(8,128)S(1)} %copy-done.5, f32[1,64,64]{2,1,0:T(8,128)S(1)} %copy-done.6, f32[64,2048]{1,0:T(8,128)S(1)} %copy-done.4, f32[64,2048]{1,0:T(8,128)S(1)} %copy-done.3, ...), custom_call_target="tpu_custom_call" | custom-call | flops 80000000 | bytes 3000000 | tf_op jit(solution)/shard_map/middle/pallas_call | solution.py:520
  82.8 2.2 %collective-permute-start.2 = (f32[64,2048]{1,0:T(8,128)S(1)}, f32[64,2048]{1,0:T(8,128)S(1)}, u32[]{:S(2)}, u32[]{:S(2)}) collective-permute-start(f32[64,2048]{1,0:T(8,128)S(1)} %get-tuple-element.33.own.image.first), channel_id=1, source_target_pairs={{0,1},{1,0},{2,3},{3,2},{4,5},{5,4},{6,7},{7,6},{8,9},{9,8},{10,11... | collective-permute-start | bytes 1572872 | tf_op jit(solution)/shard_map/ppermute | solution.py:574
  85.1 12.1 %all-to-all-start.3 = ((f32[32,1,256]{2,1,0:T(1,128)}), f32[32,1,256]{2,1,0:T(1,128)S(1)}, u32[]{:S(2)}, u32[]{:S(2)}) async-start(f32[32,1,256]{2,1,0:T(1,128)} %get-tuple-element.35), calls=%async_computation.3 | async-start | bytes 65536 | tf_op jit(solution)/shard_map/all_to_all | solution.py:578
  97.3 11.9 %near_again.1.refs_1_.near = f32[64,2048]{1,0:T(8,128)S(1)} custom-call(s32[4,6]{1,0:T(4,128)S(1)} %copy-done.9, bf16[8,128,512]{2,1,0:T(8,128)(2,1)S(1)} %joined.3.vectors, bf16[4,6,2,512,512]{4,3,2,1,0:T(8,128)(2,1)} %get-tuple-element.34.high_tiles.low_tiles, bf16[4,6,2,512,512]{4,3,2,1,0:T(8,128)(2,1)} %get-tuple-element.34.high_tiles.low_tiles), custom_call_target="tpu_custom_call" | custom-call | flops 6000000000 | bytes 28000000 | tf_op jit(solution)/shard_map/near_again/pallas_call | solution.py:473
  109.3 0.9 route.3
  110.2 2.0 %collective-permute-start.3 = (f32[1,1,128]{2,1,0:T(1,128)S(1)}, f32[1,1,128]{2,1,0:T(1,128)S(1)}, u32[]{:S(2)}, u32[]{:S(2)}) collective-permute-start(f32[1,1,128]{2,1,0:T(1,128)S(1)} %get-tuple-element.38.own), channel_id=1, source_target_pairs={{0,32},{32,0},{64,96},{96,64},{128,160},{160,128},{192,224},{224,1... | collective-permute-start | bytes 1544 | tf_op jit(solution)/shard_map/ppermute | solution.py:574
  112.2 12.4 %all-to-all-start.4 = ((f32[32,1,512]{2,1,0:T(1,128)}), f32[32,1,512]{2,1,0:T(1,128)S(1)}, u32[]{:S(2)}, u32[]{:S(2)}) async-start(f32[32,1,512]{2,1,0:T(1,128)} %get-tuple-element.37), calls=%async_computation.4 | async-start | bytes 131072 | tf_op jit(solution)/shard_map/all_to_all | solution.py:578
  124.7 3.8 %collective-permute-start.4 = (f32[2,1,128]{2,1,0:T(1,128)S(1)}, f32[2,1,128]{2,1,0:T(1,128)S(1)}, u32[]{:S(2)}, u32[]{:S(2)}) collective-permute-start(f32[2,1,128]{2,1,0:T(1,128)S(1)} %constant_dynamic-update-slice_fusion), channel_id=1, source_target_pairs={{0,64},{32,96},{64,0},{96,32},{128,192},{160,224},{192,128},{224,1... | collective-permute-start | bytes 3080 | tf_op jit(solution)/shard_map/ppermute | solution.py:574
  128.6 2.3 %collective-permute-done.4.two = f32[2,1,128]{2,1,0:T(1,128)S(1)} collective-permute-done((f32[2,1,128]{2,1,0:T(1,128)S(1)}, f32[2,1,128]{2,1,0:T(1,128)S(1)}, u32[]{:S(2)}, u32[]{:S(2)}) %collective-permute-start.4) | collective-permute-done | bytes 1056 | tf_op jit(solution)/shard_map/ppermute | solution.py:574
  130.8 2.6 %collective-permute-start.5 = (f32[4,1,128]{2,1,0:T(1,128)S(1)}, f32[4,1,128]{2,1,0:T(1,128)S(1)}, u32[]{:S(2)}, u32[]{:S(2)}) collective-permute-start(f32[4,1,128]{2,1,0:T(1,128)S(1)} %pad_maximum_fusion), channel_id=1, source_target_pairs={{0,128},{32,160},{64,192},{96,224},{128,0},{160,32},{192,64},{224,... | collective-permute-start | bytes 6152 | tf_op jit(solution)/shard_map/ppermute | solution.py:574
  133.4 4.3 %collective-permute-start.6 = (f32[2,1,128]{2,1,0:T(1,128)S(1)}, f32[2,1,128]{2,1,0:T(1,128)S(1)}, u32[]{:S(2)}, u32[]{:S(2)}) collective-permute-start(f32[2,1,128]{2,1,0:T(1,128)S(1)} %constant_dynamic-update-slice_fusion), channel_id=1, source_target_pairs={{0,256},{32,288},{64,320},{96,352},{128,384},{160,416},{192,448},{... | collective-permute-start | bytes 3080 | tf_op jit(solution)/shard_map/ppermute | solution.py:574
  137.7 1.5 collective-permute-done.6.eight
  139.3 0.9 tally.1
  140.2 12.1 %all_to_all.35.received = f32[16,2,128]{2,1,0:T(2,128)S(1)} all-to-all(f32[16,2,128]{2,1,0:T(2,128)S(1)} %get-tuple-element.40), channel_id=1, replica_groups=mesh['gx'=16,'gy'=32] {'gx'}, dimensions={0} | all-to-all | bytes 32768 | tf_op jit(solution)/shard_map/all_to_all | solution.py:578
  152.3 28.2 %all_to_all.36.received = f32[32,1,384]{2,1,0:T(1,128)S(1)} all-to-all(f32[32,1,384]{2,1,0:T(1,128)S(1)} %spread.1), channel_id=1, replica_groups=mesh['gx'=16,'gy'=32] {'gy'}, dimensions={0} | all-to-all | bytes 98304 | tf_op jit(solution)/shard_map/all_to_all | solution.py:578
  180.5 1.7 finish.1
  (35 shorter events, 2.3 us)
Async XLA Ops:
  0.6 79.3 %copy-start.6 = (f32[1,64,64]{2,1,0:T(8,128)S(1)}, f32[1,64,64]{2,1,0:T(8,128)}, u32[]{:S(2)}) copy-start(f32[1,64,64]{2,1,0:T(8,128)} %cell_transfer.5) | copy-start | bytes 49156
  0.6 96.7 %copy-start.9 = (s32[4,6]{1,0:T(4,128)S(1)}, s32[4,6]{1,0:T(4,128)}, u32[]{:S(2)}) copy-start(s32[4,6]{1,0:T(4,128)} %neighbours.3) | copy-start | bytes 292
  0.7 79.3 %copy-start.5 = (f32[1,4,64,64]{3,2,1,0:T(8,128)S(1)}, f32[1,4,64,64]{3,2,1,0:T(8,128)}, u32[]{:S(2)}) copy-start(f32[1,4,64,64]{3,2,1,0:T(8,128)} %couplings.3) | copy-start | bytes 196612
  5.2 74.7 %copy-start.3 = (f32[64,2048]{1,0:T(8,128)S(1)}, f32[64,2048]{1,0:T(8,128)}, u32[]{:S(2)}) copy-start(f32[64,2048]{1,0:T(8,128)} %get-tuple-element.23.own.vector) | copy-start | bytes 1572868
  5.2 74.7 %copy-start.4 = (f32[64,2048]{1,0:T(8,128)S(1)}, f32[64,2048]{1,0:T(8,128)}, u32[]{:S(2)}) copy-start(f32[64,2048]{1,0:T(8,128)} %get-tuple-element.22.lifts) | copy-start | bytes 1572868
  5.3 54.0 %collective-permute-start.1 = (f32[64,2048]{1,0:T(8,128)}, f32[64,2048]{1,0:T(8,128)S(1)}, u32[]{:S(2)}, u32[]{:S(2)}) collective-permute-start(f32[64,2048]{1,0:T(8,128)} %get-tuple-element.23.own.vector), channel_id=1, source_target_pairs={{0,1},{1,0},{2,3},{3,2},{4,5},{5,4},{6,7},{7,6},{8,9},{9,8},{10,11... | collective-permute-start | bytes 1572872 | tf_op jit(solution)/shard_map/ppermute | solution.py:574
  14.2 22.5 %all-to-all-start = ((f32[32,1,384]{2,1,0:T(1,128)}), f32[32,1,384]{2,1,0:T(1,128)S(1)}, u32[]{:S(2)}, u32[]{:S(2)}) async-start(f32[32,1,384]{2,1,0:T(1,128)} %get-tuple-element.28), calls=%async_computation | async-start | bytes 98304 | tf_op jit(solution)/shard_map/all_to_all | solution.py:578
  24.2 23.5 %collective-permute-start = (f32[3,2048]{1,0:T(4,128)}, f32[3,2048]{1,0:T(4,128)S(1)}, u32[]{:S(2)}, u32[]{:S(2)}) collective-permute-start(f32[3,2048]{1,0:T(4,128)} %get-tuple-element.24.own), channel_id=1, source_target_pairs={{0,1},{1,0},{2,3},{3,2},{4,5},{5,4},{6,7},{7,6},{8,9},{9,8},{10,11... | collective-permute-start | bytes 73736 | tf_op jit(solution)/shard_map/ppermute | solution.py:574
  37.6 13.0 %all-to-all-start.1 = ((f32[16,1,128]{2,1,0:T(1,128)}), f32[16,1,128]{2,1,0:T(1,128)S(1)}, u32[]{:S(2)}, u32[]{:S(2)}) async-start(f32[16,1,128]{2,1,0:T(1,128)} %get-tuple-element.29), calls=%async_computation.1 | async-start | bytes 16384 | tf_op jit(solution)/shard_map/all_to_all | solution.py:578
  47.7 0.8 copy-start.7
  49.0 1.0 copy-start.10
  50.6 1.1 copy-start
  52.7 27.2 %all-to-all-start.2 = ((f32[32,1,640]{2,1,0:T(1,128)}), f32[32,1,640]{2,1,0:T(1,128)S(1)}, u32[]{:S(2)}, u32[]{:S(2)}) async-start(f32[32,1,640]{2,1,0:T(1,128)} %boxes.1), calls=%async_computation.2 | async-start | bytes 163840 | tf_op jit(solution)/shard_map/all_to_all | solution.py:578
  59.3 1.0 copy-start.2
  60.4 0.7 copy-start.8
  61.1 1.2 copy-start.11
  82.8 14.4 %collective-permute-start.2 = (f32[64,2048]{1,0:T(8,128)S(1)}, f32[64,2048]{1,0:T(8,128)S(1)}, u32[]{:S(2)}, u32[]{:S(2)}) collective-permute-start(f32[64,2048]{1,0:T(8,128)S(1)} %get-tuple-element.33.own.image.first), channel_id=1, source_target_pairs={{0,1},{1,0},{2,3},{3,2},{4,5},{5,4},{6,7},{7,6},{8,9},{9,8},{10,11... | collective-permute-start | bytes 1572872 | tf_op jit(solution)/shard_map/ppermute | solution.py:574
  85.1 24.2 %all-to-all-start.3 = ((f32[32,1,256]{2,1,0:T(1,128)}), f32[32,1,256]{2,1,0:T(1,128)S(1)}, u32[]{:S(2)}, u32[]{:S(2)}) async-start(f32[32,1,256]{2,1,0:T(1,128)} %get-tuple-element.35), calls=%async_computation.3 | async-start | bytes 65536 | tf_op jit(solution)/shard_map/all_to_all | solution.py:578
  97.3 41.9 %copy-start.1 = (f32[1152,128]{1,0:T(8,128)S(1)}, f32[1152,128]{1,0:T(8,128)}, u32[]{:S(2)}) copy-start(f32[1152,128]{1,0:T(8,128)} %coarse.1.maps) | copy-start | bytes 1769476
  110.2 14.5 %collective-permute-start.3 = (f32[1,1,128]{2,1,0:T(1,128)S(1)}, f32[1,1,128]{2,1,0:T(1,128)S(1)}, u32[]{:S(2)}, u32[]{:S(2)}) collective-permute-start(f32[1,1,128]{2,1,0:T(1,128)S(1)} %get-tuple-element.38.own), channel_id=1, source_target_pairs={{0,32},{32,0},{64,96},{96,64},{128,160},{160,128},{192,224},{224,1... | collective-permute-start | bytes 1544 | tf_op jit(solution)/shard_map/ppermute | solution.py:574
  112.2 27.0 %all-to-all-start.4 = ((f32[32,1,512]{2,1,0:T(1,128)}), f32[32,1,512]{2,1,0:T(1,128)S(1)}, u32[]{:S(2)}, u32[]{:S(2)}) async-start(f32[32,1,512]{2,1,0:T(1,128)} %get-tuple-element.37), calls=%async_computation.4 | async-start | bytes 131072 | tf_op jit(solution)/shard_map/all_to_all | solution.py:578
  124.7 6.1 %collective-permute-start.4 = (f32[2,1,128]{2,1,0:T(1,128)S(1)}, f32[2,1,128]{2,1,0:T(1,128)S(1)}, u32[]{:S(2)}, u32[]{:S(2)}) collective-permute-start(f32[2,1,128]{2,1,0:T(1,128)S(1)} %constant_dynamic-update-slice_fusion), channel_id=1, source_target_pairs={{0,64},{32,96},{64,0},{96,32},{128,192},{160,224},{192,128},{224,1... | collective-permute-start | bytes 3080 | tf_op jit(solution)/shard_map/ppermute | solution.py:574
  130.8 8.4 %collective-permute-start.5 = (f32[4,1,128]{2,1,0:T(1,128)S(1)}, f32[4,1,128]{2,1,0:T(1,128)S(1)}, u32[]{:S(2)}, u32[]{:S(2)}) collective-permute-start(f32[4,1,128]{2,1,0:T(1,128)S(1)} %pad_maximum_fusion), channel_id=1, source_target_pairs={{0,128},{32,160},{64,192},{96,224},{128,0},{160,32},{192,64},{224,... | collective-permute-start | bytes 6152 | tf_op jit(solution)/shard_map/ppermute | solution.py:574
  133.4 5.8 %collective-permute-start.6 = (f32[2,1,128]{2,1,0:T(1,128)S(1)}, f32[2,1,128]{2,1,0:T(1,128)S(1)}, u32[]{:S(2)}, u32[]{:S(2)}) collective-permute-start(f32[2,1,128]{2,1,0:T(1,128)S(1)} %constant_dynamic-update-slice_fusion), channel_id=1, source_target_pairs={{0,256},{32,288},{64,320},{96,352},{128,384},{160,416},{192,448},{... | collective-permute-start | bytes 3080 | tf_op jit(solution)/shard_map/ppermute | solution.py:574

commit v5 on v2

--- a/solution.py
+++ b/solution.py
@@ -31,7 +31,7 @@
 TN = (((0,), (0,)), ((), ()))
 
 
-def mm(a, b, dims=NN):
+def mm_row(a, b, dims=NN):
     return lax.dot_general(a, b, dims, precision=EXACT, preferred_element_type=jnp.float32)
 
 
@@ -42,6 +42,13 @@
 def split2(value):
     high = value.astype(jnp.bfloat16)
     return high, (value - high.astype(jnp.float32)).astype(jnp.bfloat16)
+
+
+def mm(a, b, dims=NN):
+    a_high, a_low = split2(a)
+    b_high, b_low = split2(b)
+    small = mm16(a_high, b_low, dims) + mm16(a_low, b_high, dims)
+    return mm16(a_high, b_high, dims) + small
 
 
 def split3(value):
@@ -222,7 +229,7 @@
     row = jnp.concatenate(
         [received[jnp.bitwise_xor(g, m)] for m in range(1, BOX_SPAN + 1)], axis=1
     )
-    local = mm(row, maps[...])
+    local = mm_row(row, maps[...])
     message[:, 0, 0:128] = jnp.broadcast_to(local, (GROUP, 128))
     message[:, 0, 128:640] = picked[:, 0, :]
 
@@ -472,7 +479,7 @@
     row = jnp.concatenate(
         [boxes[jnp.bitwise_xor(g, m)] for m in range(1, BOX_SPAN + 1)], axis=1
     )
-    return mm(row, maps[...])
+    return mm_row(row, maps[...])
 
 
 def cell_local(couplings, cell_transfer, received):

time: 177 us -> 176 us (level)
  Pallas kernels: 46 us -> 44 us
where the time goes in v5:
time: 176 us; the launch traced here: 175 us
  blocking collectives  70.5 us (40%)
  Pallas kernels  44 us (25%)
  starting transfers between devices  41.2 us (23%)
  waiting for transfers between devices  12.3 us (7%)
  local copies, waits for them, and re-layouts  5.77 us (3%)
    all_to_all x4, blocking collectives, turn(): return lax.all_to_all(block, axis, 0, 0, tiled=True)  70.5 us
    all_to_all x4, starting transfers between devices, turn(): return lax.all_to_all(block, axis, 0, 0, tiled=True)  27.9 us
    pallas_call x1, Pallas kernels, near_tiles(): pl.pallas_call(tiles_body, grid=(OWN,), out_shape=(tile, shape(ROWS, OWN...  17.7 us
    ppermute x3, starting transfers between devices, exchange(): return lax.ppermute(block, axis, [(i, i ^ mask) for i in range(count)])  13.3 us
    all_to_all x4, waiting for transfers between devices, turn(): return lax.all_to_all(block, axis, 0, 0, tiled=True)  12.3 us
    pallas_call x1, Pallas kernels, near_again(): pl.pallas_call(again_body, grid=(OWN, 2), out_shape=(shape(ROWS, OWN * LE...  11.9 us
    unnamed x24, local copies, waits for them, and re-layouts  5.77 us
    pallas_call x1, Pallas kernels, up(): pl.pallas_call(up_body, out_shape=(shape(RANK, OWN * LEAF), shape(GROUP,...  3.93 us
  transfers between devices with their start and end apart: 7, of which 3 were waited for; matrix products, arithmetic and copies ran while one was open for 0% of the time, Pallas kernels for 21%

profile of v5, /device:TPU:1, one launch (start us, length us, event | category | flops | bytes accessed | tf_op | source)
XLA Modules:
  0.0 174.7 jit_solution(7737113836054046351)
XLA Ops:
  0.7 3.9 %up.1 = (f32[64,2048]{1,0:T(8,128)}, f32[32,1,384]{2,1,0:T(1,128)}, f32[64,2048]{1,0:T(8,128)}, f32[3,2048]{1,0:T(4,128)}) custom-call(f32[4,64,512]{2,1,0:T(8,128)} %basis.1, f32[4,64,64]{2,1,0:T(8,128)} %leaf_transfer.1, f32[1,64,64]{2,1,0:T(8,128)} %cell_transfer.5, s32[1,4]{1,0:T(1,128)} %lists.1, f32[64,2048]{1,0:T(8,128)} %vector.1, f32[3,2048]{1,0:T(4,128)} %points.1), custom_call_target="tpu_custom_call" | custom-call | flops 60000000 | bytes 2000000 | tf_op jit(solution)/shard_map/up/pallas_call | solution.py:125
  4.6 8.9 %collective-permute-start.1 = (f32[64,2048]{1,0:T(8,128)}, f32[64,2048]{1,0:T(8,128)S(1)}, u32[]{:S(2)}, u32[]{:S(2)}) collective-permute-start(f32[64,2048]{1,0:T(8,128)} %get-tuple-element.25.own.vector), channel_id=1, source_target_pairs={{0,1},{1,0},{2,3},{3,2},{4,5},{5,4},{6,7},{7,6},{8,9},{9,8},{10,11... | collective-permute-start | bytes 1572872 | tf_op jit(solution)/shard_map/ppermute | solution.py:572
  13.6 10.0 %all-to-all-start = ((f32[32,1,384]{2,1,0:T(1,128)}), f32[32,1,384]{2,1,0:T(1,128)S(1)}, u32[]{:S(2)}, u32[]{:S(2)}) async-start(f32[32,1,384]{2,1,0:T(1,128)} %get-tuple-element.30), calls=%async_computation | async-start | bytes 98304 | tf_op jit(solution)/shard_map/all_to_all | solution.py:576
  23.6 2.1 %collective-permute-start = (f32[3,2048]{1,0:T(4,128)}, f32[3,2048]{1,0:T(4,128)S(1)}, u32[]{:S(2)}, u32[]{:S(2)}) collective-permute-start(f32[3,2048]{1,0:T(4,128)} %get-tuple-element.26.own), channel_id=1, source_target_pairs={{0,1},{1,0},{2,3},{3,2},{4,5},{5,4},{6,7},{7,6},{8,9},{9,8},{10,11... | collective-permute-start | bytes 73736 | tf_op jit(solution)/shard_map/ppermute | solution.py:572
  25.7 10.4 %all-to-all-done.received = f32[32,1,384]{2,1,0:T(1,128)S(1)} async-done(((f32[32,1,384]{2,1,0:T(1,128)}), f32[32,1,384]{2,1,0:T(1,128)S(1)}, u32[]{:S(2)}, u32[]{:S(2)}) %all-to-all-start) | async-done | bytes 49184 | tf_op jit(solution)/shard_map/all_to_all | solution.py:576
  36.1 1.0 route.2
  37.0 6.8 %all-to-all-start.1 = ((f32[16,1,128]{2,1,0:T(1,128)}), f32[16,1,128]{2,1,0:T(1,128)S(1)}, u32[]{:S(2)}, u32[]{:S(2)}) async-start(f32[16,1,128]{2,1,0:T(1,128)} %get-tuple-element.31), calls=%async_computation.1 | async-start | bytes 16384 | tf_op jit(solution)/shard_map/all_to_all | solution.py:576
  43.8 3.0 %coarse.1.maps = f32[1152,128]{1,0:T(8,128)} custom-call(f32[16,64,64]{2,1,0:T(8,128)} %parent_ref.1, f32[16,3,64,64]{3,2,1,0:T(8,128)} %box_ref.1, f32[8,4,64,64]{3,2,1,0:T(8,128)} %top_ref.1), custom_call_target="tpu_custom_call" | custom-call | flops 50000000 | bytes 2000000 | tf_op jit(solution)/shard_map/coarse/pallas_call | solution.py:175
  46.9 0.7 copy-done.7
  47.6 0.5 features.1
  48.1 1.0 copy-done.10
  49.1 0.9 all-to-all-done.1.received
  50.0 1.1 copy-done
  51.1 1.0 boxes.1
  52.1 6.5 %all-to-all-start.2 = ((f32[32,1,640]{2,1,0:T(1,128)}), f32[32,1,640]{2,1,0:T(1,128)S(1)}, u32[]{:S(2)}, u32[]{:S(2)}) async-start(f32[32,1,640]{2,1,0:T(1,128)} %boxes.1), calls=%async_computation.2 | async-start | bytes 163840 | tf_op jit(solution)/shard_map/all_to_all | solution.py:576
  58.7 1.0 copy-done.2
  59.9 0.7 copy-done.8
  60.5 1.2 copy-done.11
  61.8 17.7 %near_tiles.1 = (bf16[4,6,2,512,512]{4,3,2,1,0:T(8,128)(2,1)}, f32[64,2048]{1,0:T(8,128)S(1)}) custom-call(s32[4,6]{1,0:T(4,128)S(1)} %copy-done.8, bf16[8,512,32]{2,1,0:T(8,128)(2,1)S(1)} %copy-done.11, bf16[4,32,512]{2,1,0:T(8,128)(2,1)S(1)} %get-tuple-element.28.right, bf16[8,128,512]{2,1,0:T(8,128)(2,1)S(1)} %joined.2.vectors), custom_call_target="tpu_custom_call" | custom-call | flops 8000000000 | bytes 30000000 | tf_op jit(solution)/shard_map/near_tiles/pallas_call | solution.py:428
  79.5 1.6 middle.1
  81.0 2.2 %collective-permute-start.2 = (f32[64,2048]{1,0:T(8,128)S(1)}, f32[64,2048]{1,0:T(8,128)S(1)}, u32[]{:S(2)}, u32[]{:S(2)}) collective-permute-start(f32[64,2048]{1,0:T(8,128)S(1)} %get-tuple-element.35.own.image.first), channel_id=1, source_target_pairs={{0,1},{1,0},{2,3},{3,2},{4,5},{5,4},{6,7},{7,6},{8,9},{9,8},{10,11... | collective-permute-start | bytes 1572872 | tf_op jit(solution)/shard_map/ppermute | solution.py:572
  83.3 24.0 %all_to_all.40.received = f32[32,1,256]{2,1,0:T(1,128)S(1)} all-to-all(f32[32,1,256]{2,1,0:T(1,128)S(1)} %get-tuple-element.37), channel_id=1, replica_groups=mesh['gx'=16,'gy'=32] {'gy'}, dimensions={0} | all-to-all | bytes 65536 | tf_op jit(solution)/shard_map/all_to_all | solution.py:576
  107.3 0.9 route.3
  108.2 4.6 %all-to-all-start.4 = ((f32[32,1,512]{2,1,0:T(1,128)}), f32[32,1,512]{2,1,0:T(1,128)S(1)}, u32[]{:S(2)}, u32[]{:S(2)}) async-start(f32[32,1,512]{2,1,0:T(1,128)} %get-tuple-element.41), calls=%async_computation.4 | async-start | bytes 131072 | tf_op jit(solution)/shard_map/all_to_all | solution.py:576
  112.8 0.1 joined.3.vectors
  113.0 11.9 %near_again.1 = (f32[64,2048]{1,0:T(8,128)S(1)}, f32[16,1,128]{2,1,0:T(1,128)S(1)}) custom-call(s32[4,6]{1,0:T(4,128)S(1)} %copy-done.9, bf16[8,128,512]{2,1,0:T(8,128)(2,1)S(1)} %joined.3.vectors, bf16[4,6,2,512,512]{4,3,2,1,0:T(8,128)(2,1)} %get-tuple-element.36.high_tiles.low_tiles, bf16[4,6,2,512,512]{4,3,2,1,0:T(8,128)(2,1)} %get-tuple-element.36.high_tiles.low_tiles, ...), custom_call_target="tpu_custom_call" | custom-call | flops 6000000000 | bytes 30000000 | tf_op jit(solution)/shard_map/near_again/pallas_call | solution.py:465
  124.9 1.0 all-to-all-done.4.picked
  125.9 10.9 %all_to_all.41.received = f32[16,1,128]{2,1,0:T(1,128)S(1)} all-to-all(f32[16,1,128]{2,1,0:T(1,128)S(1)} %get-tuple-element.42), channel_id=1, replica_groups=mesh['gx'=16,'gy'=32] {'gx'}, dimensions={0} | all-to-all | bytes 16384 | tf_op jit(solution)/shard_map/all_to_all | solution.py:576
  136.8 0.7 tally.1
  137.5 9.2 %all_to_all.42.received = f32[16,2,128]{2,1,0:T(2,128)S(1)} all-to-all(f32[16,2,128]{2,1,0:T(2,128)S(1)} %get-tuple-element.44), channel_id=1, replica_groups=mesh['gx'=16,'gy'=32] {'gx'}, dimensions={0} | all-to-all | bytes 32768 | tf_op jit(solution)/shard_map/all_to_all | solution.py:576
  146.7 26.4 %all_to_all.43.received = f32[32,1,384]{2,1,0:T(1,128)S(1)} all-to-all(f32[32,1,384]{2,1,0:T(1,128)S(1)} %spread.1), channel_id=1, replica_groups=mesh['gx'=16,'gy'=32] {'gy'}, dimensions={0} | all-to-all | bytes 98304 | tf_op jit(solution)/shard_map/all_to_all | solution.py:576
  173.1 1.5 finish.1
  (24 shorter events, 0.2 us)
Async XLA Ops:
  0.6 78.8 %copy-start.6 = (f32[1,64,64]{2,1,0:T(8,128)S(1)}, f32[1,64,64]{2,1,0:T(8,128)}, u32[]{:S(2)}) copy-start(f32[1,64,64]{2,1,0:T(8,128)} %cell_transfer.5) | copy-start | bytes 49156
  0.6 112.3 %copy-start.9 = (s32[4,6]{1,0:T(4,128)S(1)}, s32[4,6]{1,0:T(4,128)}, u32[]{:S(2)}) copy-start(s32[4,6]{1,0:T(4,128)} %neighbours.3) | copy-start | bytes 292
  0.7 78.8 %copy-start.5 = (f32[1,4,64,64]{3,2,1,0:T(8,128)S(1)}, f32[1,4,64,64]{3,2,1,0:T(8,128)}, u32[]{:S(2)}) copy-start(f32[1,4,64,64]{3,2,1,0:T(8,128)} %couplings.3) | copy-start | bytes 196612
  4.6 74.9 %copy-start.3 = (f32[64,2048]{1,0:T(8,128)S(1)}, f32[64,2048]{1,0:T(8,128)}, u32[]{:S(2)}) copy-start(f32[64,2048]{1,0:T(8,128)} %get-tuple-element.25.own.vector) | copy-start | bytes 1572868
  4.6 74.9 %copy-start.4 = (f32[64,2048]{1,0:T(8,128)S(1)}, f32[64,2048]{1,0:T(8,128)}, u32[]{:S(2)}) copy-start(f32[64,2048]{1,0:T(8,128)} %get-tuple-element.24.lifts) | copy-start | bytes 1572868
  4.6 54.1 %collective-permute-start.1 = (f32[64,2048]{1,0:T(8,128)}, f32[64,2048]{1,0:T(8,128)S(1)}, u32[]{:S(2)}, u32[]{:S(2)}) collective-permute-start(f32[64,2048]{1,0:T(8,128)} %get-tuple-element.25.own.vector), channel_id=1, source_target_pairs={{0,1},{1,0},{2,3},{3,2},{4,5},{5,4},{6,7},{7,6},{8,9},{9,8},{10,11... | collective-permute-start | bytes 1572872 | tf_op jit(solution)/shard_map/ppermute | solution.py:572
  13.6 22.5 %all-to-all-start = ((f32[32,1,384]{2,1,0:T(1,128)}), f32[32,1,384]{2,1,0:T(1,128)S(1)}, u32[]{:S(2)}, u32[]{:S(2)}) async-start(f32[32,1,384]{2,1,0:T(1,128)} %get-tuple-element.30), calls=%async_computation | async-start | bytes 98304 | tf_op jit(solution)/shard_map/all_to_all | solution.py:576
  23.6 23.3 %collective-permute-start = (f32[3,2048]{1,0:T(4,128)}, f32[3,2048]{1,0:T(4,128)S(1)}, u32[]{:S(2)}, u32[]{:S(2)}) collective-permute-start(f32[3,2048]{1,0:T(4,128)} %get-tuple-element.26.own), channel_id=1, source_target_pairs={{0,1},{1,0},{2,3},{3,2},{4,5},{5,4},{6,7},{7,6},{8,9},{9,8},{10,11... | collective-permute-start | bytes 73736 | tf_op jit(solution)/shard_map/ppermute | solution.py:572
  37.0 13.0 %all-to-all-start.1 = ((f32[16,1,128]{2,1,0:T(1,128)}), f32[16,1,128]{2,1,0:T(1,128)S(1)}, u32[]{:S(2)}, u32[]{:S(2)}) async-start(f32[16,1,128]{2,1,0:T(1,128)} %get-tuple-element.31), calls=%async_computation.1 | async-start | bytes 16384 | tf_op jit(solution)/shard_map/all_to_all | solution.py:576
  46.8 0.8 copy-start.7
  48.1 1.0 copy-start.10
  50.0 1.1 copy-start
  52.1 27.3 %all-to-all-start.2 = ((f32[32,1,640]{2,1,0:T(1,128)}), f32[32,1,640]{2,1,0:T(1,128)S(1)}, u32[]{:S(2)}, u32[]{:S(2)}) async-start(f32[32,1,640]{2,1,0:T(1,128)} %boxes.1), calls=%async_computation.2 | async-start | bytes 163840 | tf_op jit(solution)/shard_map/all_to_all | solution.py:576
  58.7 1.0 copy-start.2
  59.9 0.7 copy-start.8
  60.5 1.2 copy-start.11
  81.0 31.8 %collective-permute-start.2 = (f32[64,2048]{1,0:T(8,128)S(1)}, f32[64,2048]{1,0:T(8,128)S(1)}, u32[]{:S(2)}, u32[]{:S(2)}) collective-permute-start(f32[64,2048]{1,0:T(8,128)S(1)} %get-tuple-element.35.own.image.first), channel_id=1, source_target_pairs={{0,1},{1,0},{2,3},{3,2},{4,5},{5,4},{6,7},{7,6},{8,9},{9,8},{10,11... | collective-permute-start | bytes 1572872 | tf_op jit(solution)/shard_map/ppermute | solution.py:572
  108.2 17.7 %all-to-all-start.4 = ((f32[32,1,512]{2,1,0:T(1,128)}), f32[32,1,512]{2,1,0:T(1,128)S(1)}, u32[]{:S(2)}, u32[]{:S(2)}) async-start(f32[32,1,512]{2,1,0:T(1,128)} %get-tuple-element.41), calls=%async_computation.4 | async-start | bytes 131072 | tf_op jit(solution)/shard_map/all_to_all | solution.py:576
  112.9 23.8 %copy-start.1 = (f32[1152,128]{1,0:T(8,128)S(1)}, f32[1152,128]{1,0:T(8,128)}, u32[]{:S(2)}) copy-start(f32[1152,128]{1,0:T(8,128)} %coarse.1.maps) | copy-start | bytes 1769476
